TPU v7x, 32 devices: a whole 2x2x4 slice. The times are simulated.
32 devices in a mesh: rep: 4 (over x, core), shard: 8 (over z, y).
Axes of the slice: x: 2, y: 2, z: 4, core: 2. Of those that a mesh axis runs over, the one named last changes fastest.
Arguments:
- tokens: bfloat16 [256, 197, 384], P(('rep', 'shard')), may hold values from -6 to 6
- weights: float32 [2, 384, 4608], P(None, 'shard')
- vectors: float32 [2, 12, 384], P(None, None, 'shard')
- moment_one: float32 [2, 384, 4608], P(None, 'shard'), may hold values from -60 to 60
- moment_two: float32 [2, 384, 4608], P(None, 'shard'), may hold values from 1 to 100
- vector_one: float32 [2, 12, 384], P(None, None, 'shard'), may hold values from -60 to 60
- vector_two: float32 [2, 12, 384], P(None, None, 'shard'), may hold values from 1 to 100
- images: int32 [32], P(('rep', 'shard')), may hold values from 4 to 8, as said below
- cotangent: bfloat16 [256, 197, 384], P(('rep', 'shard')), may hold values from -6 to 6
Outputs:
- output: float32 [256, 197, 384], P(('rep', 'shard'))
- input_grad: float32 [256, 197, 384], P(('rep', 'shard'))
- weight_grad: float32 [2, 384, 4608], P(None, 'shard')
- vector_grad: float32 [2, 12, 384], P(None, None, 'shard')
- moment_one_new: float32 [2, 384, 4608], P(None, 'shard')
- moment_two_new: float32 [2, 384, 4608], P(None, 'shard')
- vector_one_new: float32 [2, 12, 384], P(None, None, 'shard')
- vector_two_new: float32 [2, 12, 384], P(None, None, 'shard')
- update: float32 [2, 384, 4608], P(None, 'shard')
- vector_update: float32 [2, 12, 384], P(None, None, 'shard')
Inputs may be any that keep to these rules, and one draw needn't show every extreme that they name: `images`: live image slots of each device; some device has all 8.
All inputs are finite; a program needn't handle non-finite values.
Results may differ from a plain program's by a relative error of at most 0.022.
The roundings to bfloat16 on the way count: a program that leaves them out, or rounds other values in their place, can miss the bound.
Values may be sent and summed in bfloat16 or wider, within the bound.
No kernel may reach another device: no remote copies, remote signals or barrier semaphores. Data moves between devices by JAX's collectives and lax.ppermute only.
A program may use at most 192 MiB of HBM per device.

v0:
```python
import functools
import math

import jax
import jax.numpy as jnp
from jax import lax
from jax.experimental import pallas as pl
from jax.experimental.pallas import tpu as pltpu
from jax.sharding import PartitionSpec as P

HEAD = 64
FF = 1536
STEP = 10
PAIR = 2
TILE = 128
CHUNK = 768
NEG = -1e30
F32 = jnp.float32
BF16 = jnp.bfloat16
VMEM_LIMIT = 60 * 1024 * 1024


def dot(left, right):
    return jnp.dot(left, right, preferred_element_type=F32)


def dot_nt(left, right):
    return lax.dot_general(left, right, (((1,), (1,)), ((), ())), preferred_element_type=F32)


def dot_tn(left, right):
    return lax.dot_general(left, right, (((0,), (0,)), ((), ())), preferred_element_type=F32)


def norm(values):
    center = values - jnp.mean(values, -1, keepdims=True)
    scale = lax.rsqrt(jnp.mean(center * center, -1, keepdims=True) + 1e-06)
    return center * scale, scale


def norm_back(grad, normed, scale, gain):
    inner = grad * gain
    return scale * (
        inner
        - jnp.mean(inner, -1, keepdims=True)
        - normed * jnp.mean(inner * normed, -1, keepdims=True)
    )


def gelu_parts(u):
    phi = 0.5 + 0.5 * lax.erf(u * math.sqrt(0.5))
    slope = phi + u * (jnp.exp2((u * u) * (-0.5 * math.log2(math.e))) * (1.0 / math.sqrt(2.0 * math.pi)))
    return u * phi, slope


def bias_up(vec_ref, width):
    return jnp.concatenate([vec_ref[8 + j : 9 + j, :] for j in range(FF // width)], 1)


def load_weights(core_ref, place_ref, sources, start, whole_ref, sems):
    half = whole_ref.shape[1] // 2
    per_core = len(sources) // 2
    copies = []
    for n, source in enumerate(sources):
        at = core_ref[0] if n < per_core else 1 - core_ref[0]
        cols = pl.ds(pl.multiple_of(at * half, TILE), half)
        copies += row_copies(
            place_ref, source, n % per_core, slice(start, start + half), whole_ref, cols, sems, len(copies)
        )
    for copy in copies:
        copy.start()
    for copy in copies:
        copy.wait()


def load_first(core_ref, place_ref, sources, start, whole_ref, sems):
    per_core = len(sources) // 2
    size = whole_ref.shape[1]

    def load(chosen):
        copies = []
        for n, source in enumerate(chosen):
            copies += row_copies(
                place_ref, source, n, slice(start, start + size), whole_ref, slice(0, size), sems, len(copies)
            )
        for copy in copies:
            copy.start()
        for copy in copies:
            copy.wait()

    @pl.when(core_ref[0] == 0)
    def _():
        load(sources[:per_core])

    @pl.when(core_ref[0] != 0)
    def _():
        load(sources[per_core:])


def row_copies(place_ref, source, nth, taken, whole_ref, cols, sems, at):
    count, rows = source.shape[:2]
    copies = []
    for k in range(count):
        row = pl.multiple_of(place_ref[nth * count + k] * rows, rows)
        copies.append(
            pltpu.make_async_copy(
                source.at[k, :, taken], whole_ref.at[pl.ds(row, rows), cols], sems.at[at + k]
            )
        )
    return copies


def attn_forward(first, seq, rows, at, start, core_ref, place_ref, x_ref, *refs):
    sources, refs = refs[:at], refs[at:]
    if first:
        qkv_ref, o_ref, lse_ref, vec_ref, xp_ref, w_ref, sems = refs
    else:
        qkv_ref, o_ref, lse_ref, vec_ref, w_ref, sems = refs
        xp_ref = x_ref
    width = o_ref.shape[1]
    heads = width // HEAD

    @pl.when(pl.program_id(0) == 0)
    def _():
        load_weights(core_ref, place_ref, sources, start, w_ref, sems)
        turned = w_ref[:, 3 * width : 3 * width + TILE].astype(F32).T
        vec_ref[...] = turned[: vec_ref.shape[0]]

    if first:
        for i in range(PAIR):
            xp_ref[i * rows : i * rows + seq, :] = x_ref[i].astype(F32)
            xp_ref[i * rows + seq : (i + 1) * rows, :] = jnp.zeros((rows - seq, width), F32)

    normed, _ = norm(xp_ref[...])
    hidden = (normed * vec_ref[0:1, :] + vec_ref[1:2, :]).astype(BF16)
    qkv = dot(hidden, w_ref[:, : 3 * width])
    qkv_ref[:, :width] = ((qkv[:, :width] + vec_ref[2:3, :]) * 0.125).astype(BF16)
    qkv_ref[:, width : 2 * width] = qkv[:, width : 2 * width].astype(BF16)
    qkv_ref[:, 2 * width :] = (qkv[:, 2 * width :] + vec_ref[3:4, :]).astype(BF16)

    edge = seq // 16 * 16
    alive = lax.broadcasted_iota(jnp.int32, (rows - edge, rows), 0) < seq - edge
    left = lax.broadcasted_iota(jnp.int32, (rows, TILE), 1) < HEAD
    work = [(i, h) for i in range(PAIR) for h in range(heads)]

    def scores_of(i, h):
        span = slice(i * rows, (i + 1) * rows)
        tile = h * HEAD // TILE * TILE
        mine = left if h * HEAD == tile else ~left
        query = jnp.where(mine, qkv_ref[span, tile : tile + TILE], jnp.zeros((), BF16))
        return dot_nt(qkv_ref[span, width + tile : width + tile + TILE], query)

    def finish(i, h, probs, total):
        out = dot(turned_v[i][h * HEAD : (h + 1) * HEAD], probs) * (1.0 / total)
        outs[i].append(out.astype(BF16))
        if h == heads - 1:
            o_ref[i * rows : (i + 1) * rows, :] = jnp.concatenate(outs[i], 0).T

    outs = [[] for _ in range(PAIR)]
    turned_v = [qkv_ref[i * rows : (i + 1) * rows, 2 * width :].T for i in range(PAIR)]
    ahead = [scores_of(*item) for item in work[:4]]
    behind = []
    for n, (i, h) in enumerate(work):
        if n + 4 < len(work):
            ahead.append(scores_of(*work[n + 4]))
        scores = ahead.pop(0)
        low = scores[:edge]
        high = jnp.where(alive, scores[edge:], NEG)
        top = jnp.maximum(jnp.max(low, 0, keepdims=True), jnp.max(high, 0, keepdims=True))
        low = jnp.exp(low - top)
        high = jnp.exp(high - top)
        total = jnp.sum(low, 0, keepdims=True) + jnp.sum(high, 0, keepdims=True)
        lse_ref[i, h : h + 1, :rows] = top + jnp.log(total)
        behind.append((i, h, jnp.concatenate([low.astype(BF16), high.astype(BF16)], 0), total))
        if len(behind) > 1:
            finish(*behind.pop(0))
    for item in behind:
        finish(*item)


def mlp_forward(last, seq, rows, at, start, core_ref, place_ref, x_ref, o_ref, vec_ref, *refs):
    sources, refs = refs[:at], refs[at:]
    x1_ref, act_ref, slope_ref, out_ref, w_ref, sems = refs
    width = x_ref.shape[1]

    @pl.when(pl.program_id(0) == 0)
    def _():
        load_weights(core_ref, place_ref, sources, start, w_ref, sems)

    x1 = x_ref[...] + dot(o_ref[...], w_ref[:, :width]) + vec_ref[4:5, :]
    x1_ref[...] = x1
    normed, _ = norm(x1)
    hidden = (normed * vec_ref[5:6, :] + vec_ref[6:7, :]).astype(BF16)
    bias = bias_up(vec_ref, width)
    units = [(r, j) for r in range(0, x1.shape[0], x1.shape[0]) for j in range(0, FF, CHUNK)]
    size = x1.shape[0]

    def up(r, j):
        return dot(hidden[r : r + size], w_ref[:, width + j : width + j + CHUNK])

    totals = {r: x1[r : r + size] + vec_ref[7:8, :] for r, _ in units}

    def down(r, j, act):
        start = width + FF + j
        totals[r] = totals[r] + dot_nt(act, w_ref[:, start : start + CHUNK])

    ahead = up(*units[0])
    behind = None
    for n, (r, j) in enumerate(units):
        u = ahead
        if n + 1 < len(units):
            ahead = up(*units[n + 1])
        if behind is not None:
            down(*behind)
        acts = []
        for k in range(0, size, 16):
            act, slope = gelu_parts(u[k : k + 16] + bias[:, j : j + CHUNK])
            slope_ref[r + k : r + k + 16, j : j + CHUNK] = slope
            acts.append(act.astype(BF16))
        act = jnp.concatenate(acts, 0)
        act_ref[r : r + size, j : j + CHUNK] = act
        behind = (r, j, act)
    down(*behind)
    total = jnp.concatenate([totals[r] for r in sorted(totals)], 0)
    if last:
        for i in range(PAIR):
            out_ref[i] = total[i * rows : i * rows + seq]
    else:
        out_ref[...] = total


def put_grads(core, first_of, second_of, keep_ref, send_ref):
    @pl.when(core == 0)
    def _():
        first_of(keep_ref)
        second_of(send_ref)

    @pl.when(core != 0)
    def _():
        first_of(send_ref)
        second_of(keep_ref)


def put_vectors(acc_ref, ref):
    size = acc_ref.shape[0]
    padded = jnp.concatenate(
        [acc_ref[...], jnp.zeros((TILE - size, acc_ref.shape[1]), F32)], 0
    )
    ref[:, ref.shape[1] - TILE :] = padded.T.astype(BF16)


def column_sum(values):
    return jnp.sum(values, 0, keepdims=True)


def mlp_backward(
    last, seq, rows, at, start, core_ref, place_ref, live_ref, g_ref, x1_ref, act_ref, slope_ref, vec_ref, *refs
):
    sources, refs = refs[:at], refs[at:]
    gx1_ref, keep_ref, send_ref, w_ref, up_ref, down_ref, acc_ref, bias_ref, gp_ref, sems = refs
    width = x1_ref.shape[1]
    step = pl.program_id(0)

    @pl.when(step == 0)
    def _():
        load_weights(core_ref, place_ref, sources, start, w_ref, sems)
        up_ref[...] = jnp.zeros_like(up_ref)
        bias_ref[...] = jnp.zeros_like(bias_ref)
        down_ref[...] = jnp.zeros_like(down_ref)
        acc_ref[...] = jnp.zeros_like(acc_ref)

    if last:
        for i in range(PAIR):
            keep = (step * PAIR + i < live_ref[0]).astype(F32)
            gp_ref[i * rows : i * rows + seq, :] = g_ref[i].astype(F32) * keep
            gp_ref[i * rows + seq : (i + 1) * rows, :] = jnp.zeros((rows - seq, width), F32)
        g = gp_ref[...]
    else:
        g = g_ref[...]
    low = g.astype(BF16)
    size = CHUNK

    def back(j):
        start = width + FF + j
        return dot(low, w_ref[:, start : start + size])

    ahead = back(0)
    turned = low.T
    normed, scale = norm(x1_ref[...])
    hidden = (normed * vec_ref[5:6, :] + vec_ref[6:7, :]).astype(BF16)
    turned_h = hidden.T
    acc_ref[2:3, :] += column_sum(g)
    total = None

    def finish(total, j, gu):
        up_ref[:, j : j + size] += dot(turned_h, gu)
        part = dot_nt(gu, w_ref[:, width + j : width + j + size])
        return part if total is None else total + part

    behind = None
    for j in range(0, FF, size):
        ga = ahead
        if j + size < FF:
            ahead = back(j + size)
        down_ref[:, j : j + size] += dot(turned, act_ref[:, j : j + size])
        if behind is not None:
            total = finish(total, *behind)
        gus = []
        sums = jnp.zeros((8, size), F32)
        for r in range(0, ga.shape[0], 16):
            gu = ga[r : r + 16].astype(BF16).astype(F32) * slope_ref[r : r + 16, j : j + size]
            sums = sums + gu[:8] + gu[8:]
            gus.append(gu.astype(BF16))
        bias_ref[:, j : j + size] += sums
        behind = (j, jnp.concatenate(gus, 0))
    total = finish(total, *behind)
    gh2 = total.astype(BF16).astype(F32)
    acc_ref[0:1, :] += column_sum(gh2 * normed)
    acc_ref[1:2, :] += column_sum(gh2)
    gx1_ref[...] = g + norm_back(gh2, normed, scale, vec_ref[5:6, :])

    @pl.when(step == pl.num_programs(0) - 1)
    def _():
        sums = column_sum(bias_ref[...])
        for j in range(FF // width):
            acc_ref[3 + j : 4 + j, :] = sums[:, j * width : (j + 1) * width]

        def up(ref):
            ref[:, :FF] = up_ref[...].astype(BF16)
            put_vectors(acc_ref, ref)

        def down(ref):
            ref[:, :FF] = down_ref[...].astype(BF16)
            ref[:, FF:] = jnp.zeros((width, TILE), BF16)

        put_grads(core_ref[0], up, down, keep_ref, send_ref)


def attn_backward(
    first, seq, rows, ats, starts, core_ref, qplace_ref, place_ref, g_ref, x_ref, qkv_ref, lse_ref, o_ref,
    vec_ref, *refs
):
    qsources, refs = refs[: ats[0]], refs[ats[0] :]
    sources, refs = refs[: ats[1]], refs[ats[1] :]
    gx_ref, keep_ref, send_ref, w_ref, wout_ref, gw_ref, gout_ref, acc_ref, gqkv_ref, go_ref, sems, osems = refs
    width = x_ref.shape[1]
    heads = width // HEAD
    step = pl.program_id(0)

    @pl.when(step == 0)
    def _():
        load_weights(core_ref, qplace_ref, qsources, starts[0], w_ref, sems)
        load_first(core_ref, place_ref, sources, starts[1], wout_ref, osems)
        gw_ref[...] = jnp.zeros_like(gw_ref)
        gout_ref[...] = jnp.zeros_like(gout_ref)
        acc_ref[...] = jnp.zeros_like(acc_ref)

    low = g_ref[...].astype(BF16)
    gout_ref[...] += dot(o_ref[...].T, low)
    acc_ref[4:5, :] += column_sum(g_ref[...])
    go_ref[...] = dot_nt(low, wout_ref[...]).astype(BF16)

    edge = seq // 16 * 16
    alive = lax.broadcasted_iota(jnp.int32, (rows - edge, rows), 0) < seq - edge
    left = lax.broadcasted_iota(jnp.int32, (rows, TILE), 1) < HEAD
    zero = jnp.zeros((), BF16)
    work = [(i, h) for i in range(PAIR) for h in range(heads)]

    def tile_of(ref, part, i, h):
        at = part * width + h * HEAD // TILE * TILE
        return ref[i * rows : (i + 1) * rows, at : at + TILE]

    def start(i, h):
        mine = left if h * HEAD % TILE == 0 else ~left
        query = jnp.where(mine, tile_of(qkv_ref, 0, i, h), zero)
        go = jnp.where(mine, tile_of(go_ref, 0, i, h), zero)
        return dot_nt(tile_of(qkv_ref, 1, i, h), query), dot_nt(tile_of(qkv_ref, 2, i, h), go)

    def finish(i, h, probs, gs):
        gvs[i].append(dot(probs, tile_of(go_ref, 0, i, h)))
        gks[i].append(dot(gs, tile_of(qkv_ref, 0, i, h)))
        gqs[i].append((dot(turned_k[i][h * HEAD : (h + 1) * HEAD], gs) * 0.125).astype(BF16))
        span = slice(i * rows, (i + 1) * rows)
        if h % 2:
            for part, held in ((1, gks[i]), (2, gvs[i])):
                at = part * width + h * HEAD // TILE * TILE
                gqkv_ref[span, at : at + TILE] = jnp.where(left, held[h - 1], held[h]).astype(BF16)
        if h == heads - 1:
            gqkv_ref[span, :width] = jnp.concatenate(gqs[i], 0).T

    gks, gvs, gqs = ([[] for _ in range(PAIR)] for _ in range(3))
    turned_k = [qkv_ref[i * rows : (i + 1) * rows, width : 2 * width].T for i in range(PAIR)]
    ahead = [start(*item) for item in work[:2]]
    behind = []
    for n, (i, h) in enumerate(work):
        if n + 2 < len(work):
            ahead.append(start(*work[n + 2]))
        scores, gp = ahead.pop(0)
        scores = scores - lse_ref[i, h : h + 1, :rows]
        p_low = jnp.exp(scores[:edge])
        p_high = jnp.where(alive, jnp.exp(scores[edge:]), 0.0)
        probs = jnp.concatenate([p_low.astype(BF16), p_high.astype(BF16)], 0)
        gp_low, gp_high = gp[:edge], gp[edge:]
        mean = column_sum(gp_low * p_low) + column_sum(gp_high * p_high)
        gs_low = (p_low * (gp_low - mean)).astype(BF16)
        gs_high = (p_high * (gp_high - mean)).astype(BF16)
        behind.append((i, h, probs, jnp.concatenate([gs_low, gs_high], 0)))
        if len(behind) > 1:
            finish(*behind.pop(0))
    for item in behind:
        finish(*item)

    normed, scale = norm(x_ref[...])
    hidden = (normed * vec_ref[0:1, :] + vec_ref[1:2, :]).astype(BF16)
    turned_h = hidden.T
    gqkv = gqkv_ref[...]
    gw_ref[...] += dot(turned_h, gqkv)
    total = dot_nt(gqkv, w_ref[:, : 3 * width])
    acc_ref[2:3, :] += column_sum(gqkv[:, :width].astype(F32))
    acc_ref[3:4, :] += column_sum(gqkv[:, 2 * width :].astype(F32))
    gh = total.astype(BF16).astype(F32)
    acc_ref[0:1, :] += column_sum(gh * normed)
    acc_ref[1:2, :] += column_sum(gh)
    gx = g_ref[...] + norm_back(gh, normed, scale, vec_ref[0:1, :])
    if first:
        for i in range(PAIR):
            gx_ref[i] = gx[i * rows : i * rows + seq]
    else:
        gx_ref[...] = gx

    @pl.when(step == pl.num_programs(0) - 1)
    def _():
        def one(ref):
            ref[:, : 2 * width] = gw_ref[:, : 2 * width].astype(BF16)
            put_vectors(acc_ref, ref)

        def two(ref):
            ref[:, :width] = gw_ref[:, 2 * width :].astype(BF16)
            ref[:, width : 2 * width] = gout_ref[...].astype(BF16)
            ref[:, 2 * width :] = jnp.zeros((width, TILE), BF16)

        put_grads(core_ref[0], one, two, keep_ref, send_ref)


def adamw(grad, first, second, old):
    first_new = 0.9 * first + 0.1 * grad
    second_new = 0.999 * second + 0.001 * grad * grad
    first_hat = first_new / (1.0 - 0.9**STEP)
    second_hat = second_new / (1.0 - 0.999**STEP)
    change = -0.01 * (first_hat / (jnp.sqrt(second_hat) + 1e-08) + 0.05 * old)
    return (first_new, second_new, change)


def step_kernel(aliased, core_ref, mine_ref, other_ref, one_ref, two_ref, old_ref, *refs):
    grad_ref, one_new_ref, two_new_ref, change_ref = refs[-4:]
    cols = grad_ref.shape[2]

    def put(from_ref):
        grad = from_ref[:, :cols].astype(F32)
        grad_ref[0] = grad
        one_new_ref[0], two_new_ref[0], change_ref[0] = adamw(grad, one_ref[0], two_ref[0], old_ref[0])

    @pl.when(core_ref[0] == pl.program_id(0))
    def _():
        put(mine_ref)

    @pl.when(core_ref[0] != pl.program_id(0))
    def _():
        put(other_ref)


def smem():
    return pl.BlockSpec(memory_space=pltpu.SMEM)


def whole(shape):
    zeros = (0,) * len(shape)
    return pl.BlockSpec(shape, lambda i: zeros)


def cost(flops, moved, exps):
    return pl.CostEstimate(flops=int(flops), bytes_accessed=int(moved), transcendentals=int(exps))


def params():
    return pltpu.CompilerParams(
        dimension_semantics=("arbitrary",), vmem_limit_bytes=VMEM_LIMIT
    )


def struct(shape, kind):
    return jax.ShapeDtypeStruct(shape, kind)


class Weights:
    def __init__(self, arrays, place, start, half):
        self.arrays, self.place, self.start, self.half = arrays, place, start, half

    def specs(self):
        return [pl.BlockSpec(memory_space=pl.ANY)] * len(self.arrays)

    def sems(self):
        return pltpu.SemaphoreType.DMA((sum(a.shape[0] for a in self.arrays),))


def call(kernel, after, in_specs, **rest):
    count = len(after)

    def run(*refs):
        kernel(*refs[count:])

    made = pl.pallas_call(
        run, in_specs=[pl.BlockSpec(memory_space=pl.ANY)] * count + in_specs, **rest
    )
    return lambda *args: made(*after, *args)


class Layers:
    def __init__(self, core, images, seq, width):
        self.core, self.images, self.seq, self.width = core, images, seq, width
        self.rows = -(-seq // 16) * 16
        self.grid = (images // PAIR,)
        self.total = images * self.rows
        self.block = PAIR * self.rows

    def tall(self, cols):
        return pl.BlockSpec((self.block, cols), lambda i: (i, 0))

    def images_spec(self):
        return pl.BlockSpec((PAIR, self.seq, self.width), lambda i: (i, 0, 0))

    def lse_spec(self):
        return pl.BlockSpec((PAIR, 8, 256), lambda i: (i, 0, 0))

    def attn_forward(self, x, wq, first, after):
        w, t = self.width, self.total
        outs = [
            (self.tall(3 * w), struct((t, 3 * w), BF16)),
            (self.tall(w), struct((t, w), BF16)),
            (self.lse_spec(), struct((self.images, 8, 256), F32)),
            (whole((16, w)), struct((16, w), F32)),
        ]
        if first:
            outs.append((self.tall(w), struct((t, w), F32)))
        return call(
            functools.partial(attn_forward, first, self.seq, self.rows, len(wq.arrays), wq.start),
            after,
            [smem(), smem(), self.images_spec() if first else self.tall(w)] + wq.specs(),
            grid=self.grid,
            out_specs=[o[0] for o in outs],
            out_shape=[o[1] for o in outs],
            scratch_shapes=[pltpu.VMEM((w, 2 * wq.half), BF16), wq.sems()],
            compiler_params=params(),
            cost_estimate=cost(1.7e10, 2e7, 3e6),
        )(self.core, wq.place, x, *wq.arrays)

    def mlp_forward(self, x, o, wr, vec, last, after):
        w, t = self.width, self.total
        outs = [
            (self.tall(w), struct((t, w), F32)),
            (self.tall(FF), struct((t, FF), BF16)),
            (self.tall(FF), struct((t, FF), F32)),
            (self.images_spec(), struct((self.images, self.seq, w), F32))
            if last
            else (self.tall(w), struct((t, w), F32)),
        ]
        return call(
            functools.partial(mlp_forward, last, self.seq, self.rows, len(wr.arrays), wr.start),
            after,
            [smem(), smem(), self.tall(w), self.tall(w), whole(vec.shape)] + wr.specs(),
            grid=self.grid,
            out_specs=[o[0] for o in outs],
            out_shape=[o[1] for o in outs],
            scratch_shapes=[pltpu.VMEM((w, 2 * wr.half), BF16), wr.sems()],
            compiler_params=params(),
            cost_estimate=cost(2.2e10, 3e7, 3e6),
        )(self.core, wr.place, x, o, vec, *wr.arrays)

    def mlp_backward(self, live, g, x1, act, slope, wr, vec, last, after):
        w, t = self.width, self.total
        return call(
            functools.partial(mlp_backward, last, self.seq, self.rows, len(wr.arrays), wr.start),
            after,
            [
                smem(), smem(), smem(),
                self.images_spec() if last else self.tall(w),
                self.tall(w), self.tall(FF), self.tall(FF), whole(vec.shape),
            ]
            + wr.specs(),
            grid=self.grid,
            out_specs=[self.tall(w), whole((w, FF + TILE)), whole((w, FF + TILE))],
            out_shape=[
                struct((t, w), F32), struct((w, FF + TILE), BF16), struct((w, FF + TILE), BF16),
            ],
            scratch_shapes=[
                pltpu.VMEM((w, 2 * wr.half), BF16),
                pltpu.VMEM((w, FF), F32),
                pltpu.VMEM((w, FF), F32),
                pltpu.VMEM((8, w), F32),
                pltpu.VMEM((8, FF), F32),
                pltpu.VMEM((self.block, w), F32),
                wr.sems(),
            ],
            compiler_params=params(),
            cost_estimate=cost(2.4e10, 3e7, 3e6),
        )(self.core, wr.place, live, g, x1, act, slope, vec, *wr.arrays)

    def attn_backward(self, g, x, qkv, lse, o, wq, wr, vec, first, after):
        w, t = self.width, self.total
        return call(
            functools.partial(
                attn_backward, first, self.seq, self.rows,
                (len(wq.arrays), len(wr.arrays)), (wq.start, wr.start),
            ),
            after,
            [
                smem(), smem(), smem(), self.tall(w), self.tall(w), self.tall(3 * w),
                self.lse_spec(), self.tall(w), whole(vec.shape),
            ]
            + wq.specs()
            + wr.specs(),
            grid=self.grid,
            out_specs=[
                self.images_spec() if first else self.tall(w),
                whole((w, 2 * w + TILE)), whole((w, 2 * w + TILE)),
            ],
            out_shape=[
                struct((self.images, self.seq, w), F32) if first else struct((t, w), F32),
                struct((w, 2 * w + TILE), BF16), struct((w, 2 * w + TILE), BF16),
            ],
            scratch_shapes=[
                pltpu.VMEM((w, 2 * wq.half), BF16),
                pltpu.VMEM((w, w), BF16),
                pltpu.VMEM((w, 3 * w), F32),
                pltpu.VMEM((w, w), F32),
                pltpu.VMEM((8, w), F32),
                pltpu.VMEM((self.block, 3 * w), BF16),
                pltpu.VMEM((self.block, w), BF16),
                wq.sems(),
                wr.sems(),
            ],
            compiler_params=params(),
            cost_estimate=cost(3e10, 2e7, 3e6),
        )(self.core, wq.place, wr.place, g, x, qkv, lse, o, vec, *wq.arrays, *wr.arrays)


def flip(axis, bit):
    return [(i, i ^ bit) for i in range(lax.axis_size(axis))]


def swap_cores(value):
    return lax.ppermute(value, "rep", flip("rep", 1))


def own_half(packed, core):
    half = packed.shape[1] // 2
    return lax.dynamic_slice_in_dim(packed, core * half, half, 1)


def spread(own):
    return jnp.broadcast_to(own[None], (lax.axis_size("shard"),) + own.shape)


def gather_direct(copies):
    mine = lax.all_to_all(copies, "shard", 0, 0, tiled=True)
    return [mine, swap_cores(mine)], jnp.arange(copies.shape[0], dtype=jnp.int32)


def near_permutes(own):
    count = lax.axis_size("shard")
    me = lax.axis_index("shard").astype(jnp.int32)
    parts = [own] + [lax.ppermute(own, "shard", flip("shard", k)) for k in range(2, count, 2)]
    even = jnp.arange(0, count, 2, dtype=jnp.int32)
    return jnp.stack(parts), jnp.concatenate([me ^ even, me ^ even ^ 1])


def near_exchange(own):
    count = lax.axis_size("shard")
    parity = lax.axis_index("shard").astype(jnp.int32) % 2
    groups = [list(range(p, count, 2)) for p in range(2)]
    near = lax.all_to_all(
        jnp.broadcast_to(own[None], (count // 2,) + own.shape),
        "shard", 0, 0, axis_index_groups=groups, tiled=True,
    )
    even = jnp.arange(0, count, 2, dtype=jnp.int32)
    return near, jnp.concatenate([even + parity, even + 1 - parity])


def after(value, *others):
    return lax.optimization_barrier((value,) + others)[0]


def join_cores(keep, send):
    other = swap_cores(send)
    return (keep.astype(F32) + other.astype(F32)).astype(BF16)


def exchange_shards(joined):
    count = lax.axis_size("shard")
    rows, cols = joined.shape
    return lax.all_to_all(joined.reshape(count, rows // count, cols), "shard", 0, 0, tiled=True)


def finish_group(parts):
    mine = jnp.sum(parts.astype(F32), 0).astype(BF16)
    bit = 2
    while bit < lax.axis_size("rep"):
        other = lax.ppermute(mine, "rep", flip("rep", bit))
        mine = (mine.astype(F32) + other.astype(F32)).astype(BF16)
        bit *= 2
    return mine, swap_cores(mine)


def update_group(core, pair, state, outs, layer, at, cols):
    mine, other = pair
    spec = pl.BlockSpec((1, mine.shape[0], cols), lambda j: (layer, 0, at + j))
    shape = struct(state[0].shape, F32)
    given = list(outs) if outs is not None else []
    return pl.pallas_call(
        functools.partial(step_kernel, len(given)),
        grid=(2,),
        in_specs=[smem(), whole(mine.shape), whole(other.shape), spec, spec, spec]
        + [pl.BlockSpec(memory_space=pl.ANY)] * len(given),
        out_specs=[spec] * 4,
        out_shape=[shape] * 4,
        input_output_aliases={6 + i: i for i in range(len(given))},
        compiler_params=params(),
        cost_estimate=cost(1e6, 4e6, 0),
    )(core, mine, other, *state, *given)


def local(
    tokens, weights, vectors, moment_one, moment_two, vector_one, vector_two, images, cotangent
):
    count, seq, width = tokens.shape
    layers = weights.shape[0]
    core = lax.axis_index("rep") % 2
    core_arr = core.reshape(1).astype(jnp.int32)
    plan = Layers(core_arr, count, seq, width)
    packs = []
    for index in range(layers):
        low = weights[index].astype(BF16)
        turned = jnp.pad(vectors[index].T.astype(BF16), ((0, 0), (0, TILE - vectors.shape[1])))
        attn_pack = jnp.concatenate([low[:, : 3 * width], turned], 1)
        rest = low[:, 3 * width :]
        rest_pack = jnp.pad(rest, ((0, 0), (0, -rest.shape[1] % (2 * TILE))))
        packs.append((own_half(attn_pack, core), own_half(rest_pack, core)))
    attn_own, rest_own = packs[0]
    copies, rest_own = lax.optimization_barrier((spread(attn_own), rest_own))
    arrays, place = gather_direct(copies)
    near, near_place = near_permutes(rest_own)
    gathered = [[Weights(arrays, place, 0, attn_own.shape[1]), None]]
    stored = []
    x = tokens
    for index in range(layers):
        first, last = index == 0, index == layers - 1
        wq = gathered[index][0]
        far = lax.ppermute(near, "shard", flip("shard", 1)) if first else None
        others = [near]
        if not last:
            next_own = after(jnp.concatenate(packs[index + 1], 1), near)
            next_near, next_place = near_exchange(next_own)
        qkv, o, lse, vec, *xp = plan.attn_forward(x, wq, first, others if first else [])
        xp = xp[0] if first else x
        if first:
            held = [near, far, swap_cores(near), swap_cores(after(far, o))]
            gathered[0][1] = Weights(held, near_place, 0, rest_own.shape[1])
        if not last:
            near = after(next_near, o)
            far = lax.ppermute(near, "shard", flip("shard", 1))
            near_other = swap_cores(near)
        x1, act, slope, x = plan.mlp_forward(
            xp, o, gathered[index][1], vec, last, [] if last else [near]
        )
        if not last:
            held = [near, far, near_other, swap_cores(after(far, x1))]
            qhalf, half = (p.shape[1] for p in packs[index + 1])
            gathered.append(
                [Weights(held, next_place, 0, qhalf), Weights(held, next_place, qhalf, half)]
            )
        stored.append((xp, qkv, o, lse, vec, x1, act, slope))
    output = x
    g = cotangent
    state = (moment_one, moment_two, weights)
    groups = []
    before = []

    def send_group(keep, send):
        if groups:
            keep, send, groups[-1] = lax.optimization_barrier((keep, send, groups[-1]))
        joined = join_cores(keep, send)
        groups.append(exchange_shards(joined))
        return [joined]

    for index in reversed(range(layers)):
        first, last = index == 0, index == layers - 1
        wq, wr = gathered[index]
        xp, qkv, o, lse, vec, x1, act, slope = stored[index]
        gx1, keep, send = plan.mlp_backward(images, g, x1, act, slope, wr, vec, last, before)
        before = send_group(keep, send)
        g, keep, send = plan.attn_backward(gx1, xp, qkv, lse, o, wq, wr, vec, first, before)
        before = send_group(keep, send)
    outs = None
    vec_grads = [None] * layers
    for n, index in enumerate(reversed(range(layers))):
        pair_m = finish_group(groups[2 * n])
        pair_a = finish_group(groups[2 * n + 1])
        outs = update_group(core_arr, pair_m, state, outs, index, 1, FF)
        outs = update_group(core_arr, pair_a, state, outs, index, 0, 2 * width)
        tails = [
            jnp.where(core == 0, p[0][:, -TILE:], p[1][:, -TILE:]).astype(F32).T
            for p in (pair_a, pair_m)
        ]
        vec_grads[index] = jnp.concatenate([tails[0][:5], tails[1][:7]], 0)
    vector_grad = jnp.stack(vec_grads)
    weight_grad, moment_one_new, moment_two_new, update = outs
    vector_one_new, vector_two_new, vector_update = adamw(
        vector_grad, vector_one, vector_two, vectors
    )
    return (
        output,
        g,
        weight_grad,
        vector_grad,
        moment_one_new,
        moment_two_new,
        vector_one_new,
        vector_two_new,
        update,
        vector_update,
    )


def solution(mesh):
    in_specs = (
        P(("rep", "shard"), None, None),
        P(None, "shard", None),
        P(None, None, "shard"),
        P(None, "shard", None),
        P(None, "shard", None),
        P(None, None, "shard"),
        P(None, None, "shard"),
        P(("rep", "shard")),
        P(("rep", "shard"), None, None),
    )
    out_specs = (
        P(("rep", "shard"), None, None),
        P(("rep", "shard"), None, None),
        P(None, "shard", None),
        P(None, None, "shard"),
        P(None, "shard", None),
        P(None, "shard", None),
        P(None, None, "shard"),
        P(None, None, "shard"),
        P(None, "shard", None),
        P(None, None, "shard"),
    )
    return jax.shard_map(local, mesh=mesh, in_specs=in_specs, out_specs=out_specs, check_vma=False)
```

profile of v0, /device:TPU:0, one launch (start us, length us, event | category | flops | bytes accessed | tf_op | source)
XLA Modules:
  0.0 293.5 jit_solution(15565264127251777353)
XLA Ops:
  4.0 7.3 %all-to-all-start.1 = ((bf16[8,48,640]{2,1,0:T(8,128)(2,1)}), bf16[8,48,640]{2,1,0:T(8,128)(2,1)S(1)}, u32[]{:S(2)}, u32[]{:S(2)}) async-start(bf16[8,48,640]{2,1,0:T(8,128)(2,1)} %broadcast_in_dim.4), calls=%async_computation.1 | async-start | bytes 983040 | tf_op jit(solution)/shard_map/all_to_all | solution.py:665
  11.2 3.8 %collective-permute-start.2 = (bf16[48,1792]{1,0:T(8,128)(2,1)S(1)}, bf16[48,1792]{1,0:T(8,128)(2,1)S(1)}, u32[]{:S(2)}, u32[]{:S(2)}) collective-permute-start(bf16[48,1792]{1,0:T(8,128)(2,1)S(1)} %pad_dynamic-slice_fusion), channel_id=1, source_target_pairs={{0,6},{1,7},{2,4},{3,5},{4,2},{5,3},{6,0},{7,1},{8,14},{9,15},{10,... | collective-permute-start | bytes 516104 | tf_op jit(solution)/shard_map/ppermute | solution.py:672
  17.0 16.9 %all-to-all-done.1.refs_4_.refs_10_ = bf16[8,48,640]{2,1,0:T(8,128)(2,1)S(1)} async-done(((bf16[8,48,640]{2,1,0:T(8,128)(2,1)}), bf16[8,48,640]{2,1,0:T(8,128)(2,1)S(1)}, u32[]{:S(2)}, u32[]{:S(2)}) %all-to-all-start.1) | async-done | bytes 491552 | tf_op jit(solution)/shard_map/all_to_all | solution.py:665
  33.9 5.9 %collective-permute-done.1 = bf16[48,1792]{1,0:T(8,128)(2,1)S(1)} collective-permute-done((bf16[48,1792]{1,0:T(8,128)(2,1)S(1)}, bf16[48,1792]{1,0:T(8,128)(2,1)S(1)}, u32[]{:S(2)}, u32[]{:S(2)}) %collective-permute-start.1) | collective-permute-done | bytes 172064 | tf_op jit(solution)/shard_map/ppermute | solution.py:672
  42.4 3.5 %all-to-all-start = ((bf16[4,48,2432]{2,1,0:T(8,128)(2,1)}), bf16[4,48,2432]{2,1,0:T(8,128)(2,1)S(1)}, u32[]{:S(2)}, u32[]{:S(2)}) async-start(bf16[4,48,2432]{2,1,0:T(8,128)(2,1)} %broadcast_in_dim.5), calls=%async_computation | async-start | bytes 1867776 | tf_op jit(solution)/shard_map/all_to_all | solution.py:681
  46.7 11.1 %shard_map.168 = (bf16[1664,1152]{1,0:T(8,128)(2,1)}, bf16[1664,384]{1,0:T(8,128)(2,1)}, f32[8,8,256]{2,1,0:T(8,128)}, f32[16,384]{1,0:T(8,128)}, f32[1664,384]{1,0:T(8,128)}) custom-call(bf16[4,48,1792]{2,1,0:T(8,128)(2,1)} %copy-done.6, s32[1]{0:T(128)} %bitcast.refs_1_.refs_0_.core_ref, s32[8]{0:T(128)} %iota.14.refs_2_, ...), custom_call_target="tpu_custom_call" | custom-call | flops 16999999488 | bytes 20000000 | tf_op jit(solution)/shard_map/pallas_call | solution.py:515
  59.0 11.1 %all-to-all-done.refs_0_.refs_3_.refs_5_.refs_8_.refs_10_.refs_14_ = bf16[4,48,2432]{2,1,0:T(8,128)(2,1)S(1)} async-done(((bf16[4,48,2432]{2,1,0:T(8,128)(2,1)}), bf16[4,48,2432]{2,1,0:T(8,128)(2,1)S(1)}, u32[]{:S(2)}, u32[]{:S(2)}) %all-to-all-start) | async-done | bytes 933920 | tf_op jit(solution)/shard_map/all_to_all | solution.py:681
  71.0 14.5 %shard_map.169 = (f32[1664,384]{1,0:T(8,128)}, bf16[1664,1536]{1,0:T(8,128)(2,1)}, f32[1664,1536]{1,0:T(8,128)}, f32[1664,384]{1,0:T(8,128)}) custom-call(bf16[4,48,2432]{2,1,0:T(8,128)(2,1)} %copy-done.3, s32[1]{0:T(128)} %bitcast.refs_1_.refs_0_.core_ref, s32[8]{0:T(128)} %pad_add_fusion.1.refs_2_.refs_3_, f32[1664,384]{1,0:T(8,128)} %get-tuple-element.75.refs_3_.refs_5_, ...), custom_call_target="tpu_custom_call" | custom-call | flops 22000001024 | bytes 30000000 | tf_op jit(solution)/shard_map/pallas_call | solution.py:515
  85.5 6.9 %collective-permute-done.7.refs_4_.refs_6_.refs_9_.refs_11_.refs_15_ = bf16[4,48,2432]{2,1,0:T(8,128)(2,1)S(1)} collective-permute-done((bf16[4,48,2432]{2,1,0:T(8,128)(2,1)S(1)}, bf16[4,48,2432]{2,1,0:T(8,128)(2,1)S(1)}, u32[]{:S(2)}, u32[]{:S(2)}) %collective-permute-start.7) | collective-permute-done | bytes 933920 | tf_op jit(solution)/shard_map/ppermute | solution.py:770
  95.1 11.0 %shard_map.170 = (bf16[1664,1152]{1,0:T(8,128)(2,1)}, bf16[1664,384]{1,0:T(8,128)(2,1)}, f32[8,8,256]{2,1,0:T(8,128)}, f32[16,384]{1,0:T(8,128)}) custom-call(s32[1]{0:T(128)} %bitcast.refs_1_.refs_0_.core_ref, s32[8]{0:T(128)} %pad_add_fusion.refs_1_.refs_2_.refs_3_, f32[1664,384]{1,0:T(8,128)} %get-tuple-element.78.refs_2_.refs_5_, ...), custom_call_target="tpu_custom_call" | custom-call | flops 16999999488 | bytes 20000000 | tf_op jit(solution)/shard_map/pallas_call | solution.py:515
  106.1 14.3 %shard_map.171 = (f32[1664,384]{1,0:T(8,128)}, bf16[1664,1536]{1,0:T(8,128)(2,1)}, f32[1664,1536]{1,0:T(8,128)}, f32[8,197,384]{2,1,0:T(8,128)}) custom-call(s32[1]{0:T(128)} %bitcast.refs_1_.refs_0_.core_ref, s32[8]{0:T(128)} %pad_add_fusion.refs_1_.refs_2_.refs_3_, f32[1664,384]{1,0:T(8,128)} %get-tuple-element.78.refs_2_.refs_5_, ...), custom_call_target="tpu_custom_call" | custom-call | flops 22000001024 | bytes 30000000 | tf_op jit(solution)/shard_map/pallas_call | solution.py:515
  120.4 19.5 %shard_map.172 = (f32[1664,384]{1,0:T(8,128)}, bf16[384,1664]{1,0:T(8,128)(2,1)}, bf16[384,1664]{1,0:T(8,128)(2,1)}) custom-call(s32[1]{0:T(128)} %bitcast.refs_1_.refs_0_.core_ref, s32[8]{0:T(128)} %pad_add_fusion.refs_1_.refs_2_.refs_3_, s32[1]{0:T(128)S(6)} %copy.66.refs_2_.refs_3_, bf16[8,197,384]{2,1,0:T(8,128)(2,1)} %copy.45.refs_3_, ...), custom_call_target="tpu_custom_call" | custom-call | flops 24000000000 | bytes 30000000 | tf_op jit(solution)/shard_map/pallas_call | solution.py:515
  145.8 3.6 %all-to-all-start.2 = ((bf16[8,48,1664]{2,1,0:T(8,128)(2,1)}), bf16[8,48,1664]{2,1,0:T(8,128)(2,1)S(1)}, u32[]{:S(2)}, u32[]{:S(2)}) async-start(bf16[8,48,1664]{2,1,0:T(8,128)(2,1)} %bitcast.11), calls=%async_computation.2 | async-start | bytes 2555904 | tf_op jit(solution)/shard_map/all_to_all | solution.py:701
  149.4 21.8 %shard_map.173 = (f32[1664,384]{1,0:T(8,128)}, bf16[384,896]{1,0:T(8,128)(2,1)}, bf16[384,896]{1,0:T(8,128)(2,1)}) custom-call(bf16[384,1664]{1,0:T(8,128)(2,1)} %add_convert_fusion.1.refs_0_, s32[1]{0:T(128)} %bitcast.refs_1_.refs_0_.core_ref, s32[8]{0:T(128)} %pad_add_fusion.refs_1_.refs_2_.refs_3_, s32[8]{0:T(128)} %pad_add_fusion.refs_1_.refs_2_.refs_3_, ...), custom_call_target="tpu_custom_call" | custom-call | flops 30000001024 | bytes 20000000 | tf_op jit(solution)/shard_map/pallas_call | solution.py:515
  171.2 9.6 %all-to-all-done.2 = bf16[8,48,1664]{2,1,0:T(8,128)(2,1)S(1)} async-done(((bf16[8,48,1664]{2,1,0:T(8,128)(2,1)}), bf16[8,48,1664]{2,1,0:T(8,128)(2,1)S(1)}, u32[]{:S(2)}, u32[]{:S(2)}) %all-to-all-start.2) | async-done | bytes 1277984 | tf_op jit(solution)/shard_map/all_to_all | solution.py:701
  185.2 3.6 %all-to-all-start.3 = ((bf16[8,48,896]{2,1,0:T(8,128)(2,1)}), bf16[8,48,896]{2,1,0:T(8,128)(2,1)S(1)}, u32[]{:S(2)}, u32[]{:S(2)}) async-start(bf16[8,48,896]{2,1,0:T(8,128)(2,1)} %bitcast.12), calls=%async_computation.3 | async-start | bytes 1376256 | tf_op jit(solution)/shard_map/all_to_all | solution.py:701
  188.9 19.6 %shard_map.174 = (f32[1664,384]{1,0:T(8,128)}, bf16[384,1664]{1,0:T(8,128)(2,1)}, bf16[384,1664]{1,0:T(8,128)(2,1)}) custom-call(bf16[384,896]{1,0:T(8,128)(2,1)} %add_convert_fusion.3.refs_0_, s32[1]{0:T(128)} %bitcast.refs_1_.refs_0_.core_ref, s32[8]{0:T(128)} %pad_add_fusion.1.refs_2_.refs_3_, s32[1]{0:T(128)S(6)} %copy.66.refs_2_.refs_3_, ...), custom_call_target="tpu_custom_call" | custom-call | flops 24000000000 | bytes 30000000 | tf_op jit(solution)/shard_map/pallas_call | solution.py:515
  208.6 3.1 %collective-permute-done.12 = bf16[384,1664]{1,0:T(8,128)(2,1)S(1)} collective-permute-done((bf16[384,1664]{1,0:T(8,128)(2,1)}, bf16[384,1664]{1,0:T(8,128)(2,1)S(1)}, u32[]{:S(2)}, u32[]{:S(2)}) %collective-permute-start.12) | collective-permute-done | bytes 1277984 | tf_op jit(solution)/shard_map/ppermute | solution.py:652
  214.4 6.0 %all-to-all-start.4 = ((bf16[8,48,1664]{2,1,0:T(8,128)(2,1)}), bf16[8,48,1664]{2,1,0:T(8,128)(2,1)S(1)}, u32[]{:S(2)}, u32[]{:S(2)}) async-start(bf16[8,48,1664]{2,1,0:T(8,128)(2,1)} %bitcast.37), calls=%async_computation.4 | async-start | bytes 2555904 | tf_op jit(solution)/shard_map/all_to_all | solution.py:701
  220.9 21.9 %shard_map.175 = (f32[8,197,384]{2,1,0:T(8,128)}, bf16[384,896]{1,0:T(8,128)(2,1)}, bf16[384,896]{1,0:T(8,128)(2,1)}) custom-call(bf16[384,1664]{1,0:T(8,128)(2,1)} %add_convert_fusion.refs_0_, s32[1]{0:T(128)} %bitcast.refs_1_.refs_0_.core_ref, s32[8]{0:T(128)} %iota.15.refs_2_, s32[8]{0:T(128)} %pad_add_fusion.1.refs_2_.refs_3_, ...), custom_call_target="tpu_custom_call" | custom-call | flops 30000001024 | bytes 20000000 | tf_op jit(solution)/shard_map/pallas_call | solution.py:515
  242.8 8.6 %all-to-all-done.4 = bf16[8,48,1664]{2,1,0:T(8,128)(2,1)S(1)} async-done(((bf16[8,48,1664]{2,1,0:T(8,128)(2,1)}), bf16[8,48,1664]{2,1,0:T(8,128)(2,1)S(1)}, u32[]{:S(2)}, u32[]{:S(2)}) %all-to-all-start.4) | async-done | bytes 1277984 | tf_op jit(solution)/shard_map/all_to_all | solution.py:701
  251.4 3.6 %copy.52 = f32[8,197,384]{2,0,1:T(8,128)} copy(f32[8,197,384]{2,1,0:T(8,128)} %get-tuple-element.140) | data formatting | bytes 4841472
  259.7 3.6 %all-to-all-start.5 = ((bf16[8,48,896]{2,1,0:T(8,128)(2,1)}), bf16[8,48,896]{2,1,0:T(8,128)(2,1)S(1)}, u32[]{:S(2)}, u32[]{:S(2)}) async-start(bf16[8,48,896]{2,1,0:T(8,128)(2,1)} %bitcast.14), calls=%async_computation.5 | async-start | bytes 1376256 | tf_op jit(solution)/shard_map/all_to_all | solution.py:701
  275.5 6.1 %all-to-all-done.5 = bf16[8,48,896]{2,1,0:T(8,128)(2,1)S(1)} async-done(((bf16[8,48,896]{2,1,0:T(8,128)(2,1)}), bf16[8,48,896]{2,1,0:T(8,128)(2,1)S(1)}, u32[]{:S(2)}, u32[]{:S(2)}) %all-to-all-start.5) | async-done | bytes 688160 | tf_op jit(solution)/shard_map/all_to_all | solution.py:701
  (137 shorter events, 54.9 us)
Async XLA Ops:
  4.0 29.9 %all-to-all-start.1 = ((bf16[8,48,640]{2,1,0:T(8,128)(2,1)}), bf16[8,48,640]{2,1,0:T(8,128)(2,1)S(1)}, u32[]{:S(2)}, u32[]{:S(2)}) async-start(bf16[8,48,640]{2,1,0:T(8,128)(2,1)} %broadcast_in_dim.4), calls=%async_computation.1 | async-start | bytes 983040 | tf_op jit(solution)/shard_map/all_to_all | solution.py:665
  11.2 22.7 %collective-permute-start.2 = (bf16[48,1792]{1,0:T(8,128)(2,1)S(1)}, bf16[48,1792]{1,0:T(8,128)(2,1)S(1)}, u32[]{:S(2)}, u32[]{:S(2)}) collective-permute-start(bf16[48,1792]{1,0:T(8,128)(2,1)S(1)} %pad_dynamic-slice_fusion), channel_id=1, source_target_pairs={{0,6},{1,7},{2,4},{3,5},{4,2},{5,3},{6,0},{7,1},{8,14},{9,15},{10,... | collective-permute-start | bytes 516104 | tf_op jit(solution)/shard_map/ppermute | solution.py:672
  15.1 24.7 %collective-permute-start.1 = (bf16[48,1792]{1,0:T(8,128)(2,1)S(1)}, bf16[48,1792]{1,0:T(8,128)(2,1)S(1)}, u32[]{:S(2)}, u32[]{:S(2)}) collective-permute-start(bf16[48,1792]{1,0:T(8,128)(2,1)S(1)} %pad_dynamic-slice_fusion), channel_id=1, source_target_pairs={{0,4},{1,5},{2,6},{3,7},{4,0},{5,1},{6,2},{7,3},{8,12},{9,13},{10,... | collective-permute-start | bytes 516104 | tf_op jit(solution)/shard_map/ppermute | solution.py:672
  15.1 24.7 %collective-permute-start = (bf16[48,1792]{1,0:T(8,128)(2,1)S(1)}, bf16[48,1792]{1,0:T(8,128)(2,1)S(1)}, u32[]{:S(2)}, u32[]{:S(2)}) collective-permute-start(bf16[48,1792]{1,0:T(8,128)(2,1)S(1)} %pad_dynamic-slice_fusion), channel_id=1, source_target_pairs={{0,2},{1,3},{2,0},{3,1},{4,6},{5,7},{6,4},{7,5},{8,10},{9,11},{10,... | collective-permute-start | bytes 516104 | tf_op jit(solution)/shard_map/ppermute | solution.py:672
  33.9 12.1 %collective-permute-start.3 = (bf16[8,48,640]{2,1,0:T(8,128)(2,1)S(1)}, bf16[8,48,640]{2,1,0:T(8,128)(2,1)S(1)}, u32[]{:S(2)}, u32[]{:S(2)}) collective-permute-start(bf16[8,48,640]{2,1,0:T(8,128)(2,1)S(1)} %all-to-all-done.1.refs_4_.refs_10_), channel_id=1, source_target_pairs={{0,8},{8,0},{16,24},{24,16},{1,9},{9,1},{17,25},{25,17},{2,10},{10... | collective-permute-start | bytes 1474568 | tf_op jit(solution)/shard_map/ppermute | solution.py:652
  39.9 17.9 %collective-permute-start.4 = (bf16[4,48,1792]{2,1,0:T(8,128)(2,1)S(1)}, bf16[4,48,1792]{2,1,0:T(8,128)(2,1)}, u32[]{:S(2)}, u32[]{:S(2)}) collective-permute-start(bf16[4,48,1792]{2,1,0:T(8,128)(2,1)S(1)} %pad_maximum_fusion.refs_0_.refs_6_.refs_9_.refs_12_), channel_id=1, source_target_pairs={{0,1},{1,0},{2,3},{3,2},{4,5},{5,4},{6,7},{7,6},{8,9},{9,8},{10,11... | collective-permute-start | bytes 2064392 | tf_op jit(solution)/shard_map/ppermute | solution.py:758
  41.4 29.3 %collective-permute-start.5 = (bf16[4,48,1792]{2,1,0:T(8,128)(2,1)S(1)}, bf16[4,48,1792]{2,1,0:T(8,128)(2,1)}, u32[]{:S(2)}, u32[]{:S(2)}) collective-permute-start(bf16[4,48,1792]{2,1,0:T(8,128)(2,1)S(1)} %pad_maximum_fusion.refs_0_.refs_6_.refs_9_.refs_12_), channel_id=1, source_target_pairs={{0,8},{8,0},{16,24},{24,16},{1,9},{9,1},{17,25},{25,17},{2,10},{10... | collective-permute-start | bytes 2064392 | tf_op jit(solution)/shard_map/ppermute | solution.py:652
  42.4 27.7 %all-to-all-start = ((bf16[4,48,2432]{2,1,0:T(8,128)(2,1)}), bf16[4,48,2432]{2,1,0:T(8,128)(2,1)S(1)}, u32[]{:S(2)}, u32[]{:S(2)}) async-start(bf16[4,48,2432]{2,1,0:T(8,128)(2,1)} %broadcast_in_dim.5), calls=%async_computation | async-start | bytes 1867776 | tf_op jit(solution)/shard_map/all_to_all | solution.py:681
  57.8 12.8 %collective-permute-start.6 = (bf16[4,48,1792]{2,1,0:T(8,128)(2,1)}, bf16[4,48,1792]{2,1,0:T(8,128)(2,1)}, u32[]{:S(2)}, u32[]{:S(2)}) collective-permute-start(bf16[4,48,1792]{2,1,0:T(8,128)(2,1)} %collective-permute-done.4.refs_7_.refs_10_.refs_13_), channel_id=1, source_target_pairs={{0,8},{8,0},{16,24},{24,16},{1,9},{9,1},{17,25},{25,17},{2,10},{10... | collective-permute-start | bytes 2064392 | tf_op jit(solution)/shard_map/ppermute | solution.py:652
  70.1 22.3 %collective-permute-start.7 = (bf16[4,48,2432]{2,1,0:T(8,128)(2,1)S(1)}, bf16[4,48,2432]{2,1,0:T(8,128)(2,1)S(1)}, u32[]{:S(2)}, u32[]{:S(2)}) collective-permute-start(bf16[4,48,2432]{2,1,0:T(8,128)(2,1)S(1)} %all-to-all-done.refs_0_.refs_3_.refs_5_.refs_8_.refs_10_.refs_14_), channel_id=1, source_target_pairs={{0,1},{1,0},{2,3},{3,2},{4,5},{5,4},{6,7},{7,6},{8,9},{9,8},{10,11... | collective-permute-start | bytes 2801672 | tf_op jit(solution)/shard_map/ppermute | solution.py:770
  70.7 24.2 %collective-permute-start.8 = (bf16[4,48,2432]{2,1,0:T(8,128)(2,1)S(1)}, bf16[4,48,2432]{2,1,0:T(8,128)(2,1)}, u32[]{:S(2)}, u32[]{:S(2)}) collective-permute-start(bf16[4,48,2432]{2,1,0:T(8,128)(2,1)S(1)} %all-to-all-done.refs_0_.refs_3_.refs_5_.refs_8_.refs_10_.refs_14_), channel_id=1, source_target_pairs={{0,8},{8,0},{16,24},{24,16},{1,9},{9,1},{17,25},{25,17},{2,10},{10... | collective-permute-start | bytes 2801672 | tf_op jit(solution)/shard_map/ppermute | solution.py:652
  139.9 3.3 %collective-permute-start.10 = (bf16[384,1664]{1,0:T(8,128)(2,1)}, bf16[384,1664]{1,0:T(8,128)(2,1)S(1)}, u32[]{:S(2)}, u32[]{:S(2)}) collective-permute-start(bf16[384,1664]{1,0:T(8,128)(2,1)} %get-tuple-element.88), channel_id=1, source_target_pairs={{0,8},{8,0},{16,24},{24,16},{1,9},{9,1},{17,25},{25,17},{2,10},{10... | collective-permute-start | bytes 3833864 | tf_op jit(solution)/shard_map/ppermute | solution.py:652
  145.8 35.0 %all-to-all-start.2 = ((bf16[8,48,1664]{2,1,0:T(8,128)(2,1)}), bf16[8,48,1664]{2,1,0:T(8,128)(2,1)S(1)}, u32[]{:S(2)}, u32[]{:S(2)}) async-start(bf16[8,48,1664]{2,1,0:T(8,128)(2,1)} %bitcast.11), calls=%async_computation.2 | async-start | bytes 2555904 | tf_op jit(solution)/shard_map/all_to_all | solution.py:701
  185.2 23.2 %all-to-all-start.3 = ((bf16[8,48,896]{2,1,0:T(8,128)(2,1)}), bf16[8,48,896]{2,1,0:T(8,128)(2,1)S(1)}, u32[]{:S(2)}, u32[]{:S(2)}) async-start(bf16[8,48,896]{2,1,0:T(8,128)(2,1)} %bitcast.12), calls=%async_computation.3 | async-start | bytes 1376256 | tf_op jit(solution)/shard_map/all_to_all | solution.py:701
  208.5 3.3 %collective-permute-start.12 = (bf16[384,1664]{1,0:T(8,128)(2,1)}, bf16[384,1664]{1,0:T(8,128)(2,1)S(1)}, u32[]{:S(2)}, u32[]{:S(2)}) collective-permute-start(bf16[384,1664]{1,0:T(8,128)(2,1)} %get-tuple-element.102), channel_id=1, source_target_pairs={{0,8},{8,0},{16,24},{24,16},{1,9},{9,1},{17,25},{25,17},{2,10},{10... | collective-permute-start | bytes 3833864 | tf_op jit(solution)/shard_map/ppermute | solution.py:652
  214.4 37.0 %all-to-all-start.4 = ((bf16[8,48,1664]{2,1,0:T(8,128)(2,1)}), bf16[8,48,1664]{2,1,0:T(8,128)(2,1)S(1)}, u32[]{:S(2)}, u32[]{:S(2)}) async-start(bf16[8,48,1664]{2,1,0:T(8,128)(2,1)} %bitcast.37), calls=%async_computation.4 | async-start | bytes 2555904 | tf_op jit(solution)/shard_map/all_to_all | solution.py:701
  251.4 6.0 %collective-permute-start.13 = (bf16[384,896]{1,0:T(8,128)(2,1)}, bf16[384,896]{1,0:T(8,128)(2,1)}, u32[]{:S(2)}, u32[]{:S(2)}) collective-permute-start(bf16[384,896]{1,0:T(8,128)(2,1)} %get-tuple-element.110), channel_id=1, source_target_pairs={{0,8},{8,0},{16,24},{24,16},{1,9},{9,1},{17,25},{25,17},{2,10},{10... | collective-permute-start | bytes 2064392 | tf_op jit(solution)/shard_map/ppermute | solution.py:652
  255.2 8.2 %collective-permute-start.20 = (bf16[48,1664]{1,0:T(8,128)(2,1)S(1)}, bf16[48,1664]{1,0:T(8,128)(2,1)S(1)}, u32[]{:S(2)}, u32[]{:S(2)}) collective-permute-start(bf16[48,1664]{1,0:T(8,128)(2,1)S(1)} %reduce_sum.51), channel_id=1, source_target_pairs={{0,16},{8,24},{16,0},{24,8},{1,17},{9,25},{17,1},{25,9},{2,18},{10... | collective-permute-start | bytes 479240 | tf_op jit(solution)/shard_map/ppermute | solution.py:708
  256.8 6.8 %collective-permute-start.18 = (bf16[48,896]{1,0:T(8,128)(2,1)S(1)}, bf16[48,896]{1,0:T(8,128)(2,1)S(1)}, u32[]{:S(2)}, u32[]{:S(2)}) collective-permute-start(bf16[48,896]{1,0:T(8,128)(2,1)S(1)} %reduce_sum.50), channel_id=1, source_target_pairs={{0,16},{8,24},{16,0},{24,8},{1,17},{9,25},{17,1},{25,9},{2,18},{10... | collective-permute-start | bytes 258056 | tf_op jit(solution)/shard_map/ppermute | solution.py:708
  259.7 21.9 %all-to-all-start.5 = ((bf16[8,48,896]{2,1,0:T(8,128)(2,1)}), bf16[8,48,896]{2,1,0:T(8,128)(2,1)S(1)}, u32[]{:S(2)}, u32[]{:S(2)}) async-start(bf16[8,48,896]{2,1,0:T(8,128)(2,1)} %bitcast.14), calls=%async_computation.5 | async-start | bytes 1376256 | tf_op jit(solution)/shard_map/all_to_all | solution.py:701
  263.6 6.7 %collective-permute-start.19 = (bf16[48,896]{1,0:T(8,128)(2,1)S(1)}, bf16[48,896]{1,0:T(8,128)(2,1)S(1)}, u32[]{:S(2)}, u32[]{:S(2)}) collective-permute-start(bf16[48,896]{1,0:T(8,128)(2,1)S(1)} %add_convert_fusion.6.mine_ref), channel_id=1, source_target_pairs={{0,8},{8,0},{16,24},{24,16},{1,9},{9,1},{17,25},{25,17},{2,10},{10... | collective-permute-start | bytes 258056 | tf_op jit(solution)/shard_map/ppermute | solution.py:652
  268.8 14.4 %collective-permute-start.16 = (bf16[48,1664]{1,0:T(8,128)(2,1)S(1)}, bf16[48,1664]{1,0:T(8,128)(2,1)S(1)}, u32[]{:S(2)}, u32[]{:S(2)}) collective-permute-start(bf16[48,1664]{1,0:T(8,128)(2,1)S(1)} %reduce_sum.49), channel_id=1, source_target_pairs={{0,16},{8,24},{16,0},{24,8},{1,17},{9,25},{17,1},{25,9},{2,18},{10... | collective-permute-start | bytes 479240 | tf_op jit(solution)/shard_map/ppermute | solution.py:708
  281.7 4.6 %collective-permute-start.14 = (bf16[48,896]{1,0:T(8,128)(2,1)S(1)}, bf16[48,896]{1,0:T(8,128)(2,1)S(1)}, u32[]{:S(2)}, u32[]{:S(2)}) collective-permute-start(bf16[48,896]{1,0:T(8,128)(2,1)S(1)} %reduce_sum.48), channel_id=1, source_target_pairs={{0,16},{8,24},{16,0},{24,8},{1,17},{9,25},{17,1},{25,9},{2,18},{10... | collective-permute-start | bytes 258056 | tf_op jit(solution)/shard_map/ppermute | solution.py:708
  286.3 3.9 %collective-permute-start.15 = (bf16[48,896]{1,0:T(8,128)(2,1)S(1)}, bf16[48,896]{1,0:T(8,128)(2,1)S(1)}, u32[]{:S(2)}, u32[]{:S(2)}) collective-permute-start(bf16[48,896]{1,0:T(8,128)(2,1)S(1)} %add_convert_fusion.7.mine_ref), channel_id=1, source_target_pairs={{0,8},{8,0},{16,24},{24,16},{1,9},{9,1},{17,25},{25,17},{2,10},{10... | collective-permute-start | bytes 258056 | tf_op jit(solution)/shard_map/ppermute | solution.py:652
  (25 other events, 99.1 us)
where the time goes:
time: 295 us; the launch traced here: 294 us
  Pallas kernels  145 us (49%)
  waiting for transfers between devices  77.2 us (26%)
  starting transfers between devices  41.3 us (14%)
  local copies, waits for them, and re-layouts  14.3 us (5%)
  other arithmetic  14.1 us (5%)
    pallas_call x8, Pallas kernels, call(): return lambda *args: made(*after, *args)  134 us
    all_to_all x4, waiting for transfers between devices, exchange_shards(): lax.all_to_all(joined.reshape(count, rows // count, cols), 'shard', 0, 0,...  24.2 us
    all_to_all x1, waiting for transfers between devices, gather_direct(): mine = lax.all_to_all(copies, 'shard', 0, 0, tiled=True)  16.9 us
    all_to_all x4, starting transfers between devices, exchange_shards(): lax.all_to_all(joined.reshape(count, rows // count, cols), 'shard', 0, 0,...  16.8 us
    all_to_all x1, waiting for transfers between devices, near_exchange(): lax.all_to_all(jnp.broadcast_to(own[None], (count // 2,) + own.shape), 's...  11.1 us
    pallas_call x4, Pallas kernels, update_group(): pl.pallas_call(functools.partial(step_kernel, len(given)), grid=(2,), in_...  11.1 us
    unnamed x47, local copies, waits for them, and re-layouts  10.3 us
    convert_element_type x4, other arithmetic, join_cores(): return (keep.astype(F32) + other.astype(F32)).astype(BF16)  9.76 us
  transfers between devices with their start and end apart: 28, of which 14 were waited for; matrix products, arithmetic and copies ran while one was open for 5% of the time, Pallas kernels for 33%

commit v1 on v0

--- a/solution.py
+++ b/solution.py
@@ -57,16 +57,22 @@
     return jnp.concatenate([vec_ref[8 + j : 9 + j, :] for j in range(FF // width)], 1)
 
 
-def load_weights(core_ref, place_ref, sources, start, whole_ref, sems):
+def weight_copies(core_ref, place_ref, sources, start, whole_ref, sems):
     half = whole_ref.shape[1] // 2
     per_core = len(sources) // 2
     copies = []
     for n, source in enumerate(sources):
         at = core_ref[0] if n < per_core else 1 - core_ref[0]
         cols = pl.ds(pl.multiple_of(at * half, TILE), half)
+        base = sum(piece.shape[0] for piece in sources[: n % per_core])
         copies += row_copies(
-            place_ref, source, n % per_core, slice(start, start + half), whole_ref, cols, sems, len(copies)
+            place_ref, source, base, slice(start, start + half), whole_ref, cols, sems, len(copies)
         )
+    return copies
+
+
+def load_weights(*args):
+    copies = weight_copies(*args)
     for copy in copies:
         copy.start()
     for copy in copies:
@@ -81,7 +87,8 @@
         copies = []
         for n, source in enumerate(chosen):
             copies += row_copies(
-                place_ref, source, n, slice(start, start + size), whole_ref, slice(0, size), sems, len(copies)
+                place_ref, source, len(copies), slice(start, start + size), whole_ref, slice(0, size), sems,
+                len(copies),
             )
         for copy in copies:
             copy.start()
@@ -97,11 +104,11 @@
         load(sources[per_core:])
 
 
-def row_copies(place_ref, source, nth, taken, whole_ref, cols, sems, at):
+def row_copies(place_ref, source, base, taken, whole_ref, cols, sems, at):
     count, rows = source.shape[:2]
     copies = []
     for k in range(count):
-        row = pl.multiple_of(place_ref[nth * count + k] * rows, rows)
+        row = pl.multiple_of(place_ref[base + k] * rows, rows)
         copies.append(
             pltpu.make_async_copy(
                 source.at[k, :, taken], whole_ref.at[pl.ds(row, rows), cols], sems.at[at + k]
@@ -183,9 +190,11 @@
     x1_ref, act_ref, slope_ref, out_ref, w_ref, sems = refs
     width = x_ref.shape[1]
 
-    @pl.when(pl.program_id(0) == 0)
-    def _():
-        load_weights(core_ref, place_ref, sources, start, w_ref, sems)
+    if at:
+
+        @pl.when(pl.program_id(0) == 0)
+        def _():
+            load_weights(core_ref, place_ref, sources, start, w_ref, sems)
 
     x1 = x_ref[...] + dot(o_ref[...], w_ref[:, :width]) + vec_ref[4:5, :]
     x1_ref[...] = x1
@@ -261,13 +270,13 @@
     width = x1_ref.shape[1]
     step = pl.program_id(0)
 
-    @pl.when(step == 0)
-    def _():
-        load_weights(core_ref, place_ref, sources, start, w_ref, sems)
-        up_ref[...] = jnp.zeros_like(up_ref)
-        bias_ref[...] = jnp.zeros_like(bias_ref)
-        down_ref[...] = jnp.zeros_like(down_ref)
-        acc_ref[...] = jnp.zeros_like(acc_ref)
+    if at:
+
+        @pl.when(step == 0)
+        def _():
+            load_weights(core_ref, place_ref, sources, start, w_ref, sems)
+            for ref in (up_ref, down_ref, acc_ref, bias_ref):
+                ref[...] = jnp.zeros_like(ref)
 
     if last:
         for i in range(PAIR):
@@ -336,6 +345,40 @@
         put_grads(core_ref[0], up, down, keep_ref, send_ref)
 
 
+def last_layer(seq, rows, at, starts, core_ref, place_ref, live_ref, x_ref, g_ref, *refs):
+    sources, refs = refs[:at], refs[at:]
+    (qkv_ref, o_ref, lse_ref, vec_ref, out_ref, gx1_ref, keep_ref, send_ref,
+     wq_ref, wr_ref, x1_ref, act_ref, slope_ref, up_ref, down_ref, acc_ref, bias_ref, gp_ref, sems, rsems) = refs
+    step = pl.program_id(0)
+    copies = weight_copies(core_ref, place_ref, sources, starts[1], wr_ref, rsems)
+
+    @pl.when(step == 0)
+    def _():
+        for copy in copies:
+            copy.start()
+        for ref in (up_ref, down_ref, acc_ref, bias_ref):
+            ref[...] = jnp.zeros_like(ref)
+
+    attn_forward(
+        False, seq, rows, at, starts[0], core_ref, place_ref, x_ref, *sources,
+        qkv_ref, o_ref, lse_ref, vec_ref, wq_ref, sems,
+    )
+
+    @pl.when(step == 0)
+    def _():
+        for copy in copies:
+            copy.wait()
+
+    mlp_forward(
+        True, seq, rows, 0, 0, core_ref, place_ref, x_ref, o_ref, vec_ref,
+        x1_ref, act_ref, slope_ref, out_ref, wr_ref, rsems,
+    )
+    mlp_backward(
+        True, seq, rows, 0, 0, core_ref, place_ref, live_ref, g_ref, x1_ref, act_ref, slope_ref, vec_ref,
+        gx1_ref, keep_ref, send_ref, wr_ref, up_ref, down_ref, acc_ref, bias_ref, gp_ref, rsems,
+    )
+
+
 def attn_backward(
     first, seq, rows, ats, starts, core_ref, qplace_ref, place_ref, g_ref, x_ref, qkv_ref, lse_ref, o_ref,
     vec_ref, *refs
@@ -451,12 +494,12 @@
     return (first_new, second_new, change)
 
 
-def step_kernel(aliased, core_ref, mine_ref, other_ref, one_ref, two_ref, old_ref, *refs):
+def step_kernel(start, core_ref, mine_ref, other_ref, one_ref, two_ref, old_ref, *refs):
     grad_ref, one_new_ref, two_new_ref, change_ref = refs[-4:]
-    cols = grad_ref.shape[2]
+    cols = slice(start, start + grad_ref.shape[2])
 
     def put(from_ref):
-        grad = from_ref[:, :cols].astype(F32)
+        grad = from_ref[:, cols].astype(F32)
         grad_ref[0] = grad
         one_new_ref[0], two_new_ref[0], change_ref[0] = adamw(grad, one_ref[0], two_ref[0], old_ref[0])
 
@@ -604,6 +647,43 @@
             compiler_params=params(),
             cost_estimate=cost(2.4e10, 3e7, 3e6),
         )(self.core, wr.place, live, g, x1, act, slope, vec, *wr.arrays)
+
+    def last_layer(self, live, x, g, wq, wr):
+        w, t = self.width, self.total
+        outs = [
+            (self.tall(3 * w), struct((t, 3 * w), BF16)),
+            (self.tall(w), struct((t, w), BF16)),
+            (self.lse_spec(), struct((self.images, 8, 256), F32)),
+            (whole((16, w)), struct((16, w), F32)),
+            (self.images_spec(), struct((self.images, self.seq, w), F32)),
+            (self.tall(w), struct((t, w), F32)),
+            (whole((w, FF + TILE)), struct((w, FF + TILE), BF16)),
+            (whole((w, FF + TILE)), struct((w, FF + TILE), BF16)),
+        ]
+        return call(
+            functools.partial(last_layer, self.seq, self.rows, len(wq.arrays), (wq.start, wr.start)),
+            [],
+            [smem(), smem(), smem(), self.tall(w), self.images_spec()] + wq.specs(),
+            grid=self.grid,
+            out_specs=[o[0] for o in outs],
+            out_shape=[o[1] for o in outs],
+            scratch_shapes=[
+                pltpu.VMEM((w, 2 * wq.half), BF16),
+                pltpu.VMEM((w, 2 * wr.half), BF16),
+                pltpu.VMEM((self.block, w), F32),
+                pltpu.VMEM((self.block, FF), BF16),
+                pltpu.VMEM((self.block, FF), F32),
+                pltpu.VMEM((w, FF), F32),
+                pltpu.VMEM((w, FF), F32),
+                pltpu.VMEM((8, w), F32),
+                pltpu.VMEM((8, FF), F32),
+                pltpu.VMEM((self.block, w), F32),
+                wq.sems(),
+                wr.sems(),
+            ],
+            compiler_params=params(),
+            cost_estimate=cost(4.5e10, 3e7, 3e6),
+        )(self.core, wq.place, live, x, g, *wq.arrays)
 
     def attn_backward(self, g, x, qkv, lse, o, wq, wr, vec, first, after):
         w, t = self.width, self.total
@@ -666,28 +746,57 @@
     return [mine, swap_cores(mine)], jnp.arange(copies.shape[0], dtype=jnp.int32)
 
 
-def near_permutes(own):
-    count = lax.axis_size("shard")
-    me = lax.axis_index("shard").astype(jnp.int32)
-    parts = [own] + [lax.ppermute(own, "shard", flip("shard", k)) for k in range(2, count, 2)]
-    even = jnp.arange(0, count, 2, dtype=jnp.int32)
-    return jnp.stack(parts), jnp.concatenate([me ^ even, me ^ even ^ 1])
-
-
-def near_exchange(own):
-    count = lax.axis_size("shard")
-    parity = lax.axis_index("shard").astype(jnp.int32) % 2
-    groups = [list(range(p, count, 2)) for p in range(2)]
-    near = lax.all_to_all(
-        jnp.broadcast_to(own[None], (count // 2,) + own.shape),
-        "shard", 0, 0, axis_index_groups=groups, tiled=True,
-    )
-    even = jnp.arange(0, count, 2, dtype=jnp.int32)
-    return near, jnp.concatenate([even + parity, even + 1 - parity])
+class Gathering:
+    def __init__(self, own):
+        self.near = [own[None]]
+        self.far = [self.neighbour(self.near[0])]
+        self.ids = [0]
+
+    @staticmethod
+    def neighbour(piece):
+        return lax.ppermute(piece, "shard", flip("shard", 1))
+
+    def step(self, bit, anchor=None):
+        have = self.near[0] if len(self.near) == 1 else jnp.concatenate(self.near, 0)
+        have = have if anchor is None else after(have, anchor)
+        self.near.append(lax.ppermute(have, "shard", flip("shard", bit)))
+        self.ids += [i ^ bit for i in self.ids]
+
+    def pass_on(self, *anchors):
+        piece = after(self.near[-1], *anchors) if anchors else self.near[-1]
+        self.far.append(self.neighbour(piece))
+
+    def held(self, anchor=None):
+        pieces = self.near + self.far
+        if anchor is not None:
+            pieces[-1] = after(pieces[-1], anchor)
+        return pieces + [swap_cores(p) for p in pieces]
+
+    def place(self):
+        me = lax.axis_index("shard").astype(jnp.int32)
+        return me ^ jnp.array(self.ids + [i ^ 1 for i in self.ids], jnp.int32)
 
 
 def after(value, *others):
     return lax.optimization_barrier((value,) + others)[0]
+
+
+def turn_kernel(in_ref, out_ref):
+    for i in range(in_ref.shape[0]):
+        out_ref[:, i, :] = in_ref[i]
+
+
+def turn_images(value):
+    images, seq, width = value.shape
+    return pl.pallas_call(
+        turn_kernel,
+        grid=(width // TILE,),
+        in_specs=[pl.BlockSpec((images, seq, TILE), lambda i: (0, 0, i))],
+        out_specs=pl.BlockSpec((seq, images, TILE), lambda i: (0, 0, i)),
+        out_shape=struct((seq, images, width), value.dtype),
+        compiler_params=params(),
+        cost_estimate=cost(1e6, 5e6, 0),
+    )(value)
 
 
 def join_cores(keep, send):
@@ -701,8 +810,8 @@
     return lax.all_to_all(joined.reshape(count, rows // count, cols), "shard", 0, 0, tiled=True)
 
 
-def finish_group(parts):
-    mine = jnp.sum(parts.astype(F32), 0).astype(BF16)
+def finish_groups(groups):
+    mine = jnp.concatenate([jnp.sum(parts.astype(F32), 0).astype(BF16) for parts in groups], 1)
     bit = 2
     while bit < lax.axis_size("rep"):
         other = lax.ppermute(mine, "rep", flip("rep", bit))
@@ -711,13 +820,13 @@
     return mine, swap_cores(mine)
 
 
-def update_group(core, pair, state, outs, layer, at, cols):
+def update_group(core, pair, start, state, outs, layer, at, cols):
     mine, other = pair
     spec = pl.BlockSpec((1, mine.shape[0], cols), lambda j: (layer, 0, at + j))
     shape = struct(state[0].shape, F32)
     given = list(outs) if outs is not None else []
     return pl.pallas_call(
-        functools.partial(step_kernel, len(given)),
+        functools.partial(step_kernel, start),
         grid=(2,),
         in_specs=[smem(), whole(mine.shape), whole(other.shape), spec, spec, spec]
         + [pl.BlockSpec(memory_space=pl.ANY)] * len(given),
@@ -745,73 +854,103 @@
         rest = low[:, 3 * width :]
         rest_pack = jnp.pad(rest, ((0, 0), (0, -rest.shape[1] % (2 * TILE))))
         packs.append((own_half(attn_pack, core), own_half(rest_pack, core)))
+    bits = []
+    bit = lax.axis_size("shard") // 2
+    while bit > 1:
+        bits.append(bit)
+        bit //= 2
     attn_own, rest_own = packs[0]
     copies, rest_own = lax.optimization_barrier((spread(attn_own), rest_own))
     arrays, place = gather_direct(copies)
-    near, near_place = near_permutes(rest_own)
+    rest = Gathering(rest_own)
+    for bit in bits:
+        rest.step(bit)
+        if bit != bits[-1]:
+            rest.pass_on()
     gathered = [[Weights(arrays, place, 0, attn_own.shape[1]), None]]
     stored = []
     x = tokens
     for index in range(layers):
         first, last = index == 0, index == layers - 1
-        wq = gathered[index][0]
-        far = lax.ppermute(near, "shard", flip("shard", 1)) if first else None
-        others = [near]
         if not last:
-            next_own = after(jnp.concatenate(packs[index + 1], 1), near)
-            next_near, next_place = near_exchange(next_own)
-        qkv, o, lse, vec, *xp = plan.attn_forward(x, wq, first, others if first else [])
+            ahead = Gathering(after(jnp.concatenate(packs[index + 1], 1), rest.near[1]))
+            for bit in bits[:-1]:
+                ahead.step(bit)
+        if last and not first:
+            qkv, o, lse, vec, output, *tail = plan.last_layer(images, x, cotangent, *gathered[index])
+            stored.append((x, qkv, o, lse, vec, None, None, None))
+            break
+        qkv, o, lse, vec, *xp = plan.attn_forward(
+            x, gathered[index][0], first, [rest.near[1]] if first else []
+        )
         xp = xp[0] if first else x
         if first:
-            held = [near, far, swap_cores(near), swap_cores(after(far, o))]
-            gathered[0][1] = Weights(held, near_place, 0, rest_own.shape[1])
+            rest.pass_on(o, rest.far[-1])
+            gathered[0][1] = Weights(rest.held(o), rest.place(), 0, rest_own.shape[1])
         if not last:
-            near = after(next_near, o)
-            far = lax.ppermute(near, "shard", flip("shard", 1))
-            near_other = swap_cores(near)
+            ahead.pass_on(o)
+            ahead.step(bits[-1], o)
         x1, act, slope, x = plan.mlp_forward(
-            xp, o, gathered[index][1], vec, last, [] if last else [near]
+            xp, o, gathered[index][1], vec, last, [] if last else [ahead.near[-1]]
         )
         if not last:
-            held = [near, far, near_other, swap_cores(after(far, x1))]
+            ahead.pass_on()
+            held = ahead.held(x1)
             qhalf, half = (p.shape[1] for p in packs[index + 1])
             gathered.append(
-                [Weights(held, next_place, 0, qhalf), Weights(held, next_place, qhalf, half)]
+                [Weights(held, ahead.place(), 0, qhalf), Weights(held, ahead.place(), qhalf, half)]
             )
         stored.append((xp, qkv, o, lse, vec, x1, act, slope))
-    output = x
-    g = cotangent
+    g = None
     state = (moment_one, moment_two, weights)
-    groups = []
-    before = []
-
-    def send_group(keep, send):
-        if groups:
-            keep, send, groups[-1] = lax.optimization_barrier((keep, send, groups[-1]))
-        joined = join_cores(keep, send)
-        groups.append(exchange_shards(joined))
-        return [joined]
-
+    outs, turned = None, None
+    tails = {}
+
+    def finish(done, outs):
+        pair = finish_groups([parts for parts, _ in done])
+        start = 0
+        for _, spot in done:
+            outs = update_group(core_arr, pair, start, state, outs, *spot)
+            start += spot[2]
+            mine, other = (p[:, start : start + TILE] for p in pair)
+            tails[spot[:2]] = jnp.where(core == 0, mine, other).astype(F32).T
+            start += TILE
+        return outs
+
+    groups, before = [], []
     for index in reversed(range(layers)):
         first, last = index == 0, index == layers - 1
         wq, wr = gathered[index]
         xp, qkv, o, lse, vec, x1, act, slope = stored[index]
-        gx1, keep, send = plan.mlp_backward(images, g, x1, act, slope, wr, vec, last, before)
-        before = send_group(keep, send)
-        g, keep, send = plan.attn_backward(gx1, xp, qkv, lse, o, wq, wr, vec, first, before)
-        before = send_group(keep, send)
-    outs = None
-    vec_grads = [None] * layers
-    for n, index in enumerate(reversed(range(layers))):
-        pair_m = finish_group(groups[2 * n])
-        pair_a = finish_group(groups[2 * n + 1])
-        outs = update_group(core_arr, pair_m, state, outs, index, 1, FF)
-        outs = update_group(core_arr, pair_a, state, outs, index, 0, 2 * width)
-        tails = [
-            jnp.where(core == 0, p[0][:, -TILE:], p[1][:, -TILE:]).astype(F32).T
-            for p in (pair_a, pair_m)
-        ]
-        vec_grads[index] = jnp.concatenate([tails[0][:5], tails[1][:7]], 0)
+        for half in range(2):
+            if half == 0:
+                gx1, keep, send = (
+                    tail if last else plan.mlp_backward(images, g, x1, act, slope, wr, vec, last, before)
+                )
+                spot = (index, 1, FF)
+            else:
+                g, keep, send = plan.attn_backward(gx1, xp, qkv, lse, o, wq, wr, vec, first, before)
+                spot = (index, 0, 2 * width)
+                if last:
+                    turned = turn_images(after(output, g))
+                if first:
+                    parts, at = groups.pop(0)
+                    outs = finish([(after(parts, g), at)], outs)
+            if groups:
+                parts, at = groups[-1]
+                keep, send, turned, outs, parts = lax.optimization_barrier((keep, send, turned, outs, parts))
+                groups[-1] = parts, at
+            joined = join_cores(keep, send)
+            before = [joined]
+            groups.append((exchange_shards(joined), spot))
+    output = turned.swapaxes(0, 1)
+    outs = finish(groups[:-1], outs)
+    parts, spot = groups[-1]
+    parts, outs = lax.optimization_barrier((parts, outs))
+    outs = finish([(parts, spot)], outs)
+    vec_grads = [
+        jnp.concatenate([tails[index, 0][:5], tails[index, 1][:7]], 0) for index in range(layers)
+    ]
     vector_grad = jnp.stack(vec_grads)
     weight_grad, moment_one_new, moment_two_new, update = outs
     vector_one_new, vector_two_new, vector_update = adamw(

time: 295 us -> 274 us (0.929)
  waiting for transfers between devices: 77.2 us -> 61.8 us
  Pallas kernels: 145 us -> 139 us
  starting transfers between devices: 41.3 us -> 45.8 us
  local copies, waits for them, and re-layouts: 14.3 us -> 9.91 us
    all_to_all x4, waiting for transfers between devices: 24.2 us -> 6.63 us  [exchange_shards(): lax.all_to_all(joined.reshape(count, rows // count, cols), 'shard', 0, 0,...]
    ppermute x9 -> x13, waiting for transfers between devices: 15.7 us -> 27.9 us  [the longest x6 13.1 us: neighbour(): return lax.ppermute(piece, 'shard', flip('shard', 1))]
    all_to_all x1 -> x0, waiting for transfers between devices: 11.1 us -> none  [near_exchange(): lax.all_to_all(jnp.broadcast_to(own[None], (count // 2,) + own.shape), 's...]
    pallas_call x8 -> x6, Pallas kernels: 134 us -> 123 us  [call(): return lambda *args: made(*after, *args)]
    ppermute x13 -> x20, waiting for transfers between devices: 9.28 us -> 14.1 us  [swap_cores(): return lax.ppermute(value, 'rep', flip('rep', 1))]
    pallas_call x4 -> x5, Pallas kernels: 11.1 us -> 15.8 us  [the longest x4 11.1 us: update_group(): pl.pallas_call(functools.partial(step_kernel, start), grid=(2,), in_specs...]
    ppermute x9 -> x13, starting transfers between devices: 11.8 us -> 16 us  [the longest x6 6.3 us: neighbour(): return lax.ppermute(piece, 'shard', flip('shard', 1))]
    all_to_all x1, waiting for transfers between devices: 16.9 us -> 13.2 us  [gather_direct(): mine = lax.all_to_all(copies, 'shard', 0, 0, tiled=True)]
  transfers between devices with their start and end apart: 28 -> 38, of which waited for: 14 -> 17; matrix products, arithmetic and copies ran while one was open for 5% -> 3% of each run, Pallas kernels for 33% -> 37%
where the time goes in v1:
time: 274 us; the launch traced here: 273 us
  Pallas kernels  139 us (51%)
  waiting for transfers between devices  61.8 us (23%)
  starting transfers between devices  45.8 us (17%)
  other arithmetic  13.8 us (5%)
  local copies, waits for them, and re-layouts  9.91 us (4%)
    pallas_call x6, Pallas kernels, call(): return lambda *args: made(*after, *args)  123 us
    all_to_all x4, starting transfers between devices, exchange_shards(): lax.all_to_all(joined.reshape(count, rows // count, cols), 'shard', 0, 0,...  19.3 us
    ppermute x20, waiting for transfers between devices, swap_cores(): return lax.ppermute(value, 'rep', flip('rep', 1))  14.1 us
    all_to_all x1, waiting for transfers between devices, gather_direct(): mine = lax.all_to_all(copies, 'shard', 0, 0, tiled=True)  13.2 us
    ppermute x6, waiting for transfers between devices, neighbour(): return lax.ppermute(piece, 'shard', flip('shard', 1))  13.1 us
    ppermute x3, waiting for transfers between devices, finish_groups(): other = lax.ppermute(mine, 'rep', flip('rep', bit))  12.5 us
    pallas_call x4, Pallas kernels, update_group(): pl.pallas_call(functools.partial(step_kernel, start), grid=(2,), in_specs...  11.1 us
    convert_element_type x4, other arithmetic, join_cores(): return (keep.astype(F32) + other.astype(F32)).astype(BF16)  8.45 us
  transfers between devices with their start and end apart: 38, of which 17 were waited for; matrix products, arithmetic and copies ran while one was open for 3% of the time, Pallas kernels for 37%

profile of v1, /device:TPU:0, one launch (start us, length us, event | category | flops | bytes accessed | tf_op | source)
XLA Modules:
  0.0 272.7 jit_solution(12388834484458200009)
XLA Ops:
  4.0 7.3 %all-to-all-start = ((bf16[8,48,640]{2,1,0:T(8,128)(2,1)}), bf16[8,48,640]{2,1,0:T(8,128)(2,1)S(1)}, u32[]{:S(2)}, u32[]{:S(2)}) async-start(bf16[8,48,640]{2,1,0:T(8,128)(2,1)} %broadcast_in_dim.12), calls=%async_computation | async-start | bytes 983040 | tf_op jit(solution)/shard_map/all_to_all | solution.py:745
  11.2 2.9 %collective-permute-start = (bf16[1,48,1792]{2,1,0:T(8,128)(2,1)S(1)}, bf16[1,48,1792]{2,1,0:T(8,128)(2,1)S(1)}, u32[]{:S(2)}, u32[]{:S(2)}) collective-permute-start(bf16[1,48,1792]{2,1,0:T(8,128)(2,1)S(1)} %bitcast.45), channel_id=1, source_target_pairs={{0,4},{1,5},{2,6},{3,7},{4,0},{5,1},{6,2},{7,3},{8,12},{9,13},{10,... | collective-permute-start | bytes 516104 | tf_op jit(solution)/shard_map/ppermute | solution.py:762
  16.9 13.2 %all-to-all-done.refs_4_.refs_10_ = bf16[8,48,640]{2,1,0:T(8,128)(2,1)S(1)} async-done(((bf16[8,48,640]{2,1,0:T(8,128)(2,1)}), bf16[8,48,640]{2,1,0:T(8,128)(2,1)S(1)}, u32[]{:S(2)}, u32[]{:S(2)}) %all-to-all-start) | async-done | bytes 491552 | tf_op jit(solution)/shard_map/all_to_all | solution.py:745
  36.8 11.1 %shard_map.195 = (bf16[1664,1152]{1,0:T(8,128)(2,1)}, bf16[1664,384]{1,0:T(8,128)(2,1)}, f32[8,8,256]{2,1,0:T(8,128)}, f32[16,384]{1,0:T(8,128)}, f32[1664,384]{1,0:T(8,128)}) custom-call(bf16[1,48,1792]{2,1,0:T(8,128)(2,1)} %copy-done.14, s32[1]{0:T(128)} %bitcast.refs_1_.refs_0_.core_ref, s32[8]{0:T(128)} %iota.5.refs_2_, ...), custom_call_target="tpu_custom_call" | custom-call | flops 16999999488 | bytes 20000000 | tf_op jit(solution)/shard_map/pallas_call | solution.py:558
  49.3 7.9 %collective-permute-done.7.refs_11_.refs_14_.refs_17_ = bf16[2,48,1792]{2,1,0:T(8,128)(2,1)S(1)} collective-permute-done((bf16[2,48,1792]{2,1,0:T(8,128)(2,1)S(1)}, bf16[2,48,1792]{2,1,0:T(8,128)(2,1)S(1)}, u32[]{:S(2)}, u32[]{:S(2)}) %collective-permute-start.7) | collective-permute-done | bytes 344096 | tf_op jit(solution)/shard_map/ppermute | solution.py:757
  62.4 14.3 %shard_map.196 = (f32[1664,384]{1,0:T(8,128)}, bf16[1664,1536]{1,0:T(8,128)(2,1)}, f32[1664,1536]{1,0:T(8,128)}, f32[1664,384]{1,0:T(8,128)}) custom-call(bf16[2,48,2432]{2,1,0:T(8,128)(2,1)} %copy-done.22, s32[1]{0:T(128)} %bitcast.refs_1_.refs_0_.core_ref, s32[8]{0:T(128)} %broadcast_xor_fusion.refs_2_.refs_1_.refs_3_, ...), custom_call_target="tpu_custom_call" | custom-call | flops 22000001024 | bytes 30000000 | tf_op jit(solution)/shard_map/pallas_call | solution.py:558
  76.8 5.3 %collective-permute-done.16.refs_10_.refs_15_.refs_27_ = bf16[2,48,2432]{2,1,0:T(8,128)(2,1)S(1)} collective-permute-done((bf16[2,48,2432]{2,1,0:T(8,128)(2,1)S(1)}, bf16[2,48,2432]{2,1,0:T(8,128)(2,1)S(1)}, u32[]{:S(2)}, u32[]{:S(2)}) %collective-permute-start.16) | collective-permute-done | bytes 466976 | tf_op jit(solution)/shard_map/ppermute | solution.py:757
  86.6 35.0 %shard_map.197 = (bf16[1664,1152]{1,0:T(8,128)(2,1)}, bf16[1664,384]{1,0:T(8,128)(2,1)}, f32[8,8,256]{2,1,0:T(8,128)}, f32[16,384]{1,0:T(8,128)}, f32[8,197,384]...) custom-call(s32[1]{0:T(128)} %bitcast.refs_1_.refs_0_.core_ref, ...), custom_call_target="tpu_custom_call" | custom-call | flops 44999999488 | bytes 30000000 | tf_op jit(solution)/shard_map/pallas_call | solution.py:558
  121.7 3.1 %collective-permute-done.23 = bf16[384,1664]{1,0:T(8,128)(2,1)S(1)} collective-permute-done((bf16[384,1664]{1,0:T(8,128)(2,1)}, bf16[384,1664]{1,0:T(8,128)(2,1)S(1)}, u32[]{:S(2)}, u32[]{:S(2)}) %collective-permute-start.23) | collective-permute-done | bytes 1277984 | tf_op jit(solution)/shard_map/ppermute | solution.py:732
  124.8 2.7 add_convert_fusion.1.refs_0_
  127.5 3.8 %all-to-all-start.1 = ((bf16[8,48,1664]{2,1,0:T(8,128)(2,1)}), bf16[8,48,1664]{2,1,0:T(8,128)(2,1)S(1)}, u32[]{:S(2)}, u32[]{:S(2)}) async-start(bf16[8,48,1664]{2,1,0:T(8,128)(2,1)} %bitcast.9), calls=%async_computation.1 | async-start | bytes 2555904 | tf_op jit(solution)/shard_map/all_to_all | solution.py:810
  131.3 21.5 %shard_map.198 = (f32[1664,384]{1,0:T(8,128)}, bf16[384,896]{1,0:T(8,128)(2,1)}, bf16[384,896]{1,0:T(8,128)(2,1)}) custom-call(bf16[384,1664]{1,0:T(8,128)(2,1)} %add_convert_fusion.1.refs_0_, s32[1]{0:T(128)} %bitcast.refs_1_.refs_0_.core_ref, s32[8]{0:T(128)} %broadcast_xor_fusion.refs_2_.refs_1_.refs_3_, s32[8]{0:T(128)} %broadcast_xor_fusion.refs_2_.refs_1_.refs_3_, ...), custom_call_target="tpu_custom_call" | custom-call | flops 30000001024 | bytes 20000000 | tf_op jit(solution)/shard_map/pallas_call | solution.py:558
  152.9 4.7 %shard_map.199 = f32[197,8,384]{2,1,0:T(8,128)} custom-call(f32[8,197,384]{2,1,0:T(8,128)} %get-tuple-element.107.in_ref), custom_call_target="tpu_custom_call" | custom-call | flops 1000000 | bytes 5000000 | tf_op jit(solution)/shard_map/pallas_call | solution.py:791
  157.5 4.7 %all-to-all-done.1 = bf16[8,48,1664]{2,1,0:T(8,128)(2,1)S(1)} async-done(((bf16[8,48,1664]{2,1,0:T(8,128)(2,1)}), bf16[8,48,1664]{2,1,0:T(8,128)(2,1)S(1)}, u32[]{:S(2)}, u32[]{:S(2)}) %all-to-all-start.1) | async-done | bytes 1277984 | tf_op jit(solution)/shard_map/all_to_all | solution.py:810
  165.4 3.6 %all-to-all-start.2 = ((bf16[8,48,896]{2,1,0:T(8,128)(2,1)}), bf16[8,48,896]{2,1,0:T(8,128)(2,1)S(1)}, u32[]{:S(2)}, u32[]{:S(2)}) async-start(bf16[8,48,896]{2,1,0:T(8,128)(2,1)} %bitcast.10), calls=%async_computation.2 | async-start | bytes 1376256 | tf_op jit(solution)/shard_map/all_to_all | solution.py:810
  169.1 19.7 %shard_map.200 = (f32[1664,384]{1,0:T(8,128)}, bf16[384,1664]{1,0:T(8,128)(2,1)}, bf16[384,1664]{1,0:T(8,128)(2,1)}) custom-call(bf16[384,896]{1,0:T(8,128)(2,1)} %add_convert_fusion.3.refs_0_, s32[1]{0:T(128)} %bitcast.refs_1_.refs_0_.core_ref, s32[8]{0:T(128)} %broadcast_xor_fusion.refs_2_.refs_1_.refs_3_, s32[1]{0:T(128)S(6)} %copy.67.refs_2_.refs_3_, ...), custom_call_target="tpu_custom_call" | custom-call | flops 24000000000 | bytes 30000000 | tf_op jit(solution)/shard_map/pallas_call | solution.py:558
  188.9 3.1 %collective-permute-done.25 = bf16[384,1664]{1,0:T(8,128)(2,1)S(1)} collective-permute-done((bf16[384,1664]{1,0:T(8,128)(2,1)}, bf16[384,1664]{1,0:T(8,128)(2,1)S(1)}, u32[]{:S(2)}, u32[]{:S(2)}) %collective-permute-start.25) | collective-permute-done | bytes 1277984 | tf_op jit(solution)/shard_map/ppermute | solution.py:732
  194.7 6.0 %all-to-all-start.3 = ((bf16[8,48,1664]{2,1,0:T(8,128)(2,1)}), bf16[8,48,1664]{2,1,0:T(8,128)(2,1)S(1)}, u32[]{:S(2)}, u32[]{:S(2)}) async-start(bf16[8,48,1664]{2,1,0:T(8,128)(2,1)} %bitcast.36), calls=%async_computation.3 | async-start | bytes 2555904 | tf_op jit(solution)/shard_map/all_to_all | solution.py:810
  201.2 21.9 %shard_map.201 = (f32[8,197,384]{2,1,0:T(8,128)}, bf16[384,896]{1,0:T(8,128)(2,1)}, bf16[384,896]{1,0:T(8,128)(2,1)}) custom-call(bf16[384,1664]{1,0:T(8,128)(2,1)} %add_convert_fusion.refs_0_, s32[1]{0:T(128)} %bitcast.refs_1_.refs_0_.core_ref, s32[8]{0:T(128)} %iota.6.refs_2_, s32[8]{0:T(128)} %broadcast_xor_fusion.refs_2_.refs_1_.refs_3_, ...), custom_call_target="tpu_custom_call" | custom-call | flops 30000001024 | bytes 20000000 | tf_op jit(solution)/shard_map/pallas_call | solution.py:558
  224.8 4.4 %collective-permute-done.26 = bf16[48,1664]{1,0:T(8,128)(2,1)S(1)} collective-permute-done((bf16[48,1664]{1,0:T(8,128)(2,1)S(1)}, bf16[48,1664]{1,0:T(8,128)(2,1)S(1)}, u32[]{:S(2)}, u32[]{:S(2)}) %collective-permute-start.26) | collective-permute-done | bytes 159776 | tf_op jit(solution)/shard_map/ppermute | solution.py:817
  231.4 3.0 %shard_map.202 = (f32[2,48,4608]{2,1,0:T(8,128)}, f32[2,48,4608]{2,1,0:T(8,128)}, f32[2,48,4608]{2,1,0:T(8,128)}, f32[2,48,4608]{2,1,0:T(8,128)}) custom-call(s32[1]{0:T(128)} %bitcast.refs_1_.refs_0_.core_ref, bf16[48,1664]{1,0:T(8,128)(2,1)} %copy-done.6, bf16[48,1664]{1,0:T(8,128)(2,1)} %copy-done.13, f32[2,48,4608]{2,1,0:T(8,128)} %one_ref.7, ...), custom_call_target="tpu_custom_call" | custom-call | flops 1000000 | bytes 4000000 | tf_op jit(solution)/shard_map/pallas_call | solution.py:828
  239.1 5.8 %all-to-all-start.4 = ((bf16[8,48,896]{2,1,0:T(8,128)(2,1)}), bf16[8,48,896]{2,1,0:T(8,128)(2,1)S(1)}, u32[]{:S(2)}, u32[]{:S(2)}) async-start(bf16[8,48,896]{2,1,0:T(8,128)(2,1)} %bitcast.13), calls=%async_computation.4 | async-start | bytes 1376256 | tf_op jit(solution)/shard_map/all_to_all | solution.py:810
  246.5 6.2 %collective-permute-done.29 = bf16[48,2560]{1,0:T(8,128)(2,1)S(1)} collective-permute-done((bf16[48,2560]{1,0:T(8,128)(2,1)S(1)}, bf16[48,2560]{1,0:T(8,128)(2,1)S(1)}, u32[]{:S(2)}, u32[]{:S(2)}) %collective-permute-start.29) | collective-permute-done | bytes 245792 | tf_op jit(solution)/shard_map/ppermute | solution.py:817
  258.2 3.1 %shard_map.204 = (f32[2,48,4608]{2,1,0:T(8,128)}, f32[2,48,4608]{2,1,0:T(8,128)}, f32[2,48,4608]{2,1,0:T(8,128)}, f32[2,48,4608]{2,1,0:T(8,128)}) custom-call(s32[1]{0:T(128)} %bitcast.refs_1_.refs_0_.core_ref, bf16[48,2560]{1,0:T(8,128)(2,1)} %copy-done.1, ...), custom_call_target="tpu_custom_call", output_to_operand_aliasing={{0}: (6, {}), {1}: (7, {}), {2}: (8, {}), {3}: (9, {})} | custom-call | flops 1000000 | bytes 4000000 | tf_op jit(solution)/shard_map/pallas_call | solution.py:828
  (184 shorter events, 56.3 us)
Async XLA Ops:
  4.0 26.2 %all-to-all-start = ((bf16[8,48,640]{2,1,0:T(8,128)(2,1)}), bf16[8,48,640]{2,1,0:T(8,128)(2,1)S(1)}, u32[]{:S(2)}, u32[]{:S(2)}) async-start(bf16[8,48,640]{2,1,0:T(8,128)(2,1)} %broadcast_in_dim.12), calls=%async_computation | async-start | bytes 983040 | tf_op jit(solution)/shard_map/all_to_all | solution.py:745
  11.2 21.2 %collective-permute-start = (bf16[1,48,1792]{2,1,0:T(8,128)(2,1)S(1)}, bf16[1,48,1792]{2,1,0:T(8,128)(2,1)S(1)}, u32[]{:S(2)}, u32[]{:S(2)}) collective-permute-start(bf16[1,48,1792]{2,1,0:T(8,128)(2,1)S(1)} %bitcast.45), channel_id=1, source_target_pairs={{0,4},{1,5},{2,6},{3,7},{4,0},{5,1},{6,2},{7,3},{8,12},{9,13},{10,... | collective-permute-start | bytes 516104 | tf_op jit(solution)/shard_map/ppermute | solution.py:762
  14.2 34.6 %collective-permute-start.5 = (bf16[1,48,1792]{2,1,0:T(8,128)(2,1)S(1)}, bf16[1,48,1792]{2,1,0:T(8,128)(2,1)}, u32[]{:S(2)}, u32[]{:S(2)}) collective-permute-start(bf16[1,48,1792]{2,1,0:T(8,128)(2,1)S(1)} %bitcast.46), channel_id=1, source_target_pairs={{0,1},{1,0},{2,3},{3,2},{4,5},{5,4},{6,7},{7,6},{8,9},{9,8},{10,11... | collective-permute-start | bytes 516104 | tf_op jit(solution)/shard_map/ppermute | solution.py:757
  30.2 5.8 %collective-permute-start.2 = (bf16[8,48,640]{2,1,0:T(8,128)(2,1)S(1)}, bf16[8,48,640]{2,1,0:T(8,128)(2,1)S(1)}, u32[]{:S(2)}, u32[]{:S(2)}) collective-permute-start(bf16[8,48,640]{2,1,0:T(8,128)(2,1)S(1)} %all-to-all-done.refs_4_.refs_10_), channel_id=1, source_target_pairs={{0,8},{8,0},{16,24},{24,16},{1,9},{9,1},{17,25},{25,17},{2,10},{10... | collective-permute-start | bytes 1474568 | tf_op jit(solution)/shard_map/ppermute | solution.py:732
  32.4 15.5 %collective-permute-start.4 = (bf16[2,48,1792]{2,1,0:T(8,128)(2,1)S(1)}, bf16[2,48,1792]{2,1,0:T(8,128)(2,1)S(1)}, u32[]{:S(2)}, u32[]{:S(2)}) collective-permute-start(bf16[2,48,1792]{2,1,0:T(8,128)(2,1)S(1)} %pad_maximum_fusion.1), channel_id=1, source_target_pairs={{0,2},{1,3},{2,0},{3,1},{4,6},{5,7},{6,4},{7,5},{8,10},{9,11},{10,... | collective-permute-start | bytes 1032200 | tf_op jit(solution)/shard_map/ppermute | solution.py:762
  32.5 15.8 %collective-permute-start.1 = (bf16[1,48,2432]{2,1,0:T(8,128)(2,1)S(1)}, bf16[1,48,2432]{2,1,0:T(8,128)(2,1)S(1)}, u32[]{:S(2)}, u32[]{:S(2)}) collective-permute-start(bf16[1,48,2432]{2,1,0:T(8,128)(2,1)S(1)} %bitcast.38), channel_id=1, source_target_pairs={{0,4},{1,5},{2,6},{3,7},{4,0},{5,1},{6,2},{7,3},{8,12},{9,13},{10,... | collective-permute-start | bytes 700424 | tf_op jit(solution)/shard_map/ppermute | solution.py:762
  34.3 13.7 %collective-permute-start.6 = (bf16[1,48,1792]{2,1,0:T(8,128)(2,1)S(1)}, bf16[1,48,1792]{2,1,0:T(8,128)(2,1)S(1)}, u32[]{:S(2)}, u32[]{:S(2)}) collective-permute-start(bf16[1,48,1792]{2,1,0:T(8,128)(2,1)S(1)} %collective-permute-done.refs_0_.refs_7_.refs_10_.refs_13_), channel_id=1, source_target_pairs={{0,1},{1,0},{2,3},{3,2},{4,5},{5,4},{6,7},{7,6},{8,9},{9,8},{10,11... | collective-permute-start | bytes 516104 | tf_op jit(solution)/shard_map/ppermute | solution.py:757
  48.0 9.2 %collective-permute-start.7 = (bf16[2,48,1792]{2,1,0:T(8,128)(2,1)S(1)}, bf16[2,48,1792]{2,1,0:T(8,128)(2,1)S(1)}, u32[]{:S(2)}, u32[]{:S(2)}) collective-permute-start(bf16[2,48,1792]{2,1,0:T(8,128)(2,1)S(1)} %collective-permute-done.4.refs_8_.refs_11_.refs_14_), channel_id=1, source_target_pairs={{0,1},{1,0},{2,3},{3,2},{4,5},{5,4},{6,7},{7,6},{8,9},{9,8},{10,11... | collective-permute-start | bytes 1032200 | tf_op jit(solution)/shard_map/ppermute | solution.py:757
  48.4 13.1 %collective-permute-start.3 = (bf16[2,48,2432]{2,1,0:T(8,128)(2,1)S(1)}, bf16[2,48,2432]{2,1,0:T(8,128)(2,1)S(1)}, u32[]{:S(2)}, u32[]{:S(2)}) collective-permute-start(bf16[2,48,2432]{2,1,0:T(8,128)(2,1)S(1)} %pad_maximum_fusion), channel_id=1, source_target_pairs={{0,2},{1,3},{2,0},{3,1},{4,6},{5,7},{6,4},{7,5},{8,10},{9,11},{10,... | collective-permute-start | bytes 1400840 | tf_op jit(solution)/shard_map/ppermute | solution.py:762
  48.7 8.5 %collective-permute-start.8 = (bf16[1,48,1792]{2,1,0:T(8,128)(2,1)S(1)}, bf16[1,48,1792]{2,1,0:T(8,128)(2,1)S(1)}, u32[]{:S(2)}, u32[]{:S(2)}) collective-permute-start(bf16[1,48,1792]{2,1,0:T(8,128)(2,1)S(1)} %bitcast.48), channel_id=1, source_target_pairs={{0,8},{8,0},{16,24},{24,16},{1,9},{9,1},{17,25},{25,17},{2,10},{10... | collective-permute-start | bytes 516104 | tf_op jit(solution)/shard_map/ppermute | solution.py:732
  48.7 9.0 %collective-permute-start.11 = (bf16[1,48,1792]{2,1,0:T(8,128)(2,1)}, bf16[1,48,1792]{2,1,0:T(8,128)(2,1)}, u32[]{:S(2)}, u32[]{:S(2)}) collective-permute-start(bf16[1,48,1792]{2,1,0:T(8,128)(2,1)} %collective-permute-done.5.refs_9_.refs_12_.refs_15_), channel_id=1, source_target_pairs={{0,8},{8,0},{16,24},{24,16},{1,9},{9,1},{17,25},{25,17},{2,10},{10... | collective-permute-start | bytes 516104 | tf_op jit(solution)/shard_map/ppermute | solution.py:732
  49.2 10.4 %collective-permute-start.10 = (bf16[2,48,1792]{2,1,0:T(8,128)(2,1)S(1)}, bf16[2,48,1792]{2,1,0:T(8,128)(2,1)S(1)}, u32[]{:S(2)}, u32[]{:S(2)}) collective-permute-start(bf16[2,48,1792]{2,1,0:T(8,128)(2,1)S(1)} %collective-permute-done.4.refs_8_.refs_11_.refs_14_), channel_id=1, source_target_pairs={{0,8},{8,0},{16,24},{24,16},{1,9},{9,1},{17,25},{25,17},{2,10},{10... | collective-permute-start | bytes 1032200 | tf_op jit(solution)/shard_map/ppermute | solution.py:732
  57.2 5.0 %collective-permute-start.13 = (bf16[2,48,1792]{2,1,0:T(8,128)(2,1)S(1)}, bf16[2,48,1792]{2,1,0:T(8,128)(2,1)}, u32[]{:S(2)}, u32[]{:S(2)}) collective-permute-start(bf16[2,48,1792]{2,1,0:T(8,128)(2,1)S(1)} %collective-permute-done.7.refs_11_.refs_14_.refs_17_), channel_id=1, source_target_pairs={{0,8},{8,0},{16,24},{24,16},{1,9},{9,1},{17,25},{25,17},{2,10},{10... | collective-permute-start | bytes 1032200 | tf_op jit(solution)/shard_map/ppermute | solution.py:732
  59.3 22.8 %collective-permute-start.14 = (bf16[1,48,2432]{2,1,0:T(8,128)(2,1)S(1)}, bf16[1,48,2432]{2,1,0:T(8,128)(2,1)S(1)}, u32[]{:S(2)}, u32[]{:S(2)}) collective-permute-start(bf16[1,48,2432]{2,1,0:T(8,128)(2,1)S(1)} %bitcast.40), channel_id=1, source_target_pairs={{0,1},{1,0},{2,3},{3,2},{4,5},{5,4},{6,7},{7,6},{8,9},{9,8},{10,11... | collective-permute-start | bytes 700424 | tf_op jit(solution)/shard_map/ppermute | solution.py:757
  59.6 23.0 %collective-permute-start.17 = (bf16[1,48,2432]{2,1,0:T(8,128)(2,1)S(1)}, bf16[1,48,2432]{2,1,0:T(8,128)(2,1)}, u32[]{:S(2)}, u32[]{:S(2)}) collective-permute-start(bf16[1,48,2432]{2,1,0:T(8,128)(2,1)S(1)} %bitcast.41), channel_id=1, source_target_pairs={{0,8},{8,0},{16,24},{24,16},{1,9},{9,1},{17,25},{25,17},{2,10},{10... | collective-permute-start | bytes 700424 | tf_op jit(solution)/shard_map/ppermute | solution.py:732
  59.7 23.0 %collective-permute-start.15 = (bf16[1,48,2432]{2,1,0:T(8,128)(2,1)S(1)}, bf16[1,48,2432]{2,1,0:T(8,128)(2,1)}, u32[]{:S(2)}, u32[]{:S(2)}) collective-permute-start(bf16[1,48,2432]{2,1,0:T(8,128)(2,1)S(1)} %collective-permute-done.1.refs_6_.refs_11_.refs_23_), channel_id=1, source_target_pairs={{0,1},{1,0},{2,3},{3,2},{4,5},{5,4},{6,7},{7,6},{8,9},{9,8},{10,11... | collective-permute-start | bytes 700424 | tf_op jit(solution)/shard_map/ppermute | solution.py:757
  61.5 20.5 %collective-permute-start.16 = (bf16[2,48,2432]{2,1,0:T(8,128)(2,1)S(1)}, bf16[2,48,2432]{2,1,0:T(8,128)(2,1)S(1)}, u32[]{:S(2)}, u32[]{:S(2)}) collective-permute-start(bf16[2,48,2432]{2,1,0:T(8,128)(2,1)S(1)} %collective-permute-done.3.refs_0_.refs_7_.refs_12_.refs_24_), channel_id=1, source_target_pairs={{0,1},{1,0},{2,3},{3,2},{4,5},{5,4},{6,7},{7,6},{8,9},{9,8},{10,11... | collective-permute-start | bytes 1400840 | tf_op jit(solution)/shard_map/ppermute | solution.py:757
  62.2 22.9 %collective-permute-start.19 = (bf16[2,48,2432]{2,1,0:T(8,128)(2,1)S(1)}, bf16[2,48,2432]{2,1,0:T(8,128)(2,1)S(1)}, u32[]{:S(2)}, u32[]{:S(2)}) collective-permute-start(bf16[2,48,2432]{2,1,0:T(8,128)(2,1)S(1)} %collective-permute-done.3.refs_0_.refs_7_.refs_12_.refs_24_), channel_id=1, source_target_pairs={{0,8},{8,0},{16,24},{24,16},{1,9},{9,1},{17,25},{25,17},{2,10},{10... | collective-permute-start | bytes 1400840 | tf_op jit(solution)/shard_map/ppermute | solution.py:732
  127.5 34.8 %all-to-all-start.1 = ((bf16[8,48,1664]{2,1,0:T(8,128)(2,1)}), bf16[8,48,1664]{2,1,0:T(8,128)(2,1)S(1)}, u32[]{:S(2)}, u32[]{:S(2)}) async-start(bf16[8,48,1664]{2,1,0:T(8,128)(2,1)} %bitcast.9), calls=%async_computation.1 | async-start | bytes 2555904 | tf_op jit(solution)/shard_map/all_to_all | solution.py:810
  165.4 23.3 %all-to-all-start.2 = ((bf16[8,48,896]{2,1,0:T(8,128)(2,1)}), bf16[8,48,896]{2,1,0:T(8,128)(2,1)S(1)}, u32[]{:S(2)}, u32[]{:S(2)}) async-start(bf16[8,48,896]{2,1,0:T(8,128)(2,1)} %bitcast.10), calls=%async_computation.2 | async-start | bytes 1376256 | tf_op jit(solution)/shard_map/all_to_all | solution.py:810
  194.7 39.8 %all-to-all-start.3 = ((bf16[8,48,1664]{2,1,0:T(8,128)(2,1)}), bf16[8,48,1664]{2,1,0:T(8,128)(2,1)S(1)}, u32[]{:S(2)}, u32[]{:S(2)}) async-start(bf16[8,48,1664]{2,1,0:T(8,128)(2,1)} %bitcast.36), calls=%async_computation.3 | async-start | bytes 2555904 | tf_op jit(solution)/shard_map/all_to_all | solution.py:810
  223.3 5.9 %collective-permute-start.26 = (bf16[48,1664]{1,0:T(8,128)(2,1)S(1)}, bf16[48,1664]{1,0:T(8,128)(2,1)S(1)}, u32[]{:S(2)}, u32[]{:S(2)}) collective-permute-start(bf16[48,1664]{1,0:T(8,128)(2,1)S(1)} %reduce_sum.48), channel_id=1, source_target_pairs={{0,16},{8,24},{16,0},{24,8},{1,17},{9,25},{17,1},{25,9},{2,18},{10... | collective-permute-start | bytes 479240 | tf_op jit(solution)/shard_map/ppermute | solution.py:817
  239.1 24.1 %all-to-all-start.4 = ((bf16[8,48,896]{2,1,0:T(8,128)(2,1)}), bf16[8,48,896]{2,1,0:T(8,128)(2,1)S(1)}, u32[]{:S(2)}, u32[]{:S(2)}) async-start(bf16[8,48,896]{2,1,0:T(8,128)(2,1)} %bitcast.13), calls=%async_computation.4 | async-start | bytes 1376256 | tf_op jit(solution)/shard_map/all_to_all | solution.py:810
  245.0 7.8 %collective-permute-start.29 = (bf16[48,2560]{1,0:T(8,128)(2,1)S(1)}, bf16[48,2560]{1,0:T(8,128)(2,1)S(1)}, u32[]{:S(2)}, u32[]{:S(2)}) collective-permute-start(bf16[48,2560]{1,0:T(8,128)(2,1)S(1)} %pad_maximum_fusion.2), channel_id=1, source_target_pairs={{0,16},{8,24},{16,0},{24,8},{1,17},{9,25},{17,1},{25,9},{2,18},{10... | collective-permute-start | bytes 737288 | tf_op jit(solution)/shard_map/ppermute | solution.py:817
  (52 other events, 361.7 us)

commit v2 on v1

--- a/solution.py
+++ b/solution.py
@@ -127,11 +127,12 @@
     width = o_ref.shape[1]
     heads = width // HEAD
 
+    copies = weight_copies(core_ref, place_ref, sources, start, w_ref, sems)
+
     @pl.when(pl.program_id(0) == 0)
     def _():
-        load_weights(core_ref, place_ref, sources, start, w_ref, sems)
-        turned = w_ref[:, 3 * width : 3 * width + TILE].astype(F32).T
-        vec_ref[...] = turned[: vec_ref.shape[0]]
+        for copy in copies:
+            copy.start()
 
     if first:
         for i in range(PAIR):
@@ -139,6 +140,14 @@
             xp_ref[i * rows + seq : (i + 1) * rows, :] = jnp.zeros((rows - seq, width), F32)
 
     normed, _ = norm(xp_ref[...])
+
+    @pl.when(pl.program_id(0) == 0)
+    def _():
+        for copy in copies:
+            copy.wait()
+        turned = w_ref[:, 3 * width : 3 * width + TILE].astype(F32).T
+        vec_ref[...] = turned[: vec_ref.shape[0]]
+
     hidden = (normed * vec_ref[0:1, :] + vec_ref[1:2, :]).astype(BF16)
     qkv = dot(hidden, w_ref[:, : 3 * width])
     qkv_ref[:, :width] = ((qkv[:, :width] + vec_ref[2:3, :]) * 0.125).astype(BF16)
@@ -390,18 +399,23 @@
     heads = width // HEAD
     step = pl.program_id(0)
 
+    copies = weight_copies(core_ref, qplace_ref, qsources, starts[0], w_ref, sems)
+
     @pl.when(step == 0)
     def _():
-        load_weights(core_ref, qplace_ref, qsources, starts[0], w_ref, sems)
+        for copy in copies:
+            copy.start()
         load_first(core_ref, place_ref, sources, starts[1], wout_ref, osems)
-        gw_ref[...] = jnp.zeros_like(gw_ref)
-        gout_ref[...] = jnp.zeros_like(gout_ref)
-        acc_ref[...] = jnp.zeros_like(acc_ref)
+        for ref in (gw_ref, gout_ref, acc_ref):
+            ref[...] = jnp.zeros_like(ref)
 
     low = g_ref[...].astype(BF16)
-    gout_ref[...] += dot(o_ref[...].T, low)
-    acc_ref[4:5, :] += column_sum(g_ref[...])
     go_ref[...] = dot_nt(low, wout_ref[...]).astype(BF16)
+
+    @pl.when(step == 0)
+    def _():
+        for copy in copies:
+            copy.wait()
 
     edge = seq // 16 * 16
     alive = lax.broadcasted_iota(jnp.int32, (rows - edge, rows), 0) < seq - edge
@@ -431,9 +445,30 @@
         if h == heads - 1:
             gqkv_ref[span, :width] = jnp.concatenate(gqs[i], 0).T
 
+    def post(i):
+        span = slice(i * rows, (i + 1) * rows)
+        gqkv = gqkv_ref[span, :]
+        gw_ref[...] += dot(turned_h[i], gqkv)
+        gh = dot_nt(gqkv, w_ref[:, : 3 * width]).astype(BF16).astype(F32)
+        acc_ref[2:3, :] += column_sum(gqkv[:, :width].astype(F32))
+        acc_ref[3:4, :] += column_sum(gqkv[:, 2 * width :].astype(F32))
+        acc_ref[0:1, :] += column_sum(gh * normed[i])
+        acc_ref[1:2, :] += column_sum(gh)
+        gx = g_ref[span, :] + norm_back(gh, normed[i], scale[i], vec_ref[0:1, :])
+        if first:
+            gx_ref[i] = gx[:seq]
+        else:
+            gx_ref[span, :] = gx
+
     gks, gvs, gqs = ([[] for _ in range(PAIR)] for _ in range(3))
     turned_k = [qkv_ref[i * rows : (i + 1) * rows, width : 2 * width].T for i in range(PAIR)]
     ahead = [start(*item) for item in work[:2]]
+    normed, scale, turned_h = [], [], []
+    for i in range(PAIR):
+        part, size = norm(x_ref[i * rows : (i + 1) * rows, :])
+        normed.append(part)
+        scale.append(size)
+        turned_h.append((part * vec_ref[0:1, :] + vec_ref[1:2, :]).astype(BF16).T)
     behind = []
     for n, (i, h) in enumerate(work):
         if n + 2 < len(work):
@@ -452,25 +487,10 @@
             finish(*behind.pop(0))
     for item in behind:
         finish(*item)
-
-    normed, scale = norm(x_ref[...])
-    hidden = (normed * vec_ref[0:1, :] + vec_ref[1:2, :]).astype(BF16)
-    turned_h = hidden.T
-    gqkv = gqkv_ref[...]
-    gw_ref[...] += dot(turned_h, gqkv)
-    total = dot_nt(gqkv, w_ref[:, : 3 * width])
-    acc_ref[2:3, :] += column_sum(gqkv[:, :width].astype(F32))
-    acc_ref[3:4, :] += column_sum(gqkv[:, 2 * width :].astype(F32))
-    gh = total.astype(BF16).astype(F32)
-    acc_ref[0:1, :] += column_sum(gh * normed)
-    acc_ref[1:2, :] += column_sum(gh)
-    gx = g_ref[...] + norm_back(gh, normed, scale, vec_ref[0:1, :])
-    if first:
-        for i in range(PAIR):
-            gx_ref[i] = gx[i * rows : i * rows + seq]
-    else:
-        gx_ref[...] = gx
-
+    gout_ref[...] += dot(o_ref[...].T, low)
+    acc_ref[4:5, :] += column_sum(g_ref[...])
+    for i in range(PAIR):
+        post(i)
     @pl.when(step == pl.num_programs(0) - 1)
     def _():
         def one(ref):
@@ -737,15 +757,6 @@
     return lax.dynamic_slice_in_dim(packed, core * half, half, 1)
 
 
-def spread(own):
-    return jnp.broadcast_to(own[None], (lax.axis_size("shard"),) + own.shape)
-
-
-def gather_direct(copies):
-    mine = lax.all_to_all(copies, "shard", 0, 0, tiled=True)
-    return [mine, swap_cores(mine)], jnp.arange(copies.shape[0], dtype=jnp.int32)
-
-
 class Gathering:
     def __init__(self, own):
         self.near = [own[None]]
@@ -860,14 +871,16 @@
         bits.append(bit)
         bit //= 2
     attn_own, rest_own = packs[0]
-    copies, rest_own = lax.optimization_barrier((spread(attn_own), rest_own))
-    arrays, place = gather_direct(copies)
-    rest = Gathering(rest_own)
+    query = Gathering(attn_own)
+    for bit in bits:
+        query.step(bit)
+        query.pass_on()
+    rest = Gathering(after(rest_own, query.near[1]))
     for bit in bits:
         rest.step(bit)
         if bit != bits[-1]:
             rest.pass_on()
-    gathered = [[Weights(arrays, place, 0, attn_own.shape[1]), None]]
+    gathered = [[Weights(query.held(), query.place(), 0, attn_own.shape[1]), None]]
     stored = []
     x = tokens
     for index in range(layers):
@@ -885,7 +898,7 @@
         )
         xp = xp[0] if first else x
         if first:
-            rest.pass_on(o, rest.far[-1])
+            rest.pass_on(o, rest.far[-1], ahead.far[0])
             gathered[0][1] = Weights(rest.held(o), rest.place(), 0, rest_own.shape[1])
         if not last:
             ahead.pass_on(o)

time: 274 us -> 260 us (0.949)
  waiting for transfers between devices: 61.8 us -> 42.8 us
  starting transfers between devices: 45.8 us -> 54.1 us
    all_to_all x1 -> x0, waiting for transfers between devices: 13.2 us -> none  [gather_direct(): mine = lax.all_to_all(copies, 'shard', 0, 0, tiled=True)]
    all_to_all x1 -> x0, starting transfers between devices: 7.28 us -> none  [gather_direct(): mine = lax.all_to_all(copies, 'shard', 0, 0, tiled=True)]
    ppermute x6 -> x9, starting transfers between devices: 6.3 us -> 13.3 us  [neighbour(): return lax.ppermute(piece, 'shard', flip('shard', 1))]
    ppermute x4 -> x6, starting transfers between devices: 5.08 us -> 12 us  [step(): self.near.append(lax.ppermute(have, 'shard', flip('shard', bit)))]
    ppermute x6 -> x9, waiting for transfers between devices: 13.1 us -> 7.19 us  [neighbour(): return lax.ppermute(piece, 'shard', flip('shard', 1))]
    ppermute x20 -> x25, waiting for transfers between devices: 14.1 us -> 14.5 us  [swap_cores(): return lax.ppermute(value, 'rep', flip('rep', 1))]
    unnamed x80 -> x108, local copies, waits for them, and re-layouts: 7.5 us -> 7.39 us
  transfers between devices with their start and end apart: 38 -> 47, of which waited for: 17 -> 18; matrix products, arithmetic and copies ran while one was open for 3% -> 3% of each run, Pallas kernels for 37% -> 39%
where the time goes in v2:
time: 260 us; the launch traced here: 259 us
  Pallas kernels  138 us (53%)
  starting transfers between devices  54.1 us (21%)
  waiting for transfers between devices  42.8 us (16%)
  other arithmetic  13.9 us (5%)
  local copies, waits for them, and re-layouts  7.93 us (3%)
    pallas_call x6, Pallas kernels, call(): return lambda *args: made(*after, *args)  123 us
    all_to_all x4, starting transfers between devices, exchange_shards(): lax.all_to_all(joined.reshape(count, rows // count, cols), 'shard', 0, 0,...  19.2 us
    ppermute x25, waiting for transfers between devices, swap_cores(): return lax.ppermute(value, 'rep', flip('rep', 1))  14.5 us
    ppermute x9, starting transfers between devices, neighbour(): return lax.ppermute(piece, 'shard', flip('shard', 1))  13.3 us
    ppermute x3, waiting for transfers between devices, finish_groups(): other = lax.ppermute(mine, 'rep', flip('rep', bit))  12.4 us
    ppermute x6, starting transfers between devices, step(): self.near.append(lax.ppermute(have, 'shard', flip('shard', bit)))  12 us
    pallas_call x4, Pallas kernels, update_group(): pl.pallas_call(functools.partial(step_kernel, start), grid=(2,), in_specs...  11.1 us
    convert_element_type x4, other arithmetic, join_cores(): return (keep.astype(F32) + other.astype(F32)).astype(BF16)  8.47 us
  transfers between devices with their start and end apart: 47, of which 18 were waited for; matrix products, arithmetic and copies ran while one was open for 3% of the time, Pallas kernels for 39%

profile of v2, /device:TPU:0, one launch (start us, length us, event | category | flops | bytes accessed | tf_op | source)
XLA Modules:
  0.0 259.2 jit_solution(8812245541789464733)
XLA Ops:
  2.5 4.1 %collective-permute-start = (bf16[1,48,640]{2,1,0:T(8,128)(2,1)S(1)}, bf16[1,48,640]{2,1,0:T(8,128)(2,1)S(1)}, u32[]{:S(2)}, u32[]{:S(2)}) collective-permute-start(bf16[1,48,640]{2,1,0:T(8,128)(2,1)S(1)} %fusion.3.refs_4_.refs_10_), channel_id=1, source_target_pairs={{0,4},{1,5},{2,6},{3,7},{4,0},{5,1},{6,2},{7,3},{8,12},{9,13},{10,... | collective-permute-start | bytes 184328 | tf_op jit(solution)/shard_map/ppermute | solution.py:773
  10.9 3.4 %collective-permute-start.1 = (bf16[1,48,1792]{2,1,0:T(8,128)(2,1)S(1)}, bf16[1,48,1792]{2,1,0:T(8,128)(2,1)S(1)}, u32[]{:S(2)}, u32[]{:S(2)}) collective-permute-start(bf16[1,48,1792]{2,1,0:T(8,128)(2,1)S(1)} %bitcast.47), channel_id=1, source_target_pairs={{0,4},{1,5},{2,6},{3,7},{4,0},{5,1},{6,2},{7,3},{8,12},{9,13},{10,... | collective-permute-start | bytes 516104 | tf_op jit(solution)/shard_map/ppermute | solution.py:773
  15.8 3.1 %collective-permute-start.6 = (bf16[2,48,640]{2,1,0:T(8,128)(2,1)S(1)}, bf16[2,48,640]{2,1,0:T(8,128)(2,1)S(1)}, u32[]{:S(2)}, u32[]{:S(2)}) collective-permute-start(bf16[2,48,640]{2,1,0:T(8,128)(2,1)S(1)} %collective-permute-done.3.refs_6_.refs_12_), channel_id=1, source_target_pairs={{0,1},{1,0},{2,3},{3,2},{4,5},{5,4},{6,7},{7,6},{8,9},{9,8},{10,11... | collective-permute-start | bytes 368648 | tf_op jit(solution)/shard_map/ppermute | solution.py:768
  29.2 10.9 %shard_map.204 = (bf16[1664,1152]{1,0:T(8,128)(2,1)}, bf16[1664,384]{1,0:T(8,128)(2,1)}, f32[8,8,256]{2,1,0:T(8,128)}, f32[16,384]{1,0:T(8,128)}, f32[1664,384]{1,0:T(8,128)}) custom-call(bf16[1,48,1792]{2,1,0:T(8,128)(2,1)} %copy-done.14, s32[1]{0:T(128)} %bitcast.refs_1_.refs_0_.core_ref, s32[8]{0:T(128)} %broadcast_xor_fusion.refs_2_.refs_1_.refs_3_, ...), custom_call_target="tpu_custom_call" | custom-call | flops 16999999488 | bytes 20000000 | tf_op jit(solution)/shard_map/pallas_call | solution.py:578
  42.6 6.5 %collective-permute-done.18.refs_11_.refs_14_.refs_27_ = bf16[2,48,1792]{2,1,0:T(8,128)(2,1)S(1)} collective-permute-done((bf16[2,48,1792]{2,1,0:T(8,128)(2,1)S(1)}, bf16[2,48,1792]{2,1,0:T(8,128)(2,1)S(1)}, u32[]{:S(2)}, u32[]{:S(2)}) %collective-permute-start.18) | collective-permute-done | bytes 344096 | tf_op jit(solution)/shard_map/ppermute | solution.py:768
  54.7 14.3 %shard_map.205 = (f32[1664,384]{1,0:T(8,128)}, bf16[1664,1536]{1,0:T(8,128)(2,1)}, f32[1664,1536]{1,0:T(8,128)}, f32[1664,384]{1,0:T(8,128)}) custom-call(bf16[2,48,2432]{2,1,0:T(8,128)(2,1)} %copy-done.22, s32[1]{0:T(128)} %bitcast.refs_1_.refs_0_.core_ref, s32[8]{0:T(128)} %broadcast_xor_fusion.refs_2_.refs_1_.refs_3_, ...), custom_call_target="tpu_custom_call" | custom-call | flops 22000001024 | bytes 30000000 | tf_op jit(solution)/shard_map/pallas_call | solution.py:578
  74.1 35.0 %shard_map.206 = (bf16[1664,1152]{1,0:T(8,128)(2,1)}, bf16[1664,384]{1,0:T(8,128)(2,1)}, f32[8,8,256]{2,1,0:T(8,128)}, f32[16,384]{1,0:T(8,128)}, f32[8,197,384]...) custom-call(s32[1]{0:T(128)} %bitcast.refs_1_.refs_0_.core_ref, ...), custom_call_target="tpu_custom_call" | custom-call | flops 44999999488 | bytes 30000000 | tf_op jit(solution)/shard_map/pallas_call | solution.py:578
  109.4 3.0 %collective-permute-done.33 = bf16[384,1664]{1,0:T(8,128)(2,1)S(1)} collective-permute-done((bf16[384,1664]{1,0:T(8,128)(2,1)}, bf16[384,1664]{1,0:T(8,128)(2,1)S(1)}, u32[]{:S(2)}, u32[]{:S(2)}) %collective-permute-start.33) | collective-permute-done | bytes 1277984 | tf_op jit(solution)/shard_map/ppermute | solution.py:752
  112.4 2.7 %add_convert_fusion.1.refs_0_ = bf16[384,1664]{1,0:T(8,128)(2,1)} fusion(bf16[384,1664]{1,0:T(8,128)(2,1)S(1)} %collective-permute-done.33, bf16[384,1664]{1,0:T(8,128)(2,1)} %get-tuple-element.94), kind=kLoop, calls=%fused_computation.1 | loop fusion | flops 2555904 | bytes 3833856 | tf_op jit(solution)/shard_map/convert_element_type | solution.py:815
  115.1 3.8 %all-to-all-start = ((bf16[8,48,1664]{2,1,0:T(8,128)(2,1)}), bf16[8,48,1664]{2,1,0:T(8,128)(2,1)S(1)}, u32[]{:S(2)}, u32[]{:S(2)}) async-start(bf16[8,48,1664]{2,1,0:T(8,128)(2,1)} %bitcast.10), calls=%async_computation | async-start | bytes 2555904 | tf_op jit(solution)/shard_map/all_to_all | solution.py:821
  118.9 21.2 %shard_map.207 = (f32[1664,384]{1,0:T(8,128)}, bf16[384,896]{1,0:T(8,128)(2,1)}, bf16[384,896]{1,0:T(8,128)(2,1)}) custom-call(bf16[384,1664]{1,0:T(8,128)(2,1)} %add_convert_fusion.1.refs_0_, s32[1]{0:T(128)} %bitcast.refs_1_.refs_0_.core_ref, s32[8]{0:T(128)} %broadcast_xor_fusion.refs_2_.refs_1_.refs_3_, s32[8]{0:T(128)} %broadcast_xor_fusion.refs_2_.refs_1_.refs_3_, ...), custom_call_target="tpu_custom_call" | custom-call | flops 30000001024 | bytes 20000000 | tf_op jit(solution)/shard_map/pallas_call | solution.py:578
  140.1 4.7 %shard_map.208 = f32[197,8,384]{2,1,0:T(8,128)} custom-call(f32[8,197,384]{2,1,0:T(8,128)} %get-tuple-element.105.in_ref), custom_call_target="tpu_custom_call" | custom-call | flops 1000000 | bytes 5000000 | tf_op jit(solution)/shard_map/pallas_call | solution.py:802
  144.8 5.0 %all-to-all-done = bf16[8,48,1664]{2,1,0:T(8,128)(2,1)S(1)} async-done(((bf16[8,48,1664]{2,1,0:T(8,128)(2,1)}), bf16[8,48,1664]{2,1,0:T(8,128)(2,1)S(1)}, u32[]{:S(2)}, u32[]{:S(2)}) %all-to-all-start) | async-done | bytes 1277984 | tf_op jit(solution)/shard_map/all_to_all | solution.py:821
  153.0 3.6 %all-to-all-start.1 = ((bf16[8,48,896]{2,1,0:T(8,128)(2,1)}), bf16[8,48,896]{2,1,0:T(8,128)(2,1)S(1)}, u32[]{:S(2)}, u32[]{:S(2)}) async-start(bf16[8,48,896]{2,1,0:T(8,128)(2,1)} %bitcast.11), calls=%async_computation.1 | async-start | bytes 1376256 | tf_op jit(solution)/shard_map/all_to_all | solution.py:821
  156.7 19.7 %shard_map.209 = (f32[1664,384]{1,0:T(8,128)}, bf16[384,1664]{1,0:T(8,128)(2,1)}, bf16[384,1664]{1,0:T(8,128)(2,1)}) custom-call(bf16[384,896]{1,0:T(8,128)(2,1)} %add_convert_fusion.3.refs_0_, s32[1]{0:T(128)} %bitcast.refs_1_.refs_0_.core_ref, s32[8]{0:T(128)} %broadcast_xor_fusion.refs_2_.refs_1_.refs_3_, s32[1]{0:T(128)S(6)} %copy.68.refs_2_.refs_3_, ...), custom_call_target="tpu_custom_call" | custom-call | flops 24000000000 | bytes 30000000 | tf_op jit(solution)/shard_map/pallas_call | solution.py:578
  176.5 3.1 %collective-permute-done.35 = bf16[384,1664]{1,0:T(8,128)(2,1)S(1)} collective-permute-done((bf16[384,1664]{1,0:T(8,128)(2,1)}, bf16[384,1664]{1,0:T(8,128)(2,1)S(1)}, u32[]{:S(2)}, u32[]{:S(2)}) %collective-permute-start.35) | collective-permute-done | bytes 1277984 | tf_op jit(solution)/shard_map/ppermute | solution.py:752
  179.7 2.6 %add_convert_fusion.refs_0_ = bf16[384,1664]{1,0:T(8,128)(2,1)} fusion(bf16[384,1664]{1,0:T(8,128)(2,1)S(1)} %collective-permute-done.35, bf16[384,1664]{1,0:T(8,128)(2,1)} %get-tuple-element.113), kind=kLoop, calls=%fused_computation | loop fusion | flops 2555904 | bytes 3833856 | tf_op jit(solution)/shard_map/convert_element_type | solution.py:815
  182.3 6.0 %all-to-all-start.2 = ((bf16[8,48,1664]{2,1,0:T(8,128)(2,1)}), bf16[8,48,1664]{2,1,0:T(8,128)(2,1)S(1)}, u32[]{:S(2)}, u32[]{:S(2)}) async-start(bf16[8,48,1664]{2,1,0:T(8,128)(2,1)} %bitcast.38), calls=%async_computation.2 | async-start | bytes 2555904 | tf_op jit(solution)/shard_map/all_to_all | solution.py:821
  188.3 21.3 %shard_map.210 = (f32[8,197,384]{2,1,0:T(8,128)}, bf16[384,896]{1,0:T(8,128)(2,1)}, bf16[384,896]{1,0:T(8,128)(2,1)}) custom-call(bf16[384,1664]{1,0:T(8,128)(2,1)} %add_convert_fusion.refs_0_, s32[1]{0:T(128)} %bitcast.refs_1_.refs_0_.core_ref, s32[8]{0:T(128)} %broadcast_xor_fusion.refs_2_.refs_1_.refs_3_, s32[8]{0:T(128)} %broadcast_xor_fusion.refs_2_.refs_1_.refs_3_, ...), custom_call_target="tpu_custom_call" | custom-call | flops 30000001024 | bytes 20000000 | tf_op jit(solution)/shard_map/pallas_call | solution.py:578
  211.3 4.4 %collective-permute-done.36 = bf16[48,1664]{1,0:T(8,128)(2,1)S(1)} collective-permute-done((bf16[48,1664]{1,0:T(8,128)(2,1)S(1)}, bf16[48,1664]{1,0:T(8,128)(2,1)S(1)}, u32[]{:S(2)}, u32[]{:S(2)}) %collective-permute-start.36) | collective-permute-done | bytes 159776 | tf_op jit(solution)/shard_map/ppermute | solution.py:828
  217.9 3.0 %shard_map.211 = (f32[2,48,4608]{2,1,0:T(8,128)}, f32[2,48,4608]{2,1,0:T(8,128)}, f32[2,48,4608]{2,1,0:T(8,128)}, f32[2,48,4608]{2,1,0:T(8,128)}) custom-call(s32[1]{0:T(128)} %bitcast.refs_1_.refs_0_.core_ref, bf16[48,1664]{1,0:T(8,128)(2,1)} %copy-done.6, bf16[48,1664]{1,0:T(8,128)(2,1)} %copy-done.13, f32[2,48,4608]{2,1,0:T(8,128)} %one_ref.7, ...), custom_call_target="tpu_custom_call" | custom-call | flops 1000000 | bytes 4000000 | tf_op jit(solution)/shard_map/pallas_call | solution.py:839
  225.6 5.8 %all-to-all-start.3 = ((bf16[8,48,896]{2,1,0:T(8,128)(2,1)}), bf16[8,48,896]{2,1,0:T(8,128)(2,1)S(1)}, u32[]{:S(2)}, u32[]{:S(2)}) async-start(bf16[8,48,896]{2,1,0:T(8,128)(2,1)} %bitcast.14), calls=%async_computation.3 | async-start | bytes 1376256 | tf_op jit(solution)/shard_map/all_to_all | solution.py:821
  233.1 6.2 %collective-permute-done.39 = bf16[48,2560]{1,0:T(8,128)(2,1)S(1)} collective-permute-done((bf16[48,2560]{1,0:T(8,128)(2,1)S(1)}, bf16[48,2560]{1,0:T(8,128)(2,1)S(1)}, u32[]{:S(2)}, u32[]{:S(2)}) %collective-permute-start.39) | collective-permute-done | bytes 245792 | tf_op jit(solution)/shard_map/ppermute | solution.py:828
  244.7 3.1 %shard_map.213 = (f32[2,48,4608]{2,1,0:T(8,128)}, f32[2,48,4608]{2,1,0:T(8,128)}, f32[2,48,4608]{2,1,0:T(8,128)}, f32[2,48,4608]{2,1,0:T(8,128)}) custom-call(s32[1]{0:T(128)} %bitcast.refs_1_.refs_0_.core_ref, bf16[48,2560]{1,0:T(8,128)(2,1)} %copy-done.1, ...), custom_call_target="tpu_custom_call", output_to_operand_aliasing={{0}: (6, {}), {1}: (7, {}), {2}: (8, {}), {3}: (9, {})} | custom-call | flops 1000000 | bytes 4000000 | tf_op jit(solution)/shard_map/pallas_call | solution.py:839
  (228 shorter events, 60.2 us)
Async XLA Ops:
  2.5 7.0 %collective-permute-start = (bf16[1,48,640]{2,1,0:T(8,128)(2,1)S(1)}, bf16[1,48,640]{2,1,0:T(8,128)(2,1)S(1)}, u32[]{:S(2)}, u32[]{:S(2)}) collective-permute-start(bf16[1,48,640]{2,1,0:T(8,128)(2,1)S(1)} %fusion.3.refs_4_.refs_10_), channel_id=1, source_target_pairs={{0,4},{1,5},{2,6},{3,7},{4,0},{5,1},{6,2},{7,3},{8,12},{9,13},{10,... | collective-permute-start | bytes 184328 | tf_op jit(solution)/shard_map/ppermute | solution.py:773
  6.6 13.9 %collective-permute-start.4 = (bf16[1,48,640]{2,1,0:T(8,128)(2,1)S(1)}, bf16[1,48,640]{2,1,0:T(8,128)(2,1)S(1)}, u32[]{:S(2)}, u32[]{:S(2)}) collective-permute-start(bf16[1,48,640]{2,1,0:T(8,128)(2,1)S(1)} %fusion.3.refs_4_.refs_10_), channel_id=1, source_target_pairs={{0,1},{1,0},{2,3},{3,2},{4,5},{5,4},{6,7},{7,6},{8,9},{9,8},{10,11... | collective-permute-start | bytes 184328 | tf_op jit(solution)/shard_map/ppermute | solution.py:768
  8.2 12.5 %collective-permute-start.7 = (bf16[1,48,640]{2,1,0:T(8,128)(2,1)S(1)}, bf16[1,48,640]{2,1,0:T(8,128)(2,1)S(1)}, u32[]{:S(2)}, u32[]{:S(2)}) collective-permute-start(bf16[1,48,640]{2,1,0:T(8,128)(2,1)S(1)} %fusion.3.refs_4_.refs_10_), channel_id=1, source_target_pairs={{0,8},{8,0},{16,24},{24,16},{1,9},{9,1},{17,25},{25,17},{2,10},{10... | collective-permute-start | bytes 184328 | tf_op jit(solution)/shard_map/ppermute | solution.py:752
  9.5 6.2 %collective-permute-start.3 = (bf16[2,48,640]{2,1,0:T(8,128)(2,1)S(1)}, bf16[2,48,640]{2,1,0:T(8,128)(2,1)S(1)}, u32[]{:S(2)}, u32[]{:S(2)}) collective-permute-start(bf16[2,48,640]{2,1,0:T(8,128)(2,1)S(1)} %pad_maximum_fusion.4), channel_id=1, source_target_pairs={{0,2},{1,3},{2,0},{3,1},{4,6},{5,7},{6,4},{7,5},{8,10},{9,11},{10,... | collective-permute-start | bytes 368648 | tf_op jit(solution)/shard_map/ppermute | solution.py:773
  10.9 10.9 %collective-permute-start.1 = (bf16[1,48,1792]{2,1,0:T(8,128)(2,1)S(1)}, bf16[1,48,1792]{2,1,0:T(8,128)(2,1)S(1)}, u32[]{:S(2)}, u32[]{:S(2)}) collective-permute-start(bf16[1,48,1792]{2,1,0:T(8,128)(2,1)S(1)} %bitcast.47), channel_id=1, source_target_pairs={{0,4},{1,5},{2,6},{3,7},{4,0},{5,1},{6,2},{7,3},{8,12},{9,13},{10,... | collective-permute-start | bytes 516104 | tf_op jit(solution)/shard_map/ppermute | solution.py:773
  14.2 6.9 %collective-permute-start.5 = (bf16[1,48,640]{2,1,0:T(8,128)(2,1)S(1)}, bf16[1,48,640]{2,1,0:T(8,128)(2,1)S(1)}, u32[]{:S(2)}, u32[]{:S(2)}) collective-permute-start(bf16[1,48,640]{2,1,0:T(8,128)(2,1)S(1)} %collective-permute-done.refs_5_.refs_11_), channel_id=1, source_target_pairs={{0,1},{1,0},{2,3},{3,2},{4,5},{5,4},{6,7},{7,6},{8,9},{9,8},{10,11... | collective-permute-start | bytes 184328 | tf_op jit(solution)/shard_map/ppermute | solution.py:768
  22.4 26.7 %collective-permute-start.15 = (bf16[1,48,1792]{2,1,0:T(8,128)(2,1)S(1)}, bf16[1,48,1792]{2,1,0:T(8,128)(2,1)S(1)}, u32[]{:S(2)}, u32[]{:S(2)}) collective-permute-start(bf16[1,48,1792]{2,1,0:T(8,128)(2,1)S(1)} %bitcast.49), channel_id=1, source_target_pairs={{0,1},{1,0},{2,3},{3,2},{4,5},{5,4},{6,7},{7,6},{8,9},{9,8},{10,11... | collective-permute-start | bytes 516104 | tf_op jit(solution)/shard_map/ppermute | solution.py:768
  24.1 16.0 %collective-permute-start.17 = (bf16[1,48,2432]{2,1,0:T(8,128)(2,1)S(1)}, bf16[1,48,2432]{2,1,0:T(8,128)(2,1)S(1)}, u32[]{:S(2)}, u32[]{:S(2)}) collective-permute-start(bf16[1,48,2432]{2,1,0:T(8,128)(2,1)S(1)} %bitcast.40), channel_id=1, source_target_pairs={{0,1},{1,0},{2,3},{3,2},{4,5},{5,4},{6,7},{7,6},{8,9},{9,8},{10,11... | collective-permute-start | bytes 700424 | tf_op jit(solution)/shard_map/ppermute | solution.py:768
  24.6 17.2 %collective-permute-start.2 = (bf16[1,48,2432]{2,1,0:T(8,128)(2,1)S(1)}, bf16[1,48,2432]{2,1,0:T(8,128)(2,1)S(1)}, u32[]{:S(2)}, u32[]{:S(2)}) collective-permute-start(bf16[1,48,2432]{2,1,0:T(8,128)(2,1)S(1)} %bitcast.41), channel_id=1, source_target_pairs={{0,4},{1,5},{2,6},{3,7},{4,0},{5,1},{6,2},{7,3},{8,12},{9,13},{10,... | collective-permute-start | bytes 700424 | tf_op jit(solution)/shard_map/ppermute | solution.py:773
  25.5 14.8 %collective-permute-start.14 = (bf16[2,48,1792]{2,1,0:T(8,128)(2,1)S(1)}, bf16[2,48,1792]{2,1,0:T(8,128)(2,1)S(1)}, u32[]{:S(2)}, u32[]{:S(2)}) collective-permute-start(bf16[2,48,1792]{2,1,0:T(8,128)(2,1)S(1)} %pad_maximum_fusion.1), channel_id=1, source_target_pairs={{0,2},{1,3},{2,0},{3,1},{4,6},{5,7},{6,4},{7,5},{8,10},{9,11},{10,... | collective-permute-start | bytes 1032200 | tf_op jit(solution)/shard_map/ppermute | solution.py:773
  27.6 12.5 %collective-permute-start.16 = (bf16[1,48,1792]{2,1,0:T(8,128)(2,1)S(1)}, bf16[1,48,1792]{2,1,0:T(8,128)(2,1)S(1)}, u32[]{:S(2)}, u32[]{:S(2)}) collective-permute-start(bf16[1,48,1792]{2,1,0:T(8,128)(2,1)S(1)} %collective-permute-done.1.refs_0_.refs_7_.refs_10_.refs_23_), channel_id=1, source_target_pairs={{0,1},{1,0},{2,3},{3,2},{4,5},{5,4},{6,7},{7,6},{8,9},{9,8},{10,11... | collective-permute-start | bytes 516104 | tf_op jit(solution)/shard_map/ppermute | solution.py:768
  40.2 8.9 %collective-permute-start.18 = (bf16[2,48,1792]{2,1,0:T(8,128)(2,1)S(1)}, bf16[2,48,1792]{2,1,0:T(8,128)(2,1)S(1)}, u32[]{:S(2)}, u32[]{:S(2)}) collective-permute-start(bf16[2,48,1792]{2,1,0:T(8,128)(2,1)S(1)} %collective-permute-done.14.refs_8_.refs_11_.refs_24_), channel_id=1, source_target_pairs={{0,1},{1,0},{2,3},{3,2},{4,5},{5,4},{6,7},{7,6},{8,9},{9,8},{10,11... | collective-permute-start | bytes 1032200 | tf_op jit(solution)/shard_map/ppermute | solution.py:768
  41.8 11.5 %collective-permute-start.13 = (bf16[2,48,2432]{2,1,0:T(8,128)(2,1)S(1)}, bf16[2,48,2432]{2,1,0:T(8,128)(2,1)S(1)}, u32[]{:S(2)}, u32[]{:S(2)}) collective-permute-start(bf16[2,48,2432]{2,1,0:T(8,128)(2,1)S(1)} %pad_maximum_fusion), channel_id=1, source_target_pairs={{0,2},{1,3},{2,0},{3,1},{4,6},{5,7},{6,4},{7,5},{8,10},{9,11},{10,... | collective-permute-start | bytes 1400840 | tf_op jit(solution)/shard_map/ppermute | solution.py:773
  42.1 7.6 %collective-permute-start.19 = (bf16[1,48,1792]{2,1,0:T(8,128)(2,1)S(1)}, bf16[1,48,1792]{2,1,0:T(8,128)(2,1)S(1)}, u32[]{:S(2)}, u32[]{:S(2)}) collective-permute-start(bf16[1,48,1792]{2,1,0:T(8,128)(2,1)S(1)} %bitcast.50), channel_id=1, source_target_pairs={{0,8},{8,0},{16,24},{24,16},{1,9},{9,1},{17,25},{25,17},{2,10},{10... | collective-permute-start | bytes 516104 | tf_op jit(solution)/shard_map/ppermute | solution.py:752
  42.1 7.7 %collective-permute-start.20 = (bf16[1,48,1792]{2,1,0:T(8,128)(2,1)}, bf16[1,48,1792]{2,1,0:T(8,128)(2,1)S(1)}, u32[]{:S(2)}, u32[]{:S(2)}) collective-permute-start(bf16[1,48,1792]{2,1,0:T(8,128)(2,1)} %copy-done.14), channel_id=1, source_target_pairs={{0,8},{8,0},{16,24},{24,16},{1,9},{9,1},{17,25},{25,17},{2,10},{10... | collective-permute-start | bytes 516104 | tf_op jit(solution)/shard_map/ppermute | solution.py:752
  51.5 18.6 %collective-permute-start.27 = (bf16[1,48,2432]{2,1,0:T(8,128)(2,1)S(1)}, bf16[1,48,2432]{2,1,0:T(8,128)(2,1)}, u32[]{:S(2)}, u32[]{:S(2)}) collective-permute-start(bf16[1,48,2432]{2,1,0:T(8,128)(2,1)S(1)} %bitcast.43), channel_id=1, source_target_pairs={{0,8},{8,0},{16,24},{24,16},{1,9},{9,1},{17,25},{25,17},{2,10},{10... | collective-permute-start | bytes 700424 | tf_op jit(solution)/shard_map/ppermute | solution.py:752
  51.8 18.5 %collective-permute-start.25 = (bf16[1,48,2432]{2,1,0:T(8,128)(2,1)S(1)}, bf16[1,48,2432]{2,1,0:T(8,128)(2,1)}, u32[]{:S(2)}, u32[]{:S(2)}) collective-permute-start(bf16[1,48,2432]{2,1,0:T(8,128)(2,1)S(1)} %collective-permute-done.2.refs_6_.refs_11_.refs_23_), channel_id=1, source_target_pairs={{0,1},{1,0},{2,3},{3,2},{4,5},{5,4},{6,7},{7,6},{8,9},{9,8},{10,11... | collective-permute-start | bytes 700424 | tf_op jit(solution)/shard_map/ppermute | solution.py:768
  53.3 16.3 %collective-permute-start.26 = (bf16[2,48,2432]{2,1,0:T(8,128)(2,1)S(1)}, bf16[2,48,2432]{2,1,0:T(8,128)(2,1)S(1)}, u32[]{:S(2)}, u32[]{:S(2)}) collective-permute-start(bf16[2,48,2432]{2,1,0:T(8,128)(2,1)S(1)} %collective-permute-done.13.refs_0_.refs_7_.refs_12_.refs_24_), channel_id=1, source_target_pairs={{0,1},{1,0},{2,3},{3,2},{4,5},{5,4},{6,7},{7,6},{8,9},{9,8},{10,11... | collective-permute-start | bytes 1400840 | tf_op jit(solution)/shard_map/ppermute | solution.py:768
  53.8 18.8 %collective-permute-start.29 = (bf16[2,48,2432]{2,1,0:T(8,128)(2,1)S(1)}, bf16[2,48,2432]{2,1,0:T(8,128)(2,1)S(1)}, u32[]{:S(2)}, u32[]{:S(2)}) collective-permute-start(bf16[2,48,2432]{2,1,0:T(8,128)(2,1)S(1)} %collective-permute-done.13.refs_0_.refs_7_.refs_12_.refs_24_), channel_id=1, source_target_pairs={{0,8},{8,0},{16,24},{24,16},{1,9},{9,1},{17,25},{25,17},{2,10},{10... | collective-permute-start | bytes 1400840 | tf_op jit(solution)/shard_map/ppermute | solution.py:752
  115.1 34.8 %all-to-all-start = ((bf16[8,48,1664]{2,1,0:T(8,128)(2,1)}), bf16[8,48,1664]{2,1,0:T(8,128)(2,1)S(1)}, u32[]{:S(2)}, u32[]{:S(2)}) async-start(bf16[8,48,1664]{2,1,0:T(8,128)(2,1)} %bitcast.10), calls=%async_computation | async-start | bytes 2555904 | tf_op jit(solution)/shard_map/all_to_all | solution.py:821
  153.0 23.3 %all-to-all-start.1 = ((bf16[8,48,896]{2,1,0:T(8,128)(2,1)}), bf16[8,48,896]{2,1,0:T(8,128)(2,1)S(1)}, u32[]{:S(2)}, u32[]{:S(2)}) async-start(bf16[8,48,896]{2,1,0:T(8,128)(2,1)} %bitcast.11), calls=%async_computation.1 | async-start | bytes 1376256 | tf_op jit(solution)/shard_map/all_to_all | solution.py:821
  182.3 38.7 %all-to-all-start.2 = ((bf16[8,48,1664]{2,1,0:T(8,128)(2,1)}), bf16[8,48,1664]{2,1,0:T(8,128)(2,1)S(1)}, u32[]{:S(2)}, u32[]{:S(2)}) async-start(bf16[8,48,1664]{2,1,0:T(8,128)(2,1)} %bitcast.38), calls=%async_computation.2 | async-start | bytes 2555904 | tf_op jit(solution)/shard_map/all_to_all | solution.py:821
  225.6 24.1 %all-to-all-start.3 = ((bf16[8,48,896]{2,1,0:T(8,128)(2,1)}), bf16[8,48,896]{2,1,0:T(8,128)(2,1)S(1)}, u32[]{:S(2)}, u32[]{:S(2)}) async-start(bf16[8,48,896]{2,1,0:T(8,128)(2,1)} %bitcast.14), calls=%async_computation.3 | async-start | bytes 1376256 | tf_op jit(solution)/shard_map/all_to_all | solution.py:821
  231.5 7.8 %collective-permute-start.39 = (bf16[48,2560]{1,0:T(8,128)(2,1)S(1)}, bf16[48,2560]{1,0:T(8,128)(2,1)S(1)}, u32[]{:S(2)}, u32[]{:S(2)}) collective-permute-start(bf16[48,2560]{1,0:T(8,128)(2,1)S(1)} %pad_maximum_fusion.2), channel_id=1, source_target_pairs={{0,16},{8,24},{16,0},{24,8},{1,17},{9,25},{17,1},{25,9},{2,18},{10... | collective-permute-start | bytes 737288 | tf_op jit(solution)/shard_map/ppermute | solution.py:828
  (75 other events, 497.7 us)

commit v3 on v2

--- a/solution.py
+++ b/solution.py
@@ -283,9 +283,13 @@
 
         @pl.when(step == 0)
         def _():
-            load_weights(core_ref, place_ref, sources, start, w_ref, sems)
+            copies = weight_copies(core_ref, place_ref, sources, start, w_ref, sems)
+            for copy in copies:
+                copy.start()
             for ref in (up_ref, down_ref, acc_ref, bias_ref):
                 ref[...] = jnp.zeros_like(ref)
+            for copy in copies:
+                copy.wait()
 
     if last:
         for i in range(PAIR):
@@ -949,11 +953,15 @@
                 if first:
                     parts, at = groups.pop(0)
                     outs = finish([(after(parts, g), at)], outs)
-            if groups:
+            if groups and half == 0:
                 parts, at = groups[-1]
-                keep, send, turned, outs, parts = lax.optimization_barrier((keep, send, turned, outs, parts))
+                keep, send, parts = lax.optimization_barrier((keep, send, parts))
                 groups[-1] = parts, at
             joined = join_cores(keep, send)
+            if groups and half == 1:
+                parts, at = groups[-1]
+                joined, turned, outs, parts = lax.optimization_barrier((joined, turned, outs, parts))
+                groups[-1] = parts, at
             before = [joined]
             groups.append((exchange_shards(joined), spot))
     output = turned.swapaxes(0, 1)

time: 260 us -> 254 us (0.977)
  waiting for transfers between devices: 42.8 us -> 38 us
    ppermute x25, waiting for transfers between devices: 14.5 us -> 11.1 us  [swap_cores(): return lax.ppermute(value, 'rep', flip('rep', 1))]
    unnamed x108 -> x104, local copies, waits for them, and re-layouts: 7.39 us -> 7.41 us
  transfers between devices with their start and end apart: 47 -> 47, of which waited for: 18 -> 17; matrix products, arithmetic and copies ran while one was open for 3% -> 4% of each run, Pallas kernels for 39% -> 40%
where the time goes in v3:
time: 254 us; the launch traced here: 253 us
  Pallas kernels  138 us (54%)
  starting transfers between devices  53.8 us (21%)
  waiting for transfers between devices  38 us (15%)
  other arithmetic  13.6 us (5%)
  local copies, waits for them, and re-layouts  7.95 us (3%)
    pallas_call x6, Pallas kernels, call(): return lambda *args: made(*after, *args)  122 us
    all_to_all x4, starting transfers between devices, exchange_shards(): lax.all_to_all(joined.reshape(count, rows // count, cols), 'shard', 0, 0,...  19.2 us
    ppermute x9, starting transfers between devices, neighbour(): return lax.ppermute(piece, 'shard', flip('shard', 1))  13.4 us
    ppermute x6, starting transfers between devices, step(): self.near.append(lax.ppermute(have, 'shard', flip('shard', bit)))  12 us
    ppermute x3, waiting for transfers between devices, finish_groups(): other = lax.ppermute(mine, 'rep', flip('rep', bit))  11.7 us
    pallas_call x4, Pallas kernels, update_group(): pl.pallas_call(functools.partial(step_kernel, start), grid=(2,), in_specs...  11.2 us
    ppermute x25, waiting for transfers between devices, swap_cores(): return lax.ppermute(value, 'rep', flip('rep', 1))  11.1 us
    convert_element_type x4, other arithmetic, join_cores(): return (keep.astype(F32) + other.astype(F32)).astype(BF16)  7.42 us
  transfers between devices with their start and end apart: 47, of which 17 were waited for; matrix products, arithmetic and copies ran while one was open for 4% of the time, Pallas kernels for 40%

profile of v3, /device:TPU:0, one launch (start us, length us, event | category | flops | bytes accessed | tf_op | source)
XLA Modules:
  0.0 253.3 jit_solution(146337337457581658)
XLA Ops:
  2.5 4.1 %collective-permute-start = (bf16[1,48,640]{2,1,0:T(8,128)(2,1)S(1)}, bf16[1,48,640]{2,1,0:T(8,128)(2,1)S(1)}, u32[]{:S(2)}, u32[]{:S(2)}) collective-permute-start(bf16[1,48,640]{2,1,0:T(8,128)(2,1)S(1)} %fusion.3.refs_4_.refs_10_), channel_id=1, source_target_pairs={{0,4},{1,5},{2,6},{3,7},{4,0},{5,1},{6,2},{7,3},{8,12},{9,13},{10,... | collective-permute-start | bytes 184328 | tf_op jit(solution)/shard_map/ppermute | solution.py:777
  10.9 3.4 %collective-permute-start.1 = (bf16[1,48,1792]{2,1,0:T(8,128)(2,1)S(1)}, bf16[1,48,1792]{2,1,0:T(8,128)(2,1)S(1)}, u32[]{:S(2)}, u32[]{:S(2)}) collective-permute-start(bf16[1,48,1792]{2,1,0:T(8,128)(2,1)S(1)} %bitcast.47), channel_id=1, source_target_pairs={{0,4},{1,5},{2,6},{3,7},{4,0},{5,1},{6,2},{7,3},{8,12},{9,13},{10,... | collective-permute-start | bytes 516104 | tf_op jit(solution)/shard_map/ppermute | solution.py:777
  15.8 3.1 %collective-permute-start.6 = (bf16[2,48,640]{2,1,0:T(8,128)(2,1)S(1)}, bf16[2,48,640]{2,1,0:T(8,128)(2,1)S(1)}, u32[]{:S(2)}, u32[]{:S(2)}) collective-permute-start(bf16[2,48,640]{2,1,0:T(8,128)(2,1)S(1)} %collective-permute-done.3.refs_6_.refs_12_), channel_id=1, source_target_pairs={{0,1},{1,0},{2,3},{3,2},{4,5},{5,4},{6,7},{7,6},{8,9},{9,8},{10,11... | collective-permute-start | bytes 368648 | tf_op jit(solution)/shard_map/ppermute | solution.py:772
  29.1 10.9 %shard_map.204 = (bf16[1664,1152]{1,0:T(8,128)(2,1)}, bf16[1664,384]{1,0:T(8,128)(2,1)}, f32[8,8,256]{2,1,0:T(8,128)}, f32[16,384]{1,0:T(8,128)}, f32[1664,384]{1,0:T(8,128)}) custom-call(bf16[1,48,1792]{2,1,0:T(8,128)(2,1)} %copy-done.14, s32[1]{0:T(128)} %bitcast.refs_1_.refs_0_.core_ref, s32[8]{0:T(128)} %broadcast_xor_fusion.refs_2_.refs_1_.refs_3_, ...), custom_call_target="tpu_custom_call" | custom-call | flops 16999999488 | bytes 20000000 | tf_op jit(solution)/shard_map/pallas_call | solution.py:582
  42.5 6.6 %collective-permute-done.18.refs_11_.refs_14_.refs_27_ = bf16[2,48,1792]{2,1,0:T(8,128)(2,1)S(1)} collective-permute-done((bf16[2,48,1792]{2,1,0:T(8,128)(2,1)S(1)}, bf16[2,48,1792]{2,1,0:T(8,128)(2,1)S(1)}, u32[]{:S(2)}, u32[]{:S(2)}) %collective-permute-start.18) | collective-permute-done | bytes 344096 | tf_op jit(solution)/shard_map/ppermute | solution.py:772
  54.7 14.3 %shard_map.205 = (f32[1664,384]{1,0:T(8,128)}, bf16[1664,1536]{1,0:T(8,128)(2,1)}, f32[1664,1536]{1,0:T(8,128)}, f32[1664,384]{1,0:T(8,128)}) custom-call(bf16[2,48,2432]{2,1,0:T(8,128)(2,1)} %copy-done.21, s32[1]{0:T(128)} %bitcast.refs_1_.refs_0_.core_ref, s32[8]{0:T(128)} %broadcast_xor_fusion.refs_2_.refs_1_.refs_3_, ...), custom_call_target="tpu_custom_call" | custom-call | flops 22000001024 | bytes 30000000 | tf_op jit(solution)/shard_map/pallas_call | solution.py:582
  74.0 34.8 %shard_map.206 = (bf16[1664,1152]{1,0:T(8,128)(2,1)}, bf16[1664,384]{1,0:T(8,128)(2,1)}, f32[8,8,256]{2,1,0:T(8,128)}, f32[16,384]{1,0:T(8,128)}, f32[8,197,384]...) custom-call(s32[1]{0:T(128)} %bitcast.refs_1_.refs_0_.core_ref, ...), custom_call_target="tpu_custom_call" | custom-call | flops 44999999488 | bytes 30000000 | tf_op jit(solution)/shard_map/pallas_call | solution.py:582
  109.1 3.0 %collective-permute-done.33 = bf16[384,1664]{1,0:T(8,128)(2,1)S(1)} collective-permute-done((bf16[384,1664]{1,0:T(8,128)(2,1)}, bf16[384,1664]{1,0:T(8,128)(2,1)S(1)}, u32[]{:S(2)}, u32[]{:S(2)}) %collective-permute-start.33) | collective-permute-done | bytes 1277984 | tf_op jit(solution)/shard_map/ppermute | solution.py:756
  112.1 2.7 %add_convert_fusion.1.refs_0_ = bf16[384,1664]{1,0:T(8,128)(2,1)} fusion(bf16[384,1664]{1,0:T(8,128)(2,1)S(1)} %collective-permute-done.33, bf16[384,1664]{1,0:T(8,128)(2,1)} %get-tuple-element.91), kind=kLoop, calls=%fused_computation.1 | loop fusion | flops 2555904 | bytes 3833856 | tf_op jit(solution)/shard_map/convert_element_type | solution.py:819
  114.8 3.8 %all-to-all-start = ((bf16[8,48,1664]{2,1,0:T(8,128)(2,1)}), bf16[8,48,1664]{2,1,0:T(8,128)(2,1)S(1)}, u32[]{:S(2)}, u32[]{:S(2)}) async-start(bf16[8,48,1664]{2,1,0:T(8,128)(2,1)} %bitcast.10), calls=%async_computation | async-start | bytes 2555904 | tf_op jit(solution)/shard_map/all_to_all | solution.py:825
  118.6 21.3 %shard_map.207 = (f32[1664,384]{1,0:T(8,128)}, bf16[384,896]{1,0:T(8,128)(2,1)}, bf16[384,896]{1,0:T(8,128)(2,1)}) custom-call(bf16[384,1664]{1,0:T(8,128)(2,1)} %add_convert_fusion.1.refs_0_, s32[1]{0:T(128)} %bitcast.refs_1_.refs_0_.core_ref, s32[8]{0:T(128)} %broadcast_xor_fusion.refs_2_.refs_1_.refs_3_, s32[8]{0:T(128)} %broadcast_xor_fusion.refs_2_.refs_1_.refs_3_, ...), custom_call_target="tpu_custom_call" | custom-call | flops 30000001024 | bytes 20000000 | tf_op jit(solution)/shard_map/pallas_call | solution.py:582
  140.1 4.6 %shard_map.208 = f32[197,8,384]{2,1,0:T(8,128)} custom-call(f32[8,197,384]{2,1,0:T(8,128)} %get-tuple-element.102.in_ref), custom_call_target="tpu_custom_call" | custom-call | flops 1000000 | bytes 5000000 | tf_op jit(solution)/shard_map/pallas_call | solution.py:806
  145.7 3.8 %all-to-all-done = bf16[8,48,1664]{2,1,0:T(8,128)(2,1)S(1)} async-done(((bf16[8,48,1664]{2,1,0:T(8,128)(2,1)}), bf16[8,48,1664]{2,1,0:T(8,128)(2,1)S(1)}, u32[]{:S(2)}, u32[]{:S(2)}) %all-to-all-start) | async-done | bytes 1277984 | tf_op jit(solution)/shard_map/all_to_all | solution.py:825
  149.6 3.6 %all-to-all-start.1 = ((bf16[8,48,896]{2,1,0:T(8,128)(2,1)}), bf16[8,48,896]{2,1,0:T(8,128)(2,1)S(1)}, u32[]{:S(2)}, u32[]{:S(2)}) async-start(bf16[8,48,896]{2,1,0:T(8,128)(2,1)} %bitcast.11), calls=%async_computation.1 | async-start | bytes 1376256 | tf_op jit(solution)/shard_map/all_to_all | solution.py:825
  153.2 19.4 %shard_map.209 = (f32[1664,384]{1,0:T(8,128)}, bf16[384,1664]{1,0:T(8,128)(2,1)}, bf16[384,1664]{1,0:T(8,128)(2,1)}) custom-call(bf16[384,896]{1,0:T(8,128)(2,1)} %add_convert_fusion.3.refs_0_, s32[1]{0:T(128)} %bitcast.refs_1_.refs_0_.core_ref, s32[8]{0:T(128)} %broadcast_xor_fusion.refs_2_.refs_1_.refs_3_, s32[1]{0:T(128)S(6)} %copy.68.refs_2_.refs_3_, ...), custom_call_target="tpu_custom_call" | custom-call | flops 24000000000 | bytes 30000000 | tf_op jit(solution)/shard_map/pallas_call | solution.py:582
  172.7 3.2 %collective-permute-done.35 = bf16[384,1664]{1,0:T(8,128)(2,1)S(1)} collective-permute-done((bf16[384,1664]{1,0:T(8,128)(2,1)}, bf16[384,1664]{1,0:T(8,128)(2,1)S(1)}, u32[]{:S(2)}, u32[]{:S(2)}) %collective-permute-start.35) | collective-permute-done | bytes 1277984 | tf_op jit(solution)/shard_map/ppermute | solution.py:756
  175.9 2.7 %add_convert_fusion.refs_0_ = bf16[384,1664]{1,0:T(8,128)(2,1)} fusion(bf16[384,1664]{1,0:T(8,128)(2,1)S(1)} %collective-permute-done.35, bf16[384,1664]{1,0:T(8,128)(2,1)} %get-tuple-element.108), kind=kLoop, calls=%fused_computation | loop fusion | flops 2555904 | bytes 3833856 | tf_op jit(solution)/shard_map/convert_element_type | solution.py:819
  178.6 6.0 %all-to-all-start.2 = ((bf16[8,48,1664]{2,1,0:T(8,128)(2,1)}), bf16[8,48,1664]{2,1,0:T(8,128)(2,1)S(1)}, u32[]{:S(2)}, u32[]{:S(2)}) async-start(bf16[8,48,1664]{2,1,0:T(8,128)(2,1)} %bitcast.38), calls=%async_computation.2 | async-start | bytes 2555904 | tf_op jit(solution)/shard_map/all_to_all | solution.py:825
  184.6 21.3 %shard_map.210 = (f32[8,197,384]{2,1,0:T(8,128)}, bf16[384,896]{1,0:T(8,128)(2,1)}, bf16[384,896]{1,0:T(8,128)(2,1)}) custom-call(bf16[384,1664]{1,0:T(8,128)(2,1)} %add_convert_fusion.refs_0_, s32[1]{0:T(128)} %bitcast.refs_1_.refs_0_.core_ref, s32[8]{0:T(128)} %broadcast_xor_fusion.refs_2_.refs_1_.refs_3_, s32[8]{0:T(128)} %broadcast_xor_fusion.refs_2_.refs_1_.refs_3_, ...), custom_call_target="tpu_custom_call" | custom-call | flops 30000001024 | bytes 20000000 | tf_op jit(solution)/shard_map/pallas_call | solution.py:582
  207.6 4.4 %collective-permute-done.37 = bf16[48,1664]{1,0:T(8,128)(2,1)S(1)} collective-permute-done((bf16[48,1664]{1,0:T(8,128)(2,1)S(1)}, bf16[48,1664]{1,0:T(8,128)(2,1)S(1)}, u32[]{:S(2)}, u32[]{:S(2)}) %collective-permute-start.37) | collective-permute-done | bytes 159776 | tf_op jit(solution)/shard_map/ppermute | solution.py:832
  214.6 3.1 %shard_map.211 = (f32[2,48,4608]{2,1,0:T(8,128)}, f32[2,48,4608]{2,1,0:T(8,128)}, f32[2,48,4608]{2,1,0:T(8,128)}, f32[2,48,4608]{2,1,0:T(8,128)}) custom-call(s32[1]{0:T(128)} %bitcast.refs_1_.refs_0_.core_ref, bf16[48,1664]{1,0:T(8,128)(2,1)} %copy-done.6, bf16[48,1664]{1,0:T(8,128)(2,1)} %collective-permute-done.38.other_ref, f32[2,48,4608]{2,1,0:T(8,128)} %one_ref.7, ...), custom_call_target="tpu_custom_call" | custom-call | flops 1000000 | bytes 4000000 | tf_op jit(solution)/shard_map/pallas_call | solution.py:843
  218.8 5.7 %all-to-all-start.3 = ((bf16[8,48,896]{2,1,0:T(8,128)(2,1)}), bf16[8,48,896]{2,1,0:T(8,128)(2,1)S(1)}, u32[]{:S(2)}, u32[]{:S(2)}) async-start(bf16[8,48,896]{2,1,0:T(8,128)(2,1)} %bitcast.14), calls=%async_computation.3 | async-start | bytes 1376256 | tf_op jit(solution)/shard_map/all_to_all | solution.py:825
  226.2 6.2 %collective-permute-done.39 = bf16[48,2560]{1,0:T(8,128)(2,1)S(1)} collective-permute-done((bf16[48,2560]{1,0:T(8,128)(2,1)S(1)}, bf16[48,2560]{1,0:T(8,128)(2,1)S(1)}, u32[]{:S(2)}, u32[]{:S(2)}) %collective-permute-start.39) | collective-permute-done | bytes 245792 | tf_op jit(solution)/shard_map/ppermute | solution.py:832
  237.3 3.3 %shard_map.213 = (f32[2,48,4608]{2,1,0:T(8,128)}, f32[2,48,4608]{2,1,0:T(8,128)}, f32[2,48,4608]{2,1,0:T(8,128)}, f32[2,48,4608]{2,1,0:T(8,128)}) custom-call(s32[1]{0:T(128)} %bitcast.refs_1_.refs_0_.core_ref, bf16[48,2560]{1,0:T(8,128)(2,1)} %copy-done.1, ...), custom_call_target="tpu_custom_call", output_to_operand_aliasing={{0}: (6, {}), {1}: (7, {}), {2}: (8, {}), {3}: (9, {})} | custom-call | flops 1000000 | bytes 4000000 | tf_op jit(solution)/shard_map/pallas_call | solution.py:843
  (224 shorter events, 55.9 us)
Async XLA Ops:
  2.5 7.0 %collective-permute-start = (bf16[1,48,640]{2,1,0:T(8,128)(2,1)S(1)}, bf16[1,48,640]{2,1,0:T(8,128)(2,1)S(1)}, u32[]{:S(2)}, u32[]{:S(2)}) collective-permute-start(bf16[1,48,640]{2,1,0:T(8,128)(2,1)S(1)} %fusion.3.refs_4_.refs_10_), channel_id=1, source_target_pairs={{0,4},{1,5},{2,6},{3,7},{4,0},{5,1},{6,2},{7,3},{8,12},{9,13},{10,... | collective-permute-start | bytes 184328 | tf_op jit(solution)/shard_map/ppermute | solution.py:777
  6.6 13.9 %collective-permute-start.4 = (bf16[1,48,640]{2,1,0:T(8,128)(2,1)S(1)}, bf16[1,48,640]{2,1,0:T(8,128)(2,1)S(1)}, u32[]{:S(2)}, u32[]{:S(2)}) collective-permute-start(bf16[1,48,640]{2,1,0:T(8,128)(2,1)S(1)} %fusion.3.refs_4_.refs_10_), channel_id=1, source_target_pairs={{0,1},{1,0},{2,3},{3,2},{4,5},{5,4},{6,7},{7,6},{8,9},{9,8},{10,11... | collective-permute-start | bytes 184328 | tf_op jit(solution)/shard_map/ppermute | solution.py:772
  8.2 12.5 %collective-permute-start.7 = (bf16[1,48,640]{2,1,0:T(8,128)(2,1)S(1)}, bf16[1,48,640]{2,1,0:T(8,128)(2,1)S(1)}, u32[]{:S(2)}, u32[]{:S(2)}) collective-permute-start(bf16[1,48,640]{2,1,0:T(8,128)(2,1)S(1)} %fusion.3.refs_4_.refs_10_), channel_id=1, source_target_pairs={{0,8},{8,0},{16,24},{24,16},{1,9},{9,1},{17,25},{25,17},{2,10},{10... | collective-permute-start | bytes 184328 | tf_op jit(solution)/shard_map/ppermute | solution.py:756
  10.9 10.9 %collective-permute-start.1 = (bf16[1,48,1792]{2,1,0:T(8,128)(2,1)S(1)}, bf16[1,48,1792]{2,1,0:T(8,128)(2,1)S(1)}, u32[]{:S(2)}, u32[]{:S(2)}) collective-permute-start(bf16[1,48,1792]{2,1,0:T(8,128)(2,1)S(1)} %bitcast.47), channel_id=1, source_target_pairs={{0,4},{1,5},{2,6},{3,7},{4,0},{5,1},{6,2},{7,3},{8,12},{9,13},{10,... | collective-permute-start | bytes 516104 | tf_op jit(solution)/shard_map/ppermute | solution.py:777
  14.2 6.9 %collective-permute-start.5 = (bf16[1,48,640]{2,1,0:T(8,128)(2,1)S(1)}, bf16[1,48,640]{2,1,0:T(8,128)(2,1)S(1)}, u32[]{:S(2)}, u32[]{:S(2)}) collective-permute-start(bf16[1,48,640]{2,1,0:T(8,128)(2,1)S(1)} %collective-permute-done.refs_5_.refs_11_), channel_id=1, source_target_pairs={{0,1},{1,0},{2,3},{3,2},{4,5},{5,4},{6,7},{7,6},{8,9},{9,8},{10,11... | collective-permute-start | bytes 184328 | tf_op jit(solution)/shard_map/ppermute | solution.py:772
  22.4 26.7 %collective-permute-start.15 = (bf16[1,48,1792]{2,1,0:T(8,128)(2,1)S(1)}, bf16[1,48,1792]{2,1,0:T(8,128)(2,1)S(1)}, u32[]{:S(2)}, u32[]{:S(2)}) collective-permute-start(bf16[1,48,1792]{2,1,0:T(8,128)(2,1)S(1)} %bitcast.49), channel_id=1, source_target_pairs={{0,1},{1,0},{2,3},{3,2},{4,5},{5,4},{6,7},{7,6},{8,9},{9,8},{10,11... | collective-permute-start | bytes 516104 | tf_op jit(solution)/shard_map/ppermute | solution.py:772
  24.0 16.0 %collective-permute-start.17 = (bf16[1,48,2432]{2,1,0:T(8,128)(2,1)S(1)}, bf16[1,48,2432]{2,1,0:T(8,128)(2,1)S(1)}, u32[]{:S(2)}, u32[]{:S(2)}) collective-permute-start(bf16[1,48,2432]{2,1,0:T(8,128)(2,1)S(1)} %bitcast.40), channel_id=1, source_target_pairs={{0,1},{1,0},{2,3},{3,2},{4,5},{5,4},{6,7},{7,6},{8,9},{9,8},{10,11... | collective-permute-start | bytes 700424 | tf_op jit(solution)/shard_map/ppermute | solution.py:772
  24.5 17.2 %collective-permute-start.2 = (bf16[1,48,2432]{2,1,0:T(8,128)(2,1)S(1)}, bf16[1,48,2432]{2,1,0:T(8,128)(2,1)S(1)}, u32[]{:S(2)}, u32[]{:S(2)}) collective-permute-start(bf16[1,48,2432]{2,1,0:T(8,128)(2,1)S(1)} %bitcast.41), channel_id=1, source_target_pairs={{0,4},{1,5},{2,6},{3,7},{4,0},{5,1},{6,2},{7,3},{8,12},{9,13},{10,... | collective-permute-start | bytes 700424 | tf_op jit(solution)/shard_map/ppermute | solution.py:777
  25.4 14.8 %collective-permute-start.14 = (bf16[2,48,1792]{2,1,0:T(8,128)(2,1)S(1)}, bf16[2,48,1792]{2,1,0:T(8,128)(2,1)S(1)}, u32[]{:S(2)}, u32[]{:S(2)}) collective-permute-start(bf16[2,48,1792]{2,1,0:T(8,128)(2,1)S(1)} %pad_maximum_fusion.1), channel_id=1, source_target_pairs={{0,2},{1,3},{2,0},{3,1},{4,6},{5,7},{6,4},{7,5},{8,10},{9,11},{10,... | collective-permute-start | bytes 1032200 | tf_op jit(solution)/shard_map/ppermute | solution.py:777
  27.5 12.5 %collective-permute-start.16 = (bf16[1,48,1792]{2,1,0:T(8,128)(2,1)S(1)}, bf16[1,48,1792]{2,1,0:T(8,128)(2,1)S(1)}, u32[]{:S(2)}, u32[]{:S(2)}) collective-permute-start(bf16[1,48,1792]{2,1,0:T(8,128)(2,1)S(1)} %collective-permute-done.1.refs_0_.refs_7_.refs_10_.refs_23_), channel_id=1, source_target_pairs={{0,1},{1,0},{2,3},{3,2},{4,5},{5,4},{6,7},{7,6},{8,9},{9,8},{10,11... | collective-permute-start | bytes 516104 | tf_op jit(solution)/shard_map/ppermute | solution.py:772
  40.2 8.9 %collective-permute-start.18 = (bf16[2,48,1792]{2,1,0:T(8,128)(2,1)S(1)}, bf16[2,48,1792]{2,1,0:T(8,128)(2,1)S(1)}, u32[]{:S(2)}, u32[]{:S(2)}) collective-permute-start(bf16[2,48,1792]{2,1,0:T(8,128)(2,1)S(1)} %collective-permute-done.14.refs_8_.refs_11_.refs_24_), channel_id=1, source_target_pairs={{0,1},{1,0},{2,3},{3,2},{4,5},{5,4},{6,7},{7,6},{8,9},{9,8},{10,11... | collective-permute-start | bytes 1032200 | tf_op jit(solution)/shard_map/ppermute | solution.py:772
  41.8 11.5 %collective-permute-start.13 = (bf16[2,48,2432]{2,1,0:T(8,128)(2,1)S(1)}, bf16[2,48,2432]{2,1,0:T(8,128)(2,1)S(1)}, u32[]{:S(2)}, u32[]{:S(2)}) collective-permute-start(bf16[2,48,2432]{2,1,0:T(8,128)(2,1)S(1)} %pad_maximum_fusion), channel_id=1, source_target_pairs={{0,2},{1,3},{2,0},{3,1},{4,6},{5,7},{6,4},{7,5},{8,10},{9,11},{10,... | collective-permute-start | bytes 1400840 | tf_op jit(solution)/shard_map/ppermute | solution.py:777
  42.0 7.6 %collective-permute-start.19 = (bf16[1,48,1792]{2,1,0:T(8,128)(2,1)S(1)}, bf16[1,48,1792]{2,1,0:T(8,128)(2,1)S(1)}, u32[]{:S(2)}, u32[]{:S(2)}) collective-permute-start(bf16[1,48,1792]{2,1,0:T(8,128)(2,1)S(1)} %bitcast.50), channel_id=1, source_target_pairs={{0,8},{8,0},{16,24},{24,16},{1,9},{9,1},{17,25},{25,17},{2,10},{10... | collective-permute-start | bytes 516104 | tf_op jit(solution)/shard_map/ppermute | solution.py:756
  42.0 7.7 %collective-permute-start.20 = (bf16[1,48,1792]{2,1,0:T(8,128)(2,1)}, bf16[1,48,1792]{2,1,0:T(8,128)(2,1)S(1)}, u32[]{:S(2)}, u32[]{:S(2)}) collective-permute-start(bf16[1,48,1792]{2,1,0:T(8,128)(2,1)} %copy-done.14), channel_id=1, source_target_pairs={{0,8},{8,0},{16,24},{24,16},{1,9},{9,1},{17,25},{25,17},{2,10},{10... | collective-permute-start | bytes 516104 | tf_op jit(solution)/shard_map/ppermute | solution.py:756
  51.5 18.6 %collective-permute-start.27 = (bf16[1,48,2432]{2,1,0:T(8,128)(2,1)S(1)}, bf16[1,48,2432]{2,1,0:T(8,128)(2,1)}, u32[]{:S(2)}, u32[]{:S(2)}) collective-permute-start(bf16[1,48,2432]{2,1,0:T(8,128)(2,1)S(1)} %bitcast.43), channel_id=1, source_target_pairs={{0,8},{8,0},{16,24},{24,16},{1,9},{9,1},{17,25},{25,17},{2,10},{10... | collective-permute-start | bytes 700424 | tf_op jit(solution)/shard_map/ppermute | solution.py:756
  51.7 18.5 %collective-permute-start.25 = (bf16[1,48,2432]{2,1,0:T(8,128)(2,1)S(1)}, bf16[1,48,2432]{2,1,0:T(8,128)(2,1)}, u32[]{:S(2)}, u32[]{:S(2)}) collective-permute-start(bf16[1,48,2432]{2,1,0:T(8,128)(2,1)S(1)} %collective-permute-done.2.refs_6_.refs_11_.refs_23_), channel_id=1, source_target_pairs={{0,1},{1,0},{2,3},{3,2},{4,5},{5,4},{6,7},{7,6},{8,9},{9,8},{10,11... | collective-permute-start | bytes 700424 | tf_op jit(solution)/shard_map/ppermute | solution.py:772
  53.3 16.3 %collective-permute-start.26 = (bf16[2,48,2432]{2,1,0:T(8,128)(2,1)S(1)}, bf16[2,48,2432]{2,1,0:T(8,128)(2,1)S(1)}, u32[]{:S(2)}, u32[]{:S(2)}) collective-permute-start(bf16[2,48,2432]{2,1,0:T(8,128)(2,1)S(1)} %collective-permute-done.13.refs_0_.refs_7_.refs_12_.refs_24_), channel_id=1, source_target_pairs={{0,1},{1,0},{2,3},{3,2},{4,5},{5,4},{6,7},{7,6},{8,9},{9,8},{10,11... | collective-permute-start | bytes 1400840 | tf_op jit(solution)/shard_map/ppermute | solution.py:772
  53.9 18.6 %collective-permute-start.29 = (bf16[2,48,2432]{2,1,0:T(8,128)(2,1)S(1)}, bf16[2,48,2432]{2,1,0:T(8,128)(2,1)S(1)}, u32[]{:S(2)}, u32[]{:S(2)}) collective-permute-start(bf16[2,48,2432]{2,1,0:T(8,128)(2,1)S(1)} %collective-permute-done.13.refs_0_.refs_7_.refs_12_.refs_24_), channel_id=1, source_target_pairs={{0,8},{8,0},{16,24},{24,16},{1,9},{9,1},{17,25},{25,17},{2,10},{10... | collective-permute-start | bytes 1400840 | tf_op jit(solution)/shard_map/ppermute | solution.py:756
  114.8 34.8 %all-to-all-start = ((bf16[8,48,1664]{2,1,0:T(8,128)(2,1)}), bf16[8,48,1664]{2,1,0:T(8,128)(2,1)S(1)}, u32[]{:S(2)}, u32[]{:S(2)}) async-start(bf16[8,48,1664]{2,1,0:T(8,128)(2,1)} %bitcast.10), calls=%async_computation | async-start | bytes 2555904 | tf_op jit(solution)/shard_map/all_to_all | solution.py:825
  149.6 23.0 %all-to-all-start.1 = ((bf16[8,48,896]{2,1,0:T(8,128)(2,1)}), bf16[8,48,896]{2,1,0:T(8,128)(2,1)S(1)}, u32[]{:S(2)}, u32[]{:S(2)}) async-start(bf16[8,48,896]{2,1,0:T(8,128)(2,1)} %bitcast.11), calls=%async_computation.1 | async-start | bytes 1376256 | tf_op jit(solution)/shard_map/all_to_all | solution.py:825
  178.6 40.1 %all-to-all-start.2 = ((bf16[8,48,1664]{2,1,0:T(8,128)(2,1)}), bf16[8,48,1664]{2,1,0:T(8,128)(2,1)S(1)}, u32[]{:S(2)}, u32[]{:S(2)}) async-start(bf16[8,48,1664]{2,1,0:T(8,128)(2,1)} %bitcast.38), calls=%async_computation.2 | async-start | bytes 2555904 | tf_op jit(solution)/shard_map/all_to_all | solution.py:825
  207.6 10.0 %collective-permute-start.36 = (bf16[384,896]{1,0:T(8,128)(2,1)}, bf16[384,896]{1,0:T(8,128)(2,1)S(1)}, u32[]{:S(2)}, u32[]{:S(2)}) collective-permute-start(bf16[384,896]{1,0:T(8,128)(2,1)} %get-tuple-element.114), channel_id=1, source_target_pairs={{0,8},{8,0},{16,24},{24,16},{1,9},{9,1},{17,25},{25,17},{2,10},{10... | collective-permute-start | bytes 2064392 | tf_op jit(solution)/shard_map/ppermute | solution.py:756
  218.8 24.0 %all-to-all-start.3 = ((bf16[8,48,896]{2,1,0:T(8,128)(2,1)}), bf16[8,48,896]{2,1,0:T(8,128)(2,1)S(1)}, u32[]{:S(2)}, u32[]{:S(2)}) async-start(bf16[8,48,896]{2,1,0:T(8,128)(2,1)} %bitcast.14), calls=%async_computation.3 | async-start | bytes 1376256 | tf_op jit(solution)/shard_map/all_to_all | solution.py:825
  224.6 7.8 %collective-permute-start.39 = (bf16[48,2560]{1,0:T(8,128)(2,1)S(1)}, bf16[48,2560]{1,0:T(8,128)(2,1)S(1)}, u32[]{:S(2)}, u32[]{:S(2)}) collective-permute-start(bf16[48,2560]{1,0:T(8,128)(2,1)S(1)} %pad_maximum_fusion.2), channel_id=1, source_target_pairs={{0,16},{8,24},{16,0},{24,8},{1,17},{9,25},{17,1},{25,9},{2,18},{10... | collective-permute-start | bytes 737288 | tf_op jit(solution)/shard_map/ppermute | solution.py:832
  (73 other events, 472.0 us)

commit v4 on v3

--- a/solution.py
+++ b/solution.py
@@ -862,13 +862,16 @@
     core_arr = core.reshape(1).astype(jnp.int32)
     plan = Layers(core_arr, count, seq, width)
     packs = []
+    whole_weights = weights
     for index in range(layers):
-        low = weights[index].astype(BF16)
-        turned = jnp.pad(vectors[index].T.astype(BF16), ((0, 0), (0, TILE - vectors.shape[1])))
-        attn_pack = jnp.concatenate([low[:, : 3 * width], turned], 1)
-        rest = low[:, 3 * width :]
+        turned = jnp.pad(vectors[index].T, ((0, 0), (0, TILE - vectors.shape[1])))
+        attn_pack = jnp.concatenate([whole_weights[index, :, : 3 * width], turned], 1)
+        attn_own = own_half(attn_pack, core).astype(BF16)
+        if index == 0:
+            whole_weights = after(weights, attn_own)
+        rest = whole_weights[index, :, 3 * width :].astype(BF16)
         rest_pack = jnp.pad(rest, ((0, 0), (0, -rest.shape[1] % (2 * TILE))))
-        packs.append((own_half(attn_pack, core), own_half(rest_pack, core)))
+        packs.append((attn_own, own_half(rest_pack, core)))
     bits = []
     bit = lax.axis_size("shard") // 2
     while bit > 1:

time: 254 us -> 257 us (1.012)
  starting transfers between devices: 53.8 us -> 47.4 us
  waiting for transfers between devices: 38 us -> 43.7 us
  local copies, waits for them, and re-layouts: 7.95 us -> 10.9 us
    ppermute x9, starting transfers between devices: 13.4 us -> 8.84 us  [neighbour(): return lax.ppermute(piece, 'shard', flip('shard', 1))]
    ppermute x6, waiting for transfers between devices: 1.84 us -> 6.25 us  [step(): self.near.append(lax.ppermute(have, 'shard', flip('shard', bit)))]
    unnamed x104 -> x103, local copies, waits for them, and re-layouts: 7.41 us -> 7.64 us
  transfers between devices with their start and end apart: 47 -> 47, of which waited for: 17 -> 17; matrix products, arithmetic and copies ran while one was open for 4% -> 5% of each run, Pallas kernels for 40% -> 39%
where the time goes in v4:
time: 257 us; the launch traced here: 256 us
  Pallas kernels  138 us (54%)
  starting transfers between devices  47.4 us (18%)
  waiting for transfers between devices  43.7 us (17%)
  other arithmetic  13.6 us (5%)
  local copies, waits for them, and re-layouts  10.9 us (4%)
    pallas_call x6, Pallas kernels, call(): return lambda *args: made(*after, *args)  122 us
    all_to_all x4, starting transfers between devices, exchange_shards(): lax.all_to_all(joined.reshape(count, rows // count, cols), 'shard', 0, 0,...  19.2 us
    ppermute x3, waiting for transfers between devices, finish_groups(): other = lax.ppermute(mine, 'rep', flip('rep', bit))  11.7 us
    pallas_call x4, Pallas kernels, update_group(): pl.pallas_call(functools.partial(step_kernel, start), grid=(2,), in_specs...  11.2 us
    ppermute x25, waiting for transfers between devices, swap_cores(): return lax.ppermute(value, 'rep', flip('rep', 1))  11.1 us
    ppermute x6, starting transfers between devices, step(): self.near.append(lax.ppermute(have, 'shard', flip('shard', bit)))  10.3 us
    ppermute x9, starting transfers between devices, neighbour(): return lax.ppermute(piece, 'shard', flip('shard', 1))  8.84 us
    ppermute x9, waiting for transfers between devices, neighbour(): return lax.ppermute(piece, 'shard', flip('shard', 1))  8.45 us
  transfers between devices with their start and end apart: 47, of which 17 were waited for; matrix products, arithmetic and copies ran while one was open for 5% of the time, Pallas kernels for 39%

profile of v4, /device:TPU:0, one launch (start us, length us, event | category | flops | bytes accessed | tf_op | source)
XLA Modules:
  0.0 255.5 jit_solution(7468649817572352205)
XLA Ops:
  2.6 4.1 %collective-permute-start = (bf16[1,48,640]{2,1,0:T(8,128)(2,1)S(1)}, bf16[1,48,640]{2,1,0:T(8,128)(2,1)S(1)}, u32[]{:S(2)}, u32[]{:S(2)}) collective-permute-start(bf16[1,48,640]{2,1,0:T(8,128)(2,1)S(1)} %bitcast.55), channel_id=1, source_target_pairs={{0,4},{1,5},{2,6},{3,7},{4,0},{5,1},{6,2},{7,3},{8,12},{9,13},{10,... | collective-permute-start | bytes 184328 | tf_op jit(solution)/shard_map/ppermute | solution.py:777
  20.2 3.8 %collective-permute-done.1.refs_0_.refs_7_.refs_10_.refs_23_ = bf16[1,48,1792]{2,1,0:T(8,128)(2,1)S(1)} collective-permute-done((bf16[1,48,1792]{2,1,0:T(8,128)(2,1)S(1)}, bf16[1,48,1792]{2,1,0:T(8,128)(2,1)S(1)}, u32[]{:S(2)}, u32[]{:S(2)}) %collective-permute-start.1) | collective-permute-done | bytes 172064 | tf_op jit(solution)/shard_map/ppermute | solution.py:777
  30.3 10.9 %shard_map.204 = (bf16[1664,1152]{1,0:T(8,128)(2,1)}, bf16[1664,384]{1,0:T(8,128)(2,1)}, f32[8,8,256]{2,1,0:T(8,128)}, f32[16,384]{1,0:T(8,128)}, f32[1664,384]{1,0:T(8,128)}) custom-call(bf16[1,48,1792]{2,1,0:T(8,128)(2,1)} %copy-done.14, s32[1]{0:T(128)} %bitcast.refs_1_.refs_0_.core_ref, s32[8]{0:T(128)} %broadcast_xor_fusion.refs_2_.refs_1_.refs_3_, ...), custom_call_target="tpu_custom_call" | custom-call | flops 16999999488 | bytes 20000000 | tf_op jit(solution)/shard_map/pallas_call | solution.py:582
  43.5 7.8 %collective-permute-done.18.refs_11_.refs_14_.refs_27_ = bf16[2,48,1792]{2,1,0:T(8,128)(2,1)S(1)} collective-permute-done((bf16[2,48,1792]{2,1,0:T(8,128)(2,1)S(1)}, bf16[2,48,1792]{2,1,0:T(8,128)(2,1)S(1)}, u32[]{:S(2)}, u32[]{:S(2)}) %collective-permute-start.18) | collective-permute-done | bytes 344096 | tf_op jit(solution)/shard_map/ppermute | solution.py:772
  56.8 14.3 %shard_map.205 = (f32[1664,384]{1,0:T(8,128)}, bf16[1664,1536]{1,0:T(8,128)(2,1)}, f32[1664,1536]{1,0:T(8,128)}, f32[1664,384]{1,0:T(8,128)}) custom-call(bf16[2,48,2432]{2,1,0:T(8,128)(2,1)} %copy-done.20, s32[1]{0:T(128)} %bitcast.refs_1_.refs_0_.core_ref, s32[8]{0:T(128)} %broadcast_xor_fusion.refs_2_.refs_1_.refs_3_, ...), custom_call_target="tpu_custom_call" | custom-call | flops 22000001024 | bytes 30000000 | tf_op jit(solution)/shard_map/pallas_call | solution.py:582
  76.3 34.8 %shard_map.206 = (bf16[1664,1152]{1,0:T(8,128)(2,1)}, bf16[1664,384]{1,0:T(8,128)(2,1)}, f32[8,8,256]{2,1,0:T(8,128)}, f32[16,384]{1,0:T(8,128)}, f32[8,197,384]...) custom-call(s32[1]{0:T(128)} %bitcast.refs_1_.refs_0_.core_ref, ...), custom_call_target="tpu_custom_call" | custom-call | flops 44999999488 | bytes 30000000 | tf_op jit(solution)/shard_map/pallas_call | solution.py:582
  111.3 3.0 %collective-permute-done.33 = bf16[384,1664]{1,0:T(8,128)(2,1)S(1)} collective-permute-done((bf16[384,1664]{1,0:T(8,128)(2,1)}, bf16[384,1664]{1,0:T(8,128)(2,1)S(1)}, u32[]{:S(2)}, u32[]{:S(2)}) %collective-permute-start.33) | collective-permute-done | bytes 1277984 | tf_op jit(solution)/shard_map/ppermute | solution.py:756
  114.3 2.7 %add_convert_fusion.1.refs_0_ = bf16[384,1664]{1,0:T(8,128)(2,1)} fusion(bf16[384,1664]{1,0:T(8,128)(2,1)S(1)} %collective-permute-done.33, bf16[384,1664]{1,0:T(8,128)(2,1)} %get-tuple-element.93), kind=kLoop, calls=%fused_computation.1 | loop fusion | flops 2555904 | bytes 3833856 | tf_op jit(solution)/shard_map/convert_element_type | solution.py:819
  117.0 3.8 %all-to-all-start = ((bf16[8,48,1664]{2,1,0:T(8,128)(2,1)}), bf16[8,48,1664]{2,1,0:T(8,128)(2,1)S(1)}, u32[]{:S(2)}, u32[]{:S(2)}) async-start(bf16[8,48,1664]{2,1,0:T(8,128)(2,1)} %bitcast.12), calls=%async_computation | async-start | bytes 2555904 | tf_op jit(solution)/shard_map/all_to_all | solution.py:825
  120.8 21.3 %shard_map.207 = (f32[1664,384]{1,0:T(8,128)}, bf16[384,896]{1,0:T(8,128)(2,1)}, bf16[384,896]{1,0:T(8,128)(2,1)}) custom-call(bf16[384,1664]{1,0:T(8,128)(2,1)} %add_convert_fusion.1.refs_0_, s32[1]{0:T(128)} %bitcast.refs_1_.refs_0_.core_ref, s32[8]{0:T(128)} %broadcast_xor_fusion.refs_2_.refs_1_.refs_3_, s32[8]{0:T(128)} %broadcast_xor_fusion.refs_2_.refs_1_.refs_3_, ...), custom_call_target="tpu_custom_call" | custom-call | flops 30000001024 | bytes 20000000 | tf_op jit(solution)/shard_map/pallas_call | solution.py:582
  142.3 4.6 %shard_map.208 = f32[197,8,384]{2,1,0:T(8,128)} custom-call(f32[8,197,384]{2,1,0:T(8,128)} %get-tuple-element.104.in_ref), custom_call_target="tpu_custom_call" | custom-call | flops 1000000 | bytes 5000000 | tf_op jit(solution)/shard_map/pallas_call | solution.py:806
  148.0 3.8 %all-to-all-done = bf16[8,48,1664]{2,1,0:T(8,128)(2,1)S(1)} async-done(((bf16[8,48,1664]{2,1,0:T(8,128)(2,1)}), bf16[8,48,1664]{2,1,0:T(8,128)(2,1)S(1)}, u32[]{:S(2)}, u32[]{:S(2)}) %all-to-all-start) | async-done | bytes 1277984 | tf_op jit(solution)/shard_map/all_to_all | solution.py:825
  151.8 3.6 %all-to-all-start.1 = ((bf16[8,48,896]{2,1,0:T(8,128)(2,1)}), bf16[8,48,896]{2,1,0:T(8,128)(2,1)S(1)}, u32[]{:S(2)}, u32[]{:S(2)}) async-start(bf16[8,48,896]{2,1,0:T(8,128)(2,1)} %bitcast.13), calls=%async_computation.1 | async-start | bytes 1376256 | tf_op jit(solution)/shard_map/all_to_all | solution.py:825
  155.4 19.4 %shard_map.209 = (f32[1664,384]{1,0:T(8,128)}, bf16[384,1664]{1,0:T(8,128)(2,1)}, bf16[384,1664]{1,0:T(8,128)(2,1)}) custom-call(bf16[384,896]{1,0:T(8,128)(2,1)} %add_convert_fusion.3.refs_0_, s32[1]{0:T(128)} %bitcast.refs_1_.refs_0_.core_ref, s32[8]{0:T(128)} %broadcast_xor_fusion.refs_2_.refs_1_.refs_3_, s32[1]{0:T(128)S(6)} %copy.72.refs_2_.refs_3_, ...), custom_call_target="tpu_custom_call" | custom-call | flops 24000000000 | bytes 30000000 | tf_op jit(solution)/shard_map/pallas_call | solution.py:582
  174.9 3.2 %collective-permute-done.35 = bf16[384,1664]{1,0:T(8,128)(2,1)S(1)} collective-permute-done((bf16[384,1664]{1,0:T(8,128)(2,1)}, bf16[384,1664]{1,0:T(8,128)(2,1)S(1)}, u32[]{:S(2)}, u32[]{:S(2)}) %collective-permute-start.35) | collective-permute-done | bytes 1277984 | tf_op jit(solution)/shard_map/ppermute | solution.py:756
  178.1 2.7 %add_convert_fusion.refs_0_ = bf16[384,1664]{1,0:T(8,128)(2,1)} fusion(bf16[384,1664]{1,0:T(8,128)(2,1)S(1)} %collective-permute-done.35, bf16[384,1664]{1,0:T(8,128)(2,1)} %get-tuple-element.110), kind=kLoop, calls=%fused_computation | loop fusion | flops 2555904 | bytes 3833856 | tf_op jit(solution)/shard_map/convert_element_type | solution.py:819
  180.8 6.0 %all-to-all-start.2 = ((bf16[8,48,1664]{2,1,0:T(8,128)(2,1)}), bf16[8,48,1664]{2,1,0:T(8,128)(2,1)S(1)}, u32[]{:S(2)}, u32[]{:S(2)}) async-start(bf16[8,48,1664]{2,1,0:T(8,128)(2,1)} %bitcast.39), calls=%async_computation.2 | async-start | bytes 2555904 | tf_op jit(solution)/shard_map/all_to_all | solution.py:825
  186.8 21.3 %shard_map.210 = (f32[8,197,384]{2,1,0:T(8,128)}, bf16[384,896]{1,0:T(8,128)(2,1)}, bf16[384,896]{1,0:T(8,128)(2,1)}) custom-call(bf16[384,1664]{1,0:T(8,128)(2,1)} %add_convert_fusion.refs_0_, s32[1]{0:T(128)} %bitcast.refs_1_.refs_0_.core_ref, s32[8]{0:T(128)} %broadcast_xor_fusion.refs_2_.refs_1_.refs_3_, s32[8]{0:T(128)} %broadcast_xor_fusion.refs_2_.refs_1_.refs_3_, ...), custom_call_target="tpu_custom_call" | custom-call | flops 30000001024 | bytes 20000000 | tf_op jit(solution)/shard_map/pallas_call | solution.py:582
  209.9 4.3 %collective-permute-done.37 = bf16[48,1664]{1,0:T(8,128)(2,1)S(1)} collective-permute-done((bf16[48,1664]{1,0:T(8,128)(2,1)S(1)}, bf16[48,1664]{1,0:T(8,128)(2,1)S(1)}, u32[]{:S(2)}, u32[]{:S(2)}) %collective-permute-start.37) | collective-permute-done | bytes 159776 | tf_op jit(solution)/shard_map/ppermute | solution.py:832
  216.7 3.1 %shard_map.211 = (f32[2,48,4608]{2,1,0:T(8,128)}, f32[2,48,4608]{2,1,0:T(8,128)}, f32[2,48,4608]{2,1,0:T(8,128)}, f32[2,48,4608]{2,1,0:T(8,128)}) custom-call(s32[1]{0:T(128)} %bitcast.refs_1_.refs_0_.core_ref, bf16[48,1664]{1,0:T(8,128)(2,1)} %copy-done.6, bf16[48,1664]{1,0:T(8,128)(2,1)} %collective-permute-done.38.other_ref, f32[2,48,4608]{2,1,0:T(8,128)} %one_ref.7, ...), custom_call_target="tpu_custom_call" | custom-call | flops 1000000 | bytes 4000000 | tf_op jit(solution)/shard_map/pallas_call | solution.py:843
  221.0 5.8 %all-to-all-start.3 = ((bf16[8,48,896]{2,1,0:T(8,128)(2,1)}), bf16[8,48,896]{2,1,0:T(8,128)(2,1)S(1)}, u32[]{:S(2)}, u32[]{:S(2)}) async-start(bf16[8,48,896]{2,1,0:T(8,128)(2,1)} %bitcast.16), calls=%async_computation.3 | async-start | bytes 1376256 | tf_op jit(solution)/shard_map/all_to_all | solution.py:825
  228.4 6.2 %collective-permute-done.39 = bf16[48,2560]{1,0:T(8,128)(2,1)S(1)} collective-permute-done((bf16[48,2560]{1,0:T(8,128)(2,1)S(1)}, bf16[48,2560]{1,0:T(8,128)(2,1)S(1)}, u32[]{:S(2)}, u32[]{:S(2)}) %collective-permute-start.39) | collective-permute-done | bytes 245792 | tf_op jit(solution)/shard_map/ppermute | solution.py:832
  237.0 2.5 shard_map.212
  239.5 3.3 %shard_map.213 = (f32[2,48,4608]{2,1,0:T(8,128)}, f32[2,48,4608]{2,1,0:T(8,128)}, f32[2,48,4608]{2,1,0:T(8,128)}, f32[2,48,4608]{2,1,0:T(8,128)}) custom-call(s32[1]{0:T(128)} %bitcast.refs_1_.refs_0_.core_ref, bf16[48,2560]{1,0:T(8,128)(2,1)} %copy-done.1, ...), custom_call_target="tpu_custom_call", output_to_operand_aliasing={{0}: (6, {}), {1}: (7, {}), {2}: (8, {}), {3}: (9, {})} | custom-call | flops 1000000 | bytes 4000000 | tf_op jit(solution)/shard_map/pallas_call | solution.py:843
  (221 shorter events, 57.1 us)
Async XLA Ops:
  2.6 8.6 %collective-permute-start = (bf16[1,48,640]{2,1,0:T(8,128)(2,1)S(1)}, bf16[1,48,640]{2,1,0:T(8,128)(2,1)S(1)}, u32[]{:S(2)}, u32[]{:S(2)}) collective-permute-start(bf16[1,48,640]{2,1,0:T(8,128)(2,1)S(1)} %bitcast.55), channel_id=1, source_target_pairs={{0,4},{1,5},{2,6},{3,7},{4,0},{5,1},{6,2},{7,3},{8,12},{9,13},{10,... | collective-permute-start | bytes 184328 | tf_op jit(solution)/shard_map/ppermute | solution.py:777
  6.7 12.9 %collective-permute-start.4 = (bf16[1,48,640]{2,1,0:T(8,128)(2,1)S(1)}, bf16[1,48,640]{2,1,0:T(8,128)(2,1)S(1)}, u32[]{:S(2)}, u32[]{:S(2)}) collective-permute-start(bf16[1,48,640]{2,1,0:T(8,128)(2,1)S(1)} %bitcast.56), channel_id=1, source_target_pairs={{0,1},{1,0},{2,3},{3,2},{4,5},{5,4},{6,7},{7,6},{8,9},{9,8},{10,11... | collective-permute-start | bytes 184328 | tf_op jit(solution)/shard_map/ppermute | solution.py:772
  8.2 11.4 %collective-permute-start.7 = (bf16[1,48,640]{2,1,0:T(8,128)(2,1)S(1)}, bf16[1,48,640]{2,1,0:T(8,128)(2,1)S(1)}, u32[]{:S(2)}, u32[]{:S(2)}) collective-permute-start(bf16[1,48,640]{2,1,0:T(8,128)(2,1)S(1)} %bitcast.57), channel_id=1, source_target_pairs={{0,8},{8,0},{16,24},{24,16},{1,9},{9,1},{17,25},{25,17},{2,10},{10... | collective-permute-start | bytes 184328 | tf_op jit(solution)/shard_map/ppermute | solution.py:756
  12.9 11.1 %collective-permute-start.1 = (bf16[1,48,1792]{2,1,0:T(8,128)(2,1)S(1)}, bf16[1,48,1792]{2,1,0:T(8,128)(2,1)S(1)}, u32[]{:S(2)}, u32[]{:S(2)}) collective-permute-start(bf16[1,48,1792]{2,1,0:T(8,128)(2,1)S(1)} %bitcast.48), channel_id=1, source_target_pairs={{0,4},{1,5},{2,6},{3,7},{4,0},{5,1},{6,2},{7,3},{8,12},{9,13},{10,... | collective-permute-start | bytes 516104 | tf_op jit(solution)/shard_map/ppermute | solution.py:777
  17.2 6.8 %collective-permute-start.6 = (bf16[2,48,640]{2,1,0:T(8,128)(2,1)S(1)}, bf16[2,48,640]{2,1,0:T(8,128)(2,1)S(1)}, u32[]{:S(2)}, u32[]{:S(2)}) collective-permute-start(bf16[2,48,640]{2,1,0:T(8,128)(2,1)S(1)} %collective-permute-done.3.refs_6_.refs_12_), channel_id=1, source_target_pairs={{0,1},{1,0},{2,3},{3,2},{4,5},{5,4},{6,7},{7,6},{8,9},{9,8},{10,11... | collective-permute-start | bytes 368648 | tf_op jit(solution)/shard_map/ppermute | solution.py:772
  24.6 26.7 %collective-permute-start.15 = (bf16[1,48,1792]{2,1,0:T(8,128)(2,1)S(1)}, bf16[1,48,1792]{2,1,0:T(8,128)(2,1)S(1)}, u32[]{:S(2)}, u32[]{:S(2)}) collective-permute-start(bf16[1,48,1792]{2,1,0:T(8,128)(2,1)S(1)} %bitcast.50), channel_id=1, source_target_pairs={{0,1},{1,0},{2,3},{3,2},{4,5},{5,4},{6,7},{7,6},{8,9},{9,8},{10,11... | collective-permute-start | bytes 516104 | tf_op jit(solution)/shard_map/ppermute | solution.py:772
  25.2 16.0 %collective-permute-start.17 = (bf16[1,48,2432]{2,1,0:T(8,128)(2,1)S(1)}, bf16[1,48,2432]{2,1,0:T(8,128)(2,1)S(1)}, u32[]{:S(2)}, u32[]{:S(2)}) collective-permute-start(bf16[1,48,2432]{2,1,0:T(8,128)(2,1)S(1)} %bitcast.41), channel_id=1, source_target_pairs={{0,1},{1,0},{2,3},{3,2},{4,5},{5,4},{6,7},{7,6},{8,9},{9,8},{10,11... | collective-permute-start | bytes 700424 | tf_op jit(solution)/shard_map/ppermute | solution.py:772
  26.7 16.1 %collective-permute-start.2 = (bf16[1,48,2432]{2,1,0:T(8,128)(2,1)S(1)}, bf16[1,48,2432]{2,1,0:T(8,128)(2,1)S(1)}, u32[]{:S(2)}, u32[]{:S(2)}) collective-permute-start(bf16[1,48,2432]{2,1,0:T(8,128)(2,1)S(1)} %bitcast.42), channel_id=1, source_target_pairs={{0,4},{1,5},{2,6},{3,7},{4,0},{5,1},{6,2},{7,3},{8,12},{9,13},{10,... | collective-permute-start | bytes 700424 | tf_op jit(solution)/shard_map/ppermute | solution.py:777
  27.2 15.1 %collective-permute-start.14 = (bf16[2,48,1792]{2,1,0:T(8,128)(2,1)S(1)}, bf16[2,48,1792]{2,1,0:T(8,128)(2,1)S(1)}, u32[]{:S(2)}, u32[]{:S(2)}) collective-permute-start(bf16[2,48,1792]{2,1,0:T(8,128)(2,1)S(1)} %pad_maximum_fusion.1), channel_id=1, source_target_pairs={{0,2},{1,3},{2,0},{3,1},{4,6},{5,7},{6,4},{7,5},{8,10},{9,11},{10,... | collective-permute-start | bytes 1032200 | tf_op jit(solution)/shard_map/ppermute | solution.py:777
  29.7 11.5 %collective-permute-start.16 = (bf16[1,48,1792]{2,1,0:T(8,128)(2,1)S(1)}, bf16[1,48,1792]{2,1,0:T(8,128)(2,1)S(1)}, u32[]{:S(2)}, u32[]{:S(2)}) collective-permute-start(bf16[1,48,1792]{2,1,0:T(8,128)(2,1)S(1)} %collective-permute-done.1.refs_0_.refs_7_.refs_10_.refs_23_), channel_id=1, source_target_pairs={{0,1},{1,0},{2,3},{3,2},{4,5},{5,4},{6,7},{7,6},{8,9},{9,8},{10,11... | collective-permute-start | bytes 516104 | tf_op jit(solution)/shard_map/ppermute | solution.py:772
  42.3 9.1 %collective-permute-start.18 = (bf16[2,48,1792]{2,1,0:T(8,128)(2,1)S(1)}, bf16[2,48,1792]{2,1,0:T(8,128)(2,1)S(1)}, u32[]{:S(2)}, u32[]{:S(2)}) collective-permute-start(bf16[2,48,1792]{2,1,0:T(8,128)(2,1)S(1)} %collective-permute-done.14.refs_8_.refs_11_.refs_24_), channel_id=1, source_target_pairs={{0,1},{1,0},{2,3},{3,2},{4,5},{5,4},{6,7},{7,6},{8,9},{9,8},{10,11... | collective-permute-start | bytes 1032200 | tf_op jit(solution)/shard_map/ppermute | solution.py:772
  42.9 11.8 %collective-permute-start.13 = (bf16[2,48,2432]{2,1,0:T(8,128)(2,1)S(1)}, bf16[2,48,2432]{2,1,0:T(8,128)(2,1)S(1)}, u32[]{:S(2)}, u32[]{:S(2)}) collective-permute-start(bf16[2,48,2432]{2,1,0:T(8,128)(2,1)S(1)} %pad_maximum_fusion), channel_id=1, source_target_pairs={{0,2},{1,3},{2,0},{3,1},{4,6},{5,7},{6,4},{7,5},{8,10},{9,11},{10,... | collective-permute-start | bytes 1400840 | tf_op jit(solution)/shard_map/ppermute | solution.py:777
  43.0 8.8 %collective-permute-start.19 = (bf16[1,48,1792]{2,1,0:T(8,128)(2,1)S(1)}, bf16[1,48,1792]{2,1,0:T(8,128)(2,1)S(1)}, u32[]{:S(2)}, u32[]{:S(2)}) collective-permute-start(bf16[1,48,1792]{2,1,0:T(8,128)(2,1)S(1)} %bitcast.51), channel_id=1, source_target_pairs={{0,8},{8,0},{16,24},{24,16},{1,9},{9,1},{17,25},{25,17},{2,10},{10... | collective-permute-start | bytes 516104 | tf_op jit(solution)/shard_map/ppermute | solution.py:756
  43.0 8.9 %collective-permute-start.20 = (bf16[1,48,1792]{2,1,0:T(8,128)(2,1)}, bf16[1,48,1792]{2,1,0:T(8,128)(2,1)S(1)}, u32[]{:S(2)}, u32[]{:S(2)}) collective-permute-start(bf16[1,48,1792]{2,1,0:T(8,128)(2,1)} %copy-done.14), channel_id=1, source_target_pairs={{0,8},{8,0},{16,24},{24,16},{1,9},{9,1},{17,25},{25,17},{2,10},{10... | collective-permute-start | bytes 516104 | tf_op jit(solution)/shard_map/ppermute | solution.py:756
  53.7 18.6 %collective-permute-start.27 = (bf16[1,48,2432]{2,1,0:T(8,128)(2,1)S(1)}, bf16[1,48,2432]{2,1,0:T(8,128)(2,1)}, u32[]{:S(2)}, u32[]{:S(2)}) collective-permute-start(bf16[1,48,2432]{2,1,0:T(8,128)(2,1)S(1)} %bitcast.44), channel_id=1, source_target_pairs={{0,8},{8,0},{16,24},{24,16},{1,9},{9,1},{17,25},{25,17},{2,10},{10... | collective-permute-start | bytes 700424 | tf_op jit(solution)/shard_map/ppermute | solution.py:756
  54.0 18.5 %collective-permute-start.25 = (bf16[1,48,2432]{2,1,0:T(8,128)(2,1)S(1)}, bf16[1,48,2432]{2,1,0:T(8,128)(2,1)}, u32[]{:S(2)}, u32[]{:S(2)}) collective-permute-start(bf16[1,48,2432]{2,1,0:T(8,128)(2,1)S(1)} %collective-permute-done.2.refs_6_.refs_11_.refs_23_), channel_id=1, source_target_pairs={{0,1},{1,0},{2,3},{3,2},{4,5},{5,4},{6,7},{7,6},{8,9},{9,8},{10,11... | collective-permute-start | bytes 700424 | tf_op jit(solution)/shard_map/ppermute | solution.py:772
  54.6 17.2 %collective-permute-start.26 = (bf16[2,48,2432]{2,1,0:T(8,128)(2,1)S(1)}, bf16[2,48,2432]{2,1,0:T(8,128)(2,1)S(1)}, u32[]{:S(2)}, u32[]{:S(2)}) collective-permute-start(bf16[2,48,2432]{2,1,0:T(8,128)(2,1)S(1)} %collective-permute-done.13.refs_0_.refs_7_.refs_12_.refs_24_), channel_id=1, source_target_pairs={{0,1},{1,0},{2,3},{3,2},{4,5},{5,4},{6,7},{7,6},{8,9},{9,8},{10,11... | collective-permute-start | bytes 1400840 | tf_op jit(solution)/shard_map/ppermute | solution.py:772
  56.1 18.7 %collective-permute-start.29 = (bf16[2,48,2432]{2,1,0:T(8,128)(2,1)S(1)}, bf16[2,48,2432]{2,1,0:T(8,128)(2,1)S(1)}, u32[]{:S(2)}, u32[]{:S(2)}) collective-permute-start(bf16[2,48,2432]{2,1,0:T(8,128)(2,1)S(1)} %collective-permute-done.13.refs_0_.refs_7_.refs_12_.refs_24_), channel_id=1, source_target_pairs={{0,8},{8,0},{16,24},{24,16},{1,9},{9,1},{17,25},{25,17},{2,10},{10... | collective-permute-start | bytes 1400840 | tf_op jit(solution)/shard_map/ppermute | solution.py:756
  117.0 34.8 %all-to-all-start = ((bf16[8,48,1664]{2,1,0:T(8,128)(2,1)}), bf16[8,48,1664]{2,1,0:T(8,128)(2,1)S(1)}, u32[]{:S(2)}, u32[]{:S(2)}) async-start(bf16[8,48,1664]{2,1,0:T(8,128)(2,1)} %bitcast.12), calls=%async_computation | async-start | bytes 2555904 | tf_op jit(solution)/shard_map/all_to_all | solution.py:825
  151.8 23.0 %all-to-all-start.1 = ((bf16[8,48,896]{2,1,0:T(8,128)(2,1)}), bf16[8,48,896]{2,1,0:T(8,128)(2,1)S(1)}, u32[]{:S(2)}, u32[]{:S(2)}) async-start(bf16[8,48,896]{2,1,0:T(8,128)(2,1)} %bitcast.13), calls=%async_computation.1 | async-start | bytes 1376256 | tf_op jit(solution)/shard_map/all_to_all | solution.py:825
  180.8 40.0 %all-to-all-start.2 = ((bf16[8,48,1664]{2,1,0:T(8,128)(2,1)}), bf16[8,48,1664]{2,1,0:T(8,128)(2,1)S(1)}, u32[]{:S(2)}, u32[]{:S(2)}) async-start(bf16[8,48,1664]{2,1,0:T(8,128)(2,1)} %bitcast.39), calls=%async_computation.2 | async-start | bytes 2555904 | tf_op jit(solution)/shard_map/all_to_all | solution.py:825
  209.8 10.0 %collective-permute-start.36 = (bf16[384,896]{1,0:T(8,128)(2,1)}, bf16[384,896]{1,0:T(8,128)(2,1)S(1)}, u32[]{:S(2)}, u32[]{:S(2)}) collective-permute-start(bf16[384,896]{1,0:T(8,128)(2,1)} %get-tuple-element.116), channel_id=1, source_target_pairs={{0,8},{8,0},{16,24},{24,16},{1,9},{9,1},{17,25},{25,17},{2,10},{10... | collective-permute-start | bytes 2064392 | tf_op jit(solution)/shard_map/ppermute | solution.py:756
  221.0 24.1 %all-to-all-start.3 = ((bf16[8,48,896]{2,1,0:T(8,128)(2,1)}), bf16[8,48,896]{2,1,0:T(8,128)(2,1)S(1)}, u32[]{:S(2)}, u32[]{:S(2)}) async-start(bf16[8,48,896]{2,1,0:T(8,128)(2,1)} %bitcast.16), calls=%async_computation.3 | async-start | bytes 1376256 | tf_op jit(solution)/shard_map/all_to_all | solution.py:825
  226.8 7.8 %collective-permute-start.39 = (bf16[48,2560]{1,0:T(8,128)(2,1)S(1)}, bf16[48,2560]{1,0:T(8,128)(2,1)S(1)}, u32[]{:S(2)}, u32[]{:S(2)}) collective-permute-start(bf16[48,2560]{1,0:T(8,128)(2,1)S(1)} %pad_maximum_fusion.2), channel_id=1, source_target_pairs={{0,16},{8,24},{16,0},{24,8},{1,17},{9,25},{17,1},{25,9},{2,18},{10... | collective-permute-start | bytes 737288 | tf_op jit(solution)/shard_map/ppermute | solution.py:832
  (72 other events, 452.5 us)
